TPU v7x, 256 devices: a whole 4x4x8 slice. The times are simulated.
256 devices in a mesh: ctx: 64 (over z, x, core), exp: 4 (over y).
Axes of the slice: x: 4, y: 4, z: 8, core: 2. Of those that a mesh axis runs over, the one named last changes fastest.
Arguments:
- queries: bfloat16 [16384, 4096], P('ctx', 'exp'), may hold values from -6 to 6
- keys: bfloat16 [16384, 4096], P('ctx', 'exp'), may hold values from -6 to 6
- values: bfloat16 [16384, 4096], P('ctx', 'exp'), may hold values from -6 to 6
- gates: bfloat16 [16384, 4096], P('ctx', 'exp'), may hold values from -6 to 6
- decay_rate: float32 [32], P('exp'), may hold values from 1.2207031e-06 to 0.05
- norm_gain: float32 [4096], P('exp'), may hold values from 0.1 to 1.9
- moe_rows: bfloat16 [2048, 3072], P('exp'), may hold values from -6 to 6
- tile_expert: int32 [16, 1], P('exp'), may hold values from 0 to 3; in each aligned block of 4 rows (0 to 3, 4 to 7, ...) at most 2 rows name the same one
- row_weight: float32 [2048], P('exp'), may hold values from 0.2 to 1
- w_gate: bfloat16 [4, 3072, 9216], P('exp', None, 'ctx'), may hold values from -0.109375 to 0.109375
- w_up: bfloat16 [4, 3072, 9216], P('exp', None, 'ctx'), may hold values from -0.109375 to 0.109375
- w_down: bfloat16 [4, 9216, 3072], P('exp', 'ctx'), may hold values from -0.1875 to 0.1875
Outputs:
- attention_out: bfloat16 [16384, 4096], P('ctx', 'exp')
- moe_out: bfloat16 [2048, 3072], P('exp', 'ctx')
Inputs may be any that keep to these rules, and one draw needn't show every extreme that they name: `tile_expert`: among the 4 tiles of one index of exp at most 2 name the same expert, and some index has exactly 2 tiles for one expert.
All inputs are finite; a program needn't handle non-finite values.
Results may differ from a plain program's by a relative error of at most 0.0057.
Values may be sent and summed in bfloat16 or wider, within the bound.
No kernel may reach another device: no remote copies, remote signals or barrier semaphores. Data moves between devices by JAX's collectives and lax.ppermute only.
A program may use at most 128 MiB of HBM per device.

v0:
```python
import jax
import jax.numpy as jnp
from jax import lax
from jax.sharding import PartitionSpec as P


def entering(array, axis, combine, identity):
    peers, mine = (lax.axis_size(axis), lax.axis_index(axis))
    everything = jax.tree.map(lambda part: lax.all_gather(part, axis), array)
    start = jax.tree.map(
        lambda part, zero: jnp.broadcast_to(jnp.asarray(zero, part.dtype), part.shape),
        array,
        identity,
    )

    def step(k, before):
        reached = k < mine
        new = combine(before, jax.tree.map(lambda part: part[k], everything))
        return jax.tree.map(lambda a, b: jnp.where(reached, a, b), new, before)

    return lax.fori_loop(0, peers, step, start)


def state_combine(earlier, later):
    return (earlier[0] * later[1][:, None, None] + later[0], earlier[1] * later[1])


def attention_part(queries, keys, values, gates, decay_rate, norm_gain):
    tokens_here = queries.shape[0]
    heads_here = decay_rate.shape[0]
    head_width = queries.shape[1] // heads_here
    query_heads = queries.reshape(tokens_here, heads_here, head_width)
    key_heads = keys.reshape(tokens_here, heads_here, head_width)
    value_heads = values.reshape(tokens_here, heads_here, head_width)
    positions = jnp.arange(tokens_here, dtype=jnp.float32)
    offsets = positions[:, None] - positions[None, :]
    within = jnp.exp(-decay_rate[:, None, None] * jnp.maximum(offsets, 0.0)[None])
    within = jnp.where((offsets >= 0.0)[None], within, 0.0)
    query_decay = jnp.exp(-decay_rate[None, :] * positions[:, None])
    key_decay = jnp.exp(-decay_rate[None, :] * (tokens_here - positions)[:, None])
    block_decay = jnp.exp(-decay_rate * tokens_here)
    key_scaled = (key_heads.astype(jnp.float32) * key_decay[:, :, None]).astype(jnp.bfloat16)
    local_state = jnp.einsum(
        "the,thf->hef", key_scaled, value_heads, preferred_element_type=jnp.float32
    )
    identity = (jnp.zeros_like(local_state), jnp.ones_like(block_decay))
    prefix, prefix_decay = entering((local_state, block_decay), "ctx", state_combine, identity)
    scores = jnp.einsum("the,she->hts", query_heads, key_heads, preferred_element_type=jnp.float32)
    scores = (scores * within).astype(jnp.bfloat16)
    intra = jnp.einsum("hts,she->the", scores, value_heads, preferred_element_type=jnp.float32)
    inter = jnp.einsum(
        "the,hef->thf", query_heads, prefix.astype(jnp.bfloat16), preferred_element_type=jnp.float32
    )
    mixed = (intra + inter * query_decay[:, :, None]).reshape(tokens_here, heads_here * head_width)
    square_part = jnp.sum(mixed * mixed, axis=1)
    square_total = lax.psum(square_part, "exp")
    mean_square = square_total / (heads_here * head_width * lax.axis_size("exp"))
    scaled = mixed * lax.rsqrt(mean_square + 1e-06)[:, None] * norm_gain[None, :]
    return (scaled * jax.nn.sigmoid(gates.astype(jnp.float32))).astype(jnp.bfloat16)


def expert_part(moe_rows, tile_expert, row_weight, w_gate, w_up, w_down):
    tiles_here = tile_expert.shape[0]
    tile_len = moe_rows.shape[0] // tiles_here
    model_width = moe_rows.shape[1]
    column_count = model_width // lax.axis_size("ctx")
    row_tiles = moe_rows.reshape(tiles_here, tile_len, model_width)
    tile_ids = tile_expert[:, 0]
    expert_count = lax.axis_size("exp")
    capacity = max(2, tiles_here // 2)
    order = jnp.arange(tiles_here)
    before = (tile_ids[None, :] == tile_ids[:, None]) & (order[None, :] < order[:, None])
    ranks = jnp.sum(before.astype(jnp.int32), axis=1)
    owner_match = tile_ids[None, None, :] == jnp.arange(expert_count)[:, None, None]
    slot_match = ranks[None, None, :] == jnp.arange(capacity)[None, :, None]
    select = (owner_match & slot_match).astype(jnp.bfloat16)
    send_buffer = jnp.einsum(
        "est,trd->esrd", select, row_tiles, preferred_element_type=jnp.float32
    ).astype(jnp.bfloat16)
    arrived = lax.all_to_all(send_buffer, "exp", split_axis=0, concat_axis=0, tiled=True)
    flat_rows = arrived.reshape(-1, model_width)
    gate_part = jnp.dot(flat_rows, w_gate[0], preferred_element_type=jnp.float32)
    up_part = jnp.dot(flat_rows, w_up[0], preferred_element_type=jnp.float32)
    hidden = (jax.nn.silu(gate_part) * up_part).astype(jnp.bfloat16)
    partial_out = jnp.dot(hidden, w_down[0], preferred_element_type=jnp.float32)
    summed = lax.psum_scatter(partial_out, "ctx", scatter_dimension=1, tiled=True).astype(
        jnp.bfloat16
    )
    result = summed.reshape(arrived.shape[:-1] + (column_count,))
    returned = lax.all_to_all(result, "exp", split_axis=0, concat_axis=0, tiled=True)
    expert_out = jnp.einsum(
        "est,esrd->trd", select, returned, preferred_element_type=jnp.float32
    ).astype(jnp.bfloat16)
    expert_out = lax.optimization_barrier(expert_out)
    weighted = expert_out.astype(jnp.float32) * row_weight.reshape(tiles_here, tile_len)[:, :, None]
    return weighted.astype(jnp.bfloat16).reshape(tiles_here * tile_len, column_count)


def on_device(
    queries,
    keys,
    values,
    gates,
    decay_rate,
    norm_gain,
    moe_rows,
    tile_expert,
    row_weight,
    w_gate,
    w_up,
    w_down,
):
    attention_out = attention_part(queries, keys, values, gates, decay_rate, norm_gain)
    moe_out = expert_part(moe_rows, tile_expert, row_weight, w_gate, w_up, w_down)
    return (attention_out, moe_out)


def solution(mesh):
    placed = (
        P("ctx", "exp"),
        P("ctx", "exp"),
        P("ctx", "exp"),
        P("ctx", "exp"),
        P("exp"),
        P("exp"),
        P("exp", None),
        P("exp", None),
        P("exp"),
        P("exp", None, "ctx"),
        P("exp", None, "ctx"),
        P("exp", "ctx", None),
    )
    return jax.shard_map(
        on_device,
        mesh=mesh,
        in_specs=placed,
        out_specs=(P("ctx", "exp"), P("exp", "ctx")),
        check_vma=False,
    )
```

profile of v0, /device:TPU:6, one launch (start us, length us, event | category | flops | bytes accessed | tf_op | source)
XLA Modules:
  0.0 516.6 jit_solution(9983925319370623804)
XLA Ops:
  8.8 6.3 %convolution_convert_fusion = bf16[4,2,128,3072]{3,0,2,1:T(4,128)(2,1)S(1)} fusion(bf16[4,128,3072]{2,1,0:T(8,128)(2,1)} %bitcast.95, pred[2,4]{1,0:T(4,128)(4,1)S(1)} %iota_compare_fusion.2, pred[4,4]{0,1:T(4,128)(4,1)S(1)} %iota_compare_fusion.1), kind=kOutput, calls=%fused_computation.3 | convolution fusion | flops 28311584 | bytes 9437208 | tf_op jit(solution)/shard_map/est,trd->esrd/dot_general | solution.py:77
  15.1 1.9 copy.43
  17.0 75.7 %all_to_all.10 = bf16[4,2,128,3072]{3,2,1,0:T(8,128)(2,1)S(1)} all-to-all(bf16[4,2,128,3072]{3,2,1,0:T(8,128)(2,1)S(1)} %copy.43), channel_id=1, replica_groups=mesh['ctx'=64,'exp'=4] {'exp'}, dimensions={0} | all-to-all | bytes 12582912 | tf_op jit(solution)/shard_map/all_to_all | solution.py:80
  92.7 2.7 copy-done.2
  95.4 2.2 fusion.17
  97.6 11.1 %fusion.8 = f32[1024,3072]{0,1:T(8,128)} fusion(bf16[1024,3072]{1,0:T(8,128)(2,1)} %bitcast.94, bf16[1,144,3072]{2,1,0:T(8,128)(2,1)S(1)} %copy-done, bf16[1,3072,144]{1,2,0:T(8,128)(2,1)S(1)} %copy-done.3, f32[1024,144]{0,1:T(8,128)S(1)} %fusion.17), kind=kOutput, calls=%fused_computation.14 | convolution fusion | flops 1812824064 | bytes 21233664 | tf_op jit(solution)/shard_map/dot_general | solution.py:85
  112.5 116.2 %all-reduce = f32[512]{0:T(512)S(1)} all-reduce(f32[512]{0:T(512)S(1)} %get-tuple-element.127), channel_id=2, replica_groups=mesh['ctx'=64,'exp'=4] {'ctx'}, use_global_device_ids=true, to_apply=%add | all-reduce | flops 512 | bytes 4096
  229.6 40.3 %reduce-scatter.2.cloned.1.call-done = f32[1024,48]{0,1:T(8,128)} async-done(((f32[1024,3072]{0,1:T(8,128)}), f32[1024,48]{0,1:T(8,128)}) %reduce-scatter.2.cloned.1.call-update) | async-done | bytes 196624 | tf_op jit(solution)/shard_map/reduce_scatter | solution.py:86
  271.6 4.2 all-to-all-start.1
  276.5 5.1 all-to-all-done.1
  282.5 130.9 %all-gather.4.cloned.1.call-done = f32[512,128,128]{2,1,0:T(8,128)} async-done(((f32[8,128,128]{2,1,0:T(8,128)}), f32[512,128,128]{2,1,0:T(8,128)}) %all-gather.4.cloned.1.call-update) | async-done | bytes 33554448 | tf_op jit(solution)/shard_map/all_gather | solution.py:9
  413.4 77.6 %while.14 = (s32[]{:T(128)}, f32[8,128,128]{2,1,0:T(8,128)S(1)}, s32[]{:T(128)}, f32[64,8]{1,0:T(8,128)S(1)}, f32[64,8,128,128]{3,2,1,0:T(8,128)}, /*index=5*/s32[]{:T(128)}, s32[]{:T(128)}) while((s32[]{:T(128)}, f32[8,128,128]{2,1,0:T(8,128)S(1)}, s32[]{:T(128)}, f32[64,8]{1,0:T(8,128)S(1)}, f32[64,8,128,128]{3,2,1,0:T(8,128)}, ...), condition=%wide.region_1.2_spmd.clone, body=%wide.region_0.1_spmd.clone.sunk | while | flops 524292 | bytes 1573065 | solution.py:21
  414.6 1.2 fusion.58
  415.9 1.2 fusion.58
  419.5 1.2 fusion.58
  420.7 1.2 fusion.58
  421.9 1.2 fusion.58
  425.6 1.2 fusion.58
  426.8 1.2 fusion.58
  428.0 1.2 fusion.58
  431.6 1.2 fusion.58
  432.8 1.2 fusion.58
  434.1 1.2 fusion.58
  437.7 1.2 fusion.58
  438.9 1.2 fusion.58
  442.6 1.2 fusion.58
  443.8 1.2 fusion.58
  491.1 1.5 fusion.6
  492.6 3.0 multiply_reduce_fusion
  495.6 1.6 copy.40
  497.1 10.5 %psum.7 = f32[256]{0:T(256)S(1)} all-reduce(f32[256]{0:T(256)S(1)} %get-tuple-element.129), channel_id=1, replica_groups=mesh['ctx'=64,'exp'=4] {'exp'}, use_global_device_ids=true, to_apply=%region_3.4 | all-reduce | flops 256 | bytes 2048 | tf_op jit(solution)/shard_map/psum | solution.py:56
  507.6 2.2 multiply_convert_fusion.1
  (159 shorter events, 67.0 us)
Async XLA Ops:
  7.2 90.4 %copy-start = (bf16[1,144,3072]{2,1,0:T(8,128)(2,1)S(1)}, bf16[1,144,3072]{2,1,0:T(8,128)(2,1)}, u32[]{:S(2)}) copy-start(bf16[1,144,3072]{2,1,0:T(8,128)(2,1)} %param.25) | copy-start | bytes 2654212
  7.2 262.7 %reduce-scatter.2.cloned.1.call-start = ((), (), s32[]{:S(2)}) async-start(), calls=%async_computation.3 | async-start | bytes 12779520 | tf_op jit(solution)/shard_map/reduce_scatter | solution.py:86
  17.0 78.4 %copy-start.9 = (bf16[1,3072,144]{1,2,0:T(8,128)(2,1)S(1)}, bf16[1,3072,144]{1,2,0:T(8,128)(2,1)}, u32[]{:S(2)}) copy-start(bf16[1,3072,144]{1,2,0:T(8,128)(2,1)} %param.23) | copy-start | bytes 2654212
  92.7 2.7 copy-start.2
  92.7 4.9 copy-start.3
  108.7 1.0 copy-start.5
  108.7 1.3 copy-start.10
  108.7 2.5 copy-start.8
  108.7 2.7 copy-start.4
  108.7 173.2 %copy-start.7 = (f32[512]{0:T(512)S(1)}, f32[512]{0:T(512)}, u32[]{:S(2)}) copy-start(f32[512]{0:T(512)} %param.22) | copy-start | bytes 6148
  108.7 304.7 %all-gather.4.cloned.1.call-start = ((), (), s32[]{:S(2)}) async-start(), calls=%async_computation.4 | async-start | bytes 34078720 | tf_op jit(solution)/shard_map/all_gather | solution.py:9
  271.6 10.0 %all-to-all-start.1 = ((bf16[4,2,128,48]{2,1,3,0:T(2,128)(2,1)}), bf16[4,2,128,48]{2,1,3,0:T(2,128)(2,1)S(1)}, u32[]{:S(2)}, u32[]{:S(2)}) async-start(bf16[4,2,128,48]{2,1,3,0:T(2,128)(2,1)} %copy.44), calls=%async_computation.2 | async-start | bytes 196608 | tf_op jit(solution)/shard_map/all_to_all | solution.py:90
  491.1 16.5 %copy-start.6 = (f32[1024]{0:T(1024)S(1)}, f32[1024]{0:T(1024)}, u32[]{:S(2)}) copy-start(f32[1024]{0:T(1024)} %param.19) | copy-start | bytes 12292
  491.1 18.7 %copy-start.1 = (bf16[1,144,3072]{2,1,0:T(8,128)(2,1)S(1)}, bf16[1,144,3072]{2,1,0:T(8,128)(2,1)}, u32[]{:S(2)}) copy-start(bf16[1,144,3072]{2,1,0:T(8,128)(2,1)} %param.25) | copy-start | bytes 2654212
Sparse Core Ops, SparseCore 0:
  108.9 160.9 reduce-scatter.1
  273.6 139.7 all-gather.3
where the time goes:
time: 521 us; the launch traced here: 517 us
  blocking collectives  202 us (39%)
  waiting for transfers between devices  176 us (34%)
  other arithmetic  81.4 us (16%)
  matrix products  25.5 us (5%)
  between operations  14.9 us (3%)
  local copies, waits for them, and re-layouts  9.96 us (2%)
    all_gather x1, waiting for transfers between devices, entering(): everything = jax.tree.map(lambda part: lax.all_gather(part, axis), array)  131 us
    unnamed x1, blocking collectives  116 us
    all_to_all x1, blocking collectives, expert_part(): lax.all_to_all(send_buffer, 'exp', split_axis=0, concat_axis=0, tiled=True)  75.7 us
    select_n x64, other arithmetic, step(): return jax.tree.map(lambda a, b: jnp.where(reached, a, b), new, before)  75 us
    reduce_scatter x1, waiting for transfers between devices, expert_part(): lax.psum_scatter(partial_out, 'ctx', scatter_dimension=1, tiled=True)  40.3 us
    dot_general x1, matrix products, expert_part(): partial_out = jnp.dot(hidden, w_down[0], preferred_element_type=jnp.float32)  11.1 us
    psum x1, blocking collectives, attention_part(): square_total = lax.psum(square_part, 'exp')  10.5 us
  transfers between devices with their start and end apart: 3, of which 3 were waited for; matrix products, arithmetic and copies ran while one was open for 1% of the time, Pallas kernels for 0%

commit v1 on v0

v1 whole, which is shorter than its diff:
```python
import jax
import jax.numpy as jnp
from jax import lax
from jax.experimental import pallas as pl
from jax.experimental.pallas import tpu as pltpu
from jax.sharding import Mesh
from jax.sharding import PartitionSpec as P

BF = jnp.bfloat16
F32 = jnp.float32
CTX = ("z", "x", "core")
HEAD = 128
TILE = 128


def _state_kernel(rate, k, v, out):
    tokens = k.shape[0]
    r = rate[pl.program_id(0)]
    t = lax.broadcasted_iota(jnp.int32, (tokens, HEAD), 0).astype(F32)
    scaled = (k[...].astype(F32) * jnp.exp(-r * (tokens - t))).astype(BF)
    out[...] = lax.dot_general(
        scaled, v[...], (((0,), (0,)), ((), ())), preferred_element_type=F32
    ).astype(BF)


def local_states(rate, keys, values):
    tokens, width = keys.shape
    heads = width // HEAD
    return pl.pallas_call(
        _state_kernel,
        grid=(heads,),
        in_specs=[
            pl.BlockSpec(memory_space=pltpu.SMEM),
            pl.BlockSpec((tokens, HEAD), lambda h: (0, h)),
            pl.BlockSpec((tokens, HEAD), lambda h: (0, h)),
        ],
        out_specs=pl.BlockSpec((HEAD, HEAD), lambda h: (h, 0)),
        out_shape=jax.ShapeDtypeStruct((width, HEAD), BF),
        name="local_states",
    )(rate, keys, values)


def _scan_kernel(decay, states, out):
    lam = decay[0]
    blocks = states.shape[0]
    carry = jnp.zeros(states.shape[1:], F32)
    for b in range(blocks):
        out[b] = carry.astype(BF)
        carry = carry * lam + states[b].astype(F32)


def scan_states(decay, states):
    return pl.pallas_call(
        _scan_kernel,
        in_specs=[
            pl.BlockSpec(memory_space=pltpu.SMEM),
            pl.BlockSpec(memory_space=pltpu.VMEM),
        ],
        out_specs=pl.BlockSpec(memory_space=pltpu.VMEM),
        out_shape=jax.ShapeDtypeStruct(states.shape, BF),
        name="scan_states",
    )(decay, states)


def _intra_kernel(rate, q, k, v, out):
    tokens = q.shape[0]
    r = rate[pl.program_id(0)]
    i = lax.broadcasted_iota(jnp.int32, (tokens, tokens), 0)
    j = lax.broadcasted_iota(jnp.int32, (tokens, tokens), 1)
    off = (i - j).astype(F32)
    within = jnp.where(off >= 0.0, jnp.exp(-r * jnp.maximum(off, 0.0)), 0.0)
    scores = lax.dot_general(
        q[...], k[...], (((1,), (1,)), ((), ())), preferred_element_type=F32
    )
    out[...] = jnp.dot(
        (scores * within).astype(BF), v[...], preferred_element_type=F32
    )


def intra_part(rate, queries, keys, values):
    tokens, width = keys.shape
    heads = width // HEAD
    spec = pl.BlockSpec((tokens, HEAD), lambda h: (0, h))
    return pl.pallas_call(
        _intra_kernel,
        grid=(heads,),
        in_specs=[pl.BlockSpec(memory_space=pltpu.SMEM), spec, spec, spec],
        out_specs=spec,
        out_shape=jax.ShapeDtypeStruct((tokens, width), F32),
        name="intra_part",
    )(rate, queries, keys, values)


def _mix_kernel(rate, intra, q, prefix, mixed, squares):
    tokens = q.shape[0]
    h = pl.program_id(0)
    r = rate[h]
    t = lax.broadcasted_iota(jnp.int32, (tokens, HEAD), 0).astype(F32)
    inter = jnp.dot(q[...], prefix[...], preferred_element_type=F32)
    value = intra[...] + inter * jnp.exp(-r * t)
    mixed[...] = value

    @pl.when(h == 0)
    def _():
        squares[...] = jnp.zeros_like(squares)

    squares[...] += jnp.sum(jnp.transpose(value * value), axis=0, keepdims=True)


def mix_part(rate, intra, queries, prefix):
    tokens, width = queries.shape
    heads = width // HEAD
    spec = pl.BlockSpec((tokens, HEAD), lambda h: (0, h))
    return pl.pallas_call(
        _mix_kernel,
        grid=(heads,),
        in_specs=[
            pl.BlockSpec(memory_space=pltpu.SMEM),
            spec,
            spec,
            pl.BlockSpec((HEAD, HEAD), lambda h: (h, 0)),
        ],
        out_specs=[spec, pl.BlockSpec((1, tokens), lambda h: (0, 0))],
        out_shape=[
            jax.ShapeDtypeStruct((tokens, width), F32),
            jax.ShapeDtypeStruct((1, tokens), F32),
        ],
        name="mix_part",
    )(rate, intra, queries, prefix)


def _norm_kernel(features, total, mixed, gain, gates, out):
    tokens = mixed.shape[0]
    factor = lax.rsqrt(total[...] / features + 1e-06)
    column = jnp.transpose(jnp.broadcast_to(factor, (HEAD, tokens)))
    scaled = mixed[...] * column * gain[...]
    out[...] = (scaled * jax.nn.sigmoid(gates[...].astype(F32))).astype(BF)


def norm_part(features, total, mixed, gain, gates):
    tokens, width = mixed.shape
    heads = width // HEAD
    spec = pl.BlockSpec((tokens, HEAD), lambda h: (0, h))

    def kernel(*refs):
        _norm_kernel(features, *refs)

    return pl.pallas_call(
        kernel,
        grid=(heads,),
        in_specs=[
            pl.BlockSpec((1, tokens), lambda h: (0, 0)),
            spec,
            pl.BlockSpec((1, HEAD), lambda h: (0, h)),
            spec,
        ],
        out_specs=spec,
        out_shape=jax.ShapeDtypeStruct((tokens, width), BF),
        name="norm_part",
    )(total, mixed, gain, gates)


def shift(array, axis, by):
    n = lax.axis_size(axis)
    return lax.ppermute(array, axis, [(i, (i + by) % n) for i in range(n)])


def on_device(
    queries, keys, values, gates, decay_rate, norm_gain,
    moe_rows, tile_expert, row_weight, w_gate, w_up, w_down,
):
    n_exp, n_z = lax.axis_size("exp"), lax.axis_size("z")
    n_x, n_core = lax.axis_size("x"), lax.axis_size("core")
    n_ctx = n_z * n_x * n_core
    me_e, me_core = lax.axis_index("exp"), lax.axis_index("core")
    tokens, width = queries.shape
    heads = width // HEAD
    model = moe_rows.shape[1]
    tiles = tile_expert.shape[0]

    ids = tile_expert[:, 0]
    order = jnp.arange(tiles)
    earlier = (ids[None, :] == ids[:, None]) & (order[None, :] < order[:, None])
    ranks = jnp.sum(earlier.astype(jnp.int32), axis=1)

    arrived = []
    for k in range(n_exp):
        target = lax.rem(me_e + k, n_exp)
        hit = (ids == target) & (ranks == me_core)
        tile = jnp.sum(jnp.where(hit, order, 0))
        rows = lax.dynamic_slice(moe_rows, (tile * TILE, 0), (TILE, model))
        arrived.append(shift(rows, "exp", k) if k else rows)

    states = local_states(decay_rate, keys, values)
    pieces = states.reshape(n_ctx, width // n_ctx, HEAD)
    pieces = lax.all_to_all(pieces, CTX, 0, 0, tiled=True)
    mine = lax.axis_index(CTX) * (width // n_ctx) // HEAD
    lam = jnp.exp(-decay_rate * tokens)
    pieces = scan_states(lax.dynamic_slice(lam, (mine,), (1,)), pieces)
    prefix = lax.all_to_all(pieces, CTX, 0, 0, tiled=True).reshape(width, HEAD)
    intra = intra_part(decay_rate, queries, keys, values)
    mixed, squares = mix_part(decay_rate, intra, queries, prefix)
    total = lax.psum(squares, "exp")
    attention_out = norm_part(
        float(width * n_exp), total, mixed, norm_gain[None, :], gates
    )

    gate_own = jnp.swapaxes(w_gate[0], 0, 1)
    up_own = jnp.swapaxes(w_up[0], 0, 1)
    gate_other = shift(gate_own, "core", 1)
    up_other = shift(up_own, "core", 1)
    units = gate_own.shape[0]
    chunk = model // n_z
    down_own = jnp.swapaxes(w_down[0].reshape(units, n_z, chunk), 0, 1)
    down_own = lax.all_to_all(down_own, "z", 0, 0, tiled=True)
    down_other = shift(down_own, "core", 1)
    down = jnp.stack([down_own, down_other], axis=1)

    inner = jnp.concatenate([gate_own, gate_other, up_own, up_other], axis=0)
    hidden = []
    for rows in arrived:
        both = lax.dot_general(
            inner, rows, (((1,), (1,)), ((), ())), preferred_element_type=F32
        )
        half = jax.nn.silu(both[: 2 * units]) * both[2 * units :]
        hidden.append(half.astype(BF))
    turned = [hidden[(-m) % n_exp] for m in range(n_exp)]
    twice = jnp.concatenate(turned + turned, axis=1)
    rows_here = n_exp * TILE
    hidden = lax.dynamic_slice(
        twice, (0, (n_exp - me_e) * TILE), (2 * units, rows_here)
    )
    hidden = lax.all_gather(hidden, "z").reshape(n_z, 2, units, rows_here)
    partial = lax.dot_general(
        down.reshape(n_z * 2 * units, chunk),
        hidden.reshape(n_z * 2 * units, rows_here),
        (((0,), (0,)), ((), ())),
        preferred_element_type=F32,
    ).astype(BF)
    columns = chunk // (n_x * n_core)
    parts = partial.reshape(n_x * n_core, columns, n_exp, TILE)
    parts = jnp.swapaxes(parts, 1, 2).reshape(-1, columns, TILE)
    parts = lax.all_to_all(parts, ("x", "core", "exp"), 0, 0, tiled=True)
    parts = parts.reshape(n_x, n_core * n_exp, columns, TILE)
    summed = jnp.sum(parts.astype(F32), axis=0).astype(BF)
    summed = lax.optimization_barrier(summed)
    picked = []
    for t in range(tiles):
        slot = ranks[t] * n_exp + ids[t]
        tile = lax.dynamic_index_in_dim(summed, slot, 0, keepdims=False)
        weight = row_weight[t * TILE : (t + 1) * TILE]
        picked.append((tile.astype(F32) * weight[None, :]).astype(BF))
    moe_out = jnp.swapaxes(jnp.concatenate(picked, axis=1), 0, 1)
    return attention_out, moe_out


def solution(mesh):
    n_core, n_x = 2, 4
    grid = mesh.devices.reshape(-1, n_x, n_core, mesh.devices.shape[1])
    fine = Mesh(grid, ("z", "x", "core", "exp"))
    placed = (
        P(CTX, "exp"),
        P(CTX, "exp"),
        P(CTX, "exp"),
        P(CTX, "exp"),
        P("exp"),
        P("exp"),
        P("exp", None),
        P("exp", None),
        P("exp"),
        P("exp", None, CTX),
        P("exp", None, CTX),
        P("exp", CTX, None),
    )
    return jax.shard_map(
        on_device,
        mesh=fine,
        in_specs=placed,
        out_specs=(P(CTX, "exp"), P("exp", CTX)),
        check_vma=False,
    )
```

time: 521 us -> 199 us (0.38)
  blocking collectives: 202 us -> 51.3 us
  waiting for transfers between devices: 176 us -> 46.3 us
  other arithmetic: 81.4 us -> 4.94 us
  Pallas kernels: 0 us -> 26.4 us
  starting transfers between devices: 4.27 us -> 25.8 us
  matrix products: 25.5 us -> 11.7 us
  between operations: 14.9 us -> 22 us
    all_gather x1, waiting for transfers between devices: 131 us -> 0.02 us  [on_device(): hidden = lax.all_gather(hidden, 'z').reshape(n_z, 2, units, rows_here)]
    unnamed x1 -> x0, blocking collectives: 116 us -> none
    select_n x64 -> x0, other arithmetic: 75 us -> none  [step(): return jax.tree.map(lambda a, b: jnp.where(reached, a, b), new, before)]
    reduce_scatter x1 -> x0, waiting for transfers between devices: 40.3 us -> none  [expert_part(): lax.psum_scatter(partial_out, 'ctx', scatter_dimension=1, tiled=True)]
    all_to_all x1, blocking collectives: 75.7 us -> 40.2 us  [on_device(): down_own = lax.all_to_all(down_own, 'z', 0, 0, tiled=True)]
    ppermute x0 -> x6, waiting for transfers between devices: none -> 29.5 us  [shift(): return lax.ppermute(array, axis, [(i, (i + by) % n) for i in range(n)])]
    pallas_call x0 -> x5, Pallas kernels: none -> 26.4 us  [the longest x1 6.57 us: intra_part(): pl.pallas_call(_intra_kernel, grid=(heads,), in_specs=[pl.BlockSpec(memor...]
    all_to_all x1 -> x3, starting transfers between devices: 4.18 us -> 20.6 us  [the longest x1 8.74 us: on_device(): parts = lax.all_to_all(parts, ('x', 'core', 'exp'), 0, 0, tiled=True)]
  transfers between devices with their start and end apart: 3 -> 10, of which waited for: 3 -> 3; matrix products, arithmetic and copies ran while one was open for 1% -> 10% of each run, Pallas kernels for 0% -> 13%
where the time goes in v1:
time: 199 us; the launch traced here: 197 us
  blocking collectives  51.3 us (26%)
  waiting for transfers between devices  46.3 us (23%)
  Pallas kernels  26.4 us (13%)
  starting transfers between devices  25.8 us (13%)
  between operations  22 us (11%)
  matrix products  11.7 us (6%)
  local copies, waits for them, and re-layouts  8.64 us (4%)
  other arithmetic  4.94 us (2%)
    all_to_all x1, blocking collectives, on_device(): down_own = lax.all_to_all(down_own, 'z', 0, 0, tiled=True)  40.2 us
    ppermute x6, waiting for transfers between devices, shift(): return lax.ppermute(array, axis, [(i, (i + by) % n) for i in range(n)])  29.5 us
    psum x1, blocking collectives, on_device(): total = lax.psum(squares, 'exp')  11.1 us
    all_to_all x1, waiting for transfers between devices, on_device(): pieces = lax.all_to_all(pieces, CTX, 0, 0, tiled=True)  10.9 us
    dot_general x4, matrix products, on_device(): lax.dot_general(inner, rows, (((1,), (1,)), ((), ())), preferred_element_...  8.94 us
    all_to_all x1, starting transfers between devices, on_device(): parts = lax.all_to_all(parts, ('x', 'core', 'exp'), 0, 0, tiled=True)  8.74 us
    pallas_call x1, Pallas kernels, intra_part(): pl.pallas_call(_intra_kernel, grid=(heads,), in_specs=[pl.BlockSpec(memor...  6.57 us
    all_to_all x1, starting transfers between devices, on_device(): prefix = lax.all_to_all(pieces, CTX, 0, 0, tiled=True).reshape(width, HEAD)  6.42 us
  transfers between devices with their start and end apart: 10, of which 3 were waited for; matrix products, arithmetic and copies ran while one was open for 10% of the time, Pallas kernels for 13%

profile of v1, /device:TPU:6, one launch (start us, length us, event | category | flops | bytes accessed | tf_op | source)
XLA Modules:
  0.0 197.1 jit_solution(9716358520405747939)
XLA Ops:
  7.8 0.9 convert_reduce_fusion
  8.7 1.4 fusion.15
  12.1 3.1 %constant_dynamic-slice_fusion.1 = (bf16[128,3072]{1,0:T(8,128)(2,1)}, bf16[128,3072]{1,0:T(8,128)(2,1)}, bf16[128,3072]{1,0:T(8,128)(2,1)}) fusion(bf16[512,3072]{1,0:T(8,128)(2,1)} %param.18, s32[]{:T(128)S(6)} %select_n.58, s32[]{:T(128)S(6)} %select_n.54, s32[]{:T(128)S(6)} %select_n.56), kind=kLoop, calls=%fused_computation.31 | loop fusion | bytes 4718604 | tf_op jit(solution)/shard_map/dynamic_slice | solution.py:191
  15.2 3.0 %collective-permute-start.3 = (bf16[128,3072]{1,0:T(8,128)(2,1)}, bf16[128,3072]{1,0:T(8,128)(2,1)}, u32[]{:S(2)}, u32[]{:S(2)}) collective-permute-start(bf16[128,3072]{1,0:T(8,128)(2,1)} %get-tuple-element.19), channel_id=1, source_target_pairs={{0,3},{1,0},{2,1},{3,2},{4,7},{5,4},{6,5},{7,6},{8,11},{9,8},{10,9... | collective-permute-start | bytes 2359304 | tf_op jit(solution)/shard_map/ppermute | solution.py:165
  18.2 0.6 collective-permute-start.4
  18.8 1.0 collective-permute-start.5
  20.8 2.2 %fusion = f32[576,128]{1,0:T(8,128)S(1)} fusion(bf16[576,3072]{1,0:T(8,128)(2,1)S(1)} %pad_maximum_fusion, bf16[512,3072]{1,0:T(8,128)(2,1)} %param.18, s32[]{:T(128)S(6)} %select_n.52), kind=kOutput, calls=%fused_computation.3 | convolution fusion | flops 452984832 | bytes 4620292 | tf_op jit(solution)/shard_map/dot_general | solution.py:222
  23.1 29.5 %collective-permute-done.3 = bf16[128,3072]{1,0:T(8,128)(2,1)} collective-permute-done((bf16[128,3072]{1,0:T(8,128)(2,1)}, bf16[128,3072]{1,0:T(8,128)(2,1)}, u32[]{:S(2)}, u32[]{:S(2)}) %collective-permute-start.3) | collective-permute-done | bytes 786464 | tf_op jit(solution)/shard_map/ppermute | solution.py:165
  52.5 2.2 %fusion.23 = f32[576,128]{1,0:T(8,128)S(1)} fusion(bf16[576,3072]{1,0:T(8,128)(2,1)S(1)} %pad_maximum_fusion, bf16[128,3072]{1,0:T(8,128)(2,1)} %collective-permute-done.3), kind=kOutput, calls=%fused_computation.51 | convolution fusion | flops 452984832 | bytes 4620288 | tf_op jit(solution)/shard_map/dot_general | solution.py:222
  54.8 2.2 %fusion.24 = f32[576,128]{1,0:T(8,128)S(1)} fusion(bf16[576,3072]{1,0:T(8,128)(2,1)S(1)} %pad_maximum_fusion, bf16[128,3072]{1,0:T(8,128)(2,1)} %collective-permute-done.4), kind=kOutput, calls=%fused_computation.52 | convolution fusion | flops 452984832 | bytes 4620288 | tf_op jit(solution)/shard_map/dot_general | solution.py:222
  57.1 2.3 %fusion.25 = f32[576,128]{1,0:T(8,128)S(1)} fusion(bf16[576,3072]{1,0:T(8,128)(2,1)S(1)} %pad_maximum_fusion, bf16[128,3072]{1,0:T(8,128)(2,1)} %collective-permute-done.5), kind=kOutput, calls=%fused_computation.53 | convolution fusion | flops 452984832 | bytes 4620288 | tf_op jit(solution)/shard_map/dot_general | solution.py:222
  59.6 0.7 constant_dynamic-slice_fusion
  60.7 40.2 %all_to_all.20 = bf16[8,144,384]{2,1,0:T(8,128)(2,1)S(1)} all-to-all(bf16[8,144,384]{2,1,0:T(8,128)(2,1)S(1)} %copy.20), channel_id=1, replica_groups=mesh['z'=8,'x'=4,'core'=2,'exp'=4] {'z'}, dimensions={0} | all-to-all | bytes 1769472 | tf_op jit(solution)/shard_map/all_to_all | solution.py:215
  100.8 5.8 %local_states.1 = bf16[1024,128]{1,0:T(8,128)(2,1)} custom-call(f32[8]{0:T(128)} %rate.5, bf16[256,1024]{1,0:T(8,128)(2,1)} %k.3, bf16[256,1024]{1,0:T(8,128)(2,1)} %v.3), custom_call_target="tpu_custom_call" | custom-call | tf_op jit(solution)/shard_map/local_states/pallas_call | solution.py:29
  106.6 5.4 %all-to-all-start = ((bf16[64,16,128]{2,1,0:T(8,128)(2,1)}), bf16[64,16,128]{2,1,0:T(8,128)(2,1)S(1)}, u32[]{:S(2)}, u32[]{:S(2)}) async-start(bf16[64,16,128]{2,1,0:T(8,128)(2,1)} %bitcast.61), calls=%async_computation | async-start | bytes 524288 | tf_op jit(solution)/shard_map/all_to_all | solution.py:196
  112.7 10.9 %all-to-all-done.states = bf16[64,16,128]{2,1,0:T(8,128)(2,1)S(1)} async-done(((bf16[64,16,128]{2,1,0:T(8,128)(2,1)}), bf16[64,16,128]{2,1,0:T(8,128)(2,1)S(1)}, u32[]{:S(2)}, u32[]{:S(2)}) %all-to-all-start) | async-done | bytes 262176 | tf_op jit(solution)/shard_map/all_to_all | solution.py:196
  123.6 0.7 copy-done
  124.3 2.4 %scan_states.1 = bf16[64,16,128]{2,1,0:T(8,128)(2,1)} custom-call(f32[1]{0:T(128)} %dynamic_slice.31.decay, bf16[64,16,128]{2,1,0:T(8,128)(2,1)} %copy-done), custom_call_target="tpu_custom_call" | custom-call | tf_op jit(solution)/shard_map/scan_states/pallas_call | solution.py:53
  126.7 6.4 %all-to-all-start.1 = ((bf16[64,16,128]{2,1,0:T(8,128)(2,1)}), bf16[64,16,128]{2,1,0:T(8,128)(2,1)S(1)}, u32[]{:S(2)}, u32[]{:S(2)}) async-start(bf16[64,16,128]{2,1,0:T(8,128)(2,1)} %scan_states.1), calls=%async_computation.1 | async-start | bytes 524288 | tf_op jit(solution)/shard_map/all_to_all | solution.py:200
  133.2 0.9 copy-done.2
  134.1 1.4 pad_maximum_fusion.1
  135.5 2.8 %convolution_convert_fusion = bf16[384,512]{1,0:T(8,128)(2,1)S(1)} fusion(bf16[2304,384]{1,0:T(8,128)(2,1)S(1)} %bitcast.59, bf16[2304,512]{1,0:T(8,128)(2,1)} %all-gather.3.cloned.1.call-done), kind=kOutput, calls=%fused_computation.2 | convolution fusion | flops 906166272 | bytes 4521984 | tf_op jit(solution)/shard_map/dot_general | solution.py:234
  138.4 0.8 copy.21
  139.2 5.9 %all-to-all-done.1 = bf16[64,16,128]{2,1,0:T(8,128)(2,1)S(1)} async-done(((bf16[64,16,128]{2,1,0:T(8,128)(2,1)}), bf16[64,16,128]{2,1,0:T(8,128)(2,1)S(1)}, u32[]{:S(2)}, u32[]{:S(2)}) %all-to-all-start.1) | async-done | bytes 262176 | tf_op jit(solution)/shard_map/all_to_all | solution.py:200
  145.1 8.7 %all-to-all-start.3 = ((bf16[32,48,128]{2,1,0:T(8,128)(2,1)}), bf16[32,48,128]{2,1,0:T(8,128)(2,1)S(1)}, u32[]{:S(2)}, u32[]{:S(2)}) async-start(bf16[32,48,128]{2,1,0:T(8,128)(2,1)} %bitcast.15), calls=%async_computation.3 | async-start | bytes 786432 | tf_op jit(solution)/shard_map/all_to_all | solution.py:243
  153.8 0.7 fusion.22
  155.2 0.7 fusion.21
  160.2 6.6 %intra_part.1.intra = f32[256,1024]{1,0:T(8,128)} custom-call(f32[8]{0:T(128)} %rate.5, bf16[256,1024]{1,0:T(8,128)(2,1)} %q.3, bf16[256,1024]{1,0:T(8,128)(2,1)} %k.3, bf16[256,1024]{1,0:T(8,128)(2,1)} %v.3), custom_call_target="tpu_custom_call" | custom-call | tf_op jit(solution)/shard_map/intra_part/pallas_call | solution.py:84
  166.8 6.1 %mix_part.1 = (f32[256,1024]{1,0:T(8,128)}, f32[1,256]{1,0:T(1,128)}) custom-call(f32[8]{0:T(128)} %rate.5, f32[256,1024]{1,0:T(8,128)} %intra_part.1.intra, bf16[256,1024]{1,0:T(8,128)(2,1)} %q.3, bf16[1024,128]{1,0:T(8,128)(2,1)} %bitcast.62), custom_call_target="tpu_custom_call" | custom-call | tf_op jit(solution)/shard_map/mix_part/pallas_call | solution.py:114
  172.9 11.1 %psum.7.refs_0_ = f32[1,256]{1,0:T(1,128)} all-reduce(f32[1,256]{1,0:T(1,128)} %get-tuple-element.4), channel_id=1, replica_groups=mesh['z'=8,'x'=4,'core'=2,'exp'=4] {'exp'}, use_global_device_ids=true, to_apply=%region_0.0 | all-reduce | flops 256 | bytes 2048 | tf_op jit(solution)/shard_map/psum | solution.py:203
  184.0 5.5 %norm_part.1 = bf16[256,1024]{1,0:T(8,128)(2,1)} custom-call(f32[1,256]{1,0:T(1,128)} %psum.7.refs_0_, f32[256,1024]{1,0:T(8,128)} %get-tuple-element.5.refs_1_, f32[1,1024]{1,0:T(1,128)} %bitcast.70, bf16[256,1024]{1,0:T(8,128)(2,1)} %refs_3_.1), custom_call_target="tpu_custom_call" | custom-call | tf_op jit(solution)/shard_map/norm_part/pallas_call | solution.py:148
  189.7 0.6 maximum_bitcast_fusion
  (45 shorter events, 2.4 us)
Async XLA Ops:
  7.2 13.3 %copy-start.4 = (bf16[1,3072,144]{1,2,0:T(8,128)(2,1)S(1)}, bf16[1,3072,144]{1,2,0:T(8,128)(2,1)}, u32[]{:S(2)}) copy-start(bf16[1,3072,144]{1,2,0:T(8,128)(2,1)} %param.21) | copy-start | bytes 2654212
  7.2 13.3 %copy-start.3 = (bf16[1,3072,144]{1,2,0:T(8,128)(2,1)S(1)}, bf16[1,3072,144]{1,2,0:T(8,128)(2,1)}, u32[]{:S(2)}) copy-start(bf16[1,3072,144]{1,2,0:T(8,128)(2,1)} %param.22) | copy-start | bytes 2654212
  7.2 128.3 %all-gather.3.cloned.1.call-start = ((), (), s32[]{:S(2)}) async-start(), calls=%async_computation.4 | async-start | bytes 2654208 | tf_op jit(solution)/shard_map/all_gather | solution.py:233
  7.2 13.2 %collective-permute-start.1 = (bf16[144,3072]{1,0:T(8,128)(2,1)}, bf16[144,3072]{1,0:T(8,128)(2,1)S(1)}, u32[]{:S(2)}, u32[]{:S(2)}) collective-permute-start(bf16[144,3072]{1,0:T(8,128)(2,1)} %bitcast.66), channel_id=1, source_target_pairs={{0,4},{4,0},{1,5},{5,1},{2,6},{6,2},{3,7},{7,3},{8,12},{12,8},{9,1... | collective-permute-start | bytes 2654216 | tf_op jit(solution)/shard_map/ppermute | solution.py:165
  7.3 13.1 %collective-permute-start.2 = (bf16[144,3072]{1,0:T(8,128)(2,1)}, bf16[144,3072]{1,0:T(8,128)(2,1)S(1)}, u32[]{:S(2)}, u32[]{:S(2)}) collective-permute-start(bf16[144,3072]{1,0:T(8,128)(2,1)} %bitcast.64), channel_id=1, source_target_pairs={{0,4},{4,0},{1,5},{5,1},{2,6},{6,2},{3,7},{7,3},{8,12},{12,8},{9,1... | collective-permute-start | bytes 2654216 | tf_op jit(solution)/shard_map/ppermute | solution.py:165
  15.2 37.4 %collective-permute-start.3 = (bf16[128,3072]{1,0:T(8,128)(2,1)}, bf16[128,3072]{1,0:T(8,128)(2,1)}, u32[]{:S(2)}, u32[]{:S(2)}) collective-permute-start(bf16[128,3072]{1,0:T(8,128)(2,1)} %get-tuple-element.19), channel_id=1, source_target_pairs={{0,3},{1,0},{2,1},{3,2},{4,7},{5,4},{6,5},{7,6},{8,11},{9,8},{10,9... | collective-permute-start | bytes 2359304 | tf_op jit(solution)/shard_map/ppermute | solution.py:165
  18.2 36.6 %collective-permute-start.4 = (bf16[128,3072]{1,0:T(8,128)(2,1)}, bf16[128,3072]{1,0:T(8,128)(2,1)}, u32[]{:S(2)}, u32[]{:S(2)}) collective-permute-start(bf16[128,3072]{1,0:T(8,128)(2,1)} %get-tuple-element.20), channel_id=1, source_target_pairs={{0,2},{1,3},{2,0},{3,1},{4,6},{5,7},{6,4},{7,5},{8,10},{9,11},{10,... | collective-permute-start | bytes 2359304 | tf_op jit(solution)/shard_map/ppermute | solution.py:165
  18.8 38.3 %collective-permute-start.5 = (bf16[128,3072]{1,0:T(8,128)(2,1)}, bf16[128,3072]{1,0:T(8,128)(2,1)}, u32[]{:S(2)}, u32[]{:S(2)}) collective-permute-start(bf16[128,3072]{1,0:T(8,128)(2,1)} %get-tuple-element.18), channel_id=1, source_target_pairs={{0,1},{1,2},{2,3},{3,0},{4,5},{5,6},{6,7},{7,4},{8,9},{9,10},{10,1... | collective-permute-start | bytes 2359304 | tf_op jit(solution)/shard_map/ppermute | solution.py:165
  57.1 3.3 %copy-start.5 = (bf16[1,144,3072]{2,1,0:T(8,128)(2,1)S(1)}, bf16[1,144,3072]{2,1,0:T(8,128)(2,1)}, u32[]{:S(2)}) copy-start(bf16[1,144,3072]{2,1,0:T(8,128)(2,1)} %param.23) | copy-start | bytes 2654212
  60.4 51.7 %copy-start.7 = (f32[8]{0:T(128)S(1)}, f32[8]{0:T(128)}, u32[]{:S(2)}) copy-start(f32[8]{0:T(128)} %rate.5) | copy-start | bytes 100
  100.8 32.3 %collective-permute-start = (bf16[8,144,384]{2,1,0:T(8,128)(2,1)S(1)}, bf16[8,144,384]{2,1,0:T(8,128)(2,1)S(1)}, u32[]{:S(2)}, u32[]{:S(2)}) collective-permute-start(bf16[8,144,384]{2,1,0:T(8,128)(2,1)S(1)} %all_to_all.20), channel_id=1, source_target_pairs={{0,4},{4,0},{1,5},{5,1},{2,6},{6,2},{3,7},{7,3},{8,12},{12,8},{9,1... | collective-permute-start | bytes 2654216 | tf_op jit(solution)/shard_map/ppermute | solution.py:165
  106.6 17.0 %all-to-all-start = ((bf16[64,16,128]{2,1,0:T(8,128)(2,1)}), bf16[64,16,128]{2,1,0:T(8,128)(2,1)S(1)}, u32[]{:S(2)}, u32[]{:S(2)}) async-start(bf16[64,16,128]{2,1,0:T(8,128)(2,1)} %bitcast.61), calls=%async_computation | async-start | bytes 524288 | tf_op jit(solution)/shard_map/all_to_all | solution.py:196
  123.6 0.7 copy-start
  126.7 18.4 %all-to-all-start.1 = ((bf16[64,16,128]{2,1,0:T(8,128)(2,1)}), bf16[64,16,128]{2,1,0:T(8,128)(2,1)S(1)}, u32[]{:S(2)}, u32[]{:S(2)}) async-start(bf16[64,16,128]{2,1,0:T(8,128)(2,1)} %scan_states.1), calls=%async_computation.1 | async-start | bytes 524288 | tf_op jit(solution)/shard_map/all_to_all | solution.py:200
  133.2 0.9 copy-start.2
  135.5 19.7 %copy-start.6 = (s32[4,1]{0,1:T(1,128)S(1)}, s32[4,1]{0,1:T(1,128)}, u32[]{:S(2)}) copy-start(s32[4,1]{0,1:T(1,128)} %param.19) | copy-start | bytes 52
  138.3 28.5 %copy-start.8 = (f32[512]{0:T(512)S(1)}, f32[512]{0:T(512)}, u32[]{:S(2)}) copy-start(f32[512]{0:T(512)} %param.20) | copy-start | bytes 6148
  145.1 21.7 %copy-start.1 = (bf16[64,16,128]{2,1,0:T(8,128)(2,1)}, bf16[64,16,128]{2,1,0:T(8,128)(2,1)S(1)}, u32[]{:S(2)}) copy-start(bf16[64,16,128]{2,1,0:T(8,128)(2,1)S(1)} %all-to-all-done.1) | copy-start | bytes 786436
  145.1 44.5 %all-to-all-start.3 = ((bf16[32,48,128]{2,1,0:T(8,128)(2,1)}), bf16[32,48,128]{2,1,0:T(8,128)(2,1)S(1)}, u32[]{:S(2)}, u32[]{:S(2)}) async-start(bf16[32,48,128]{2,1,0:T(8,128)(2,1)} %bitcast.15), calls=%async_computation.3 | async-start | bytes 786432 | tf_op jit(solution)/shard_map/all_to_all | solution.py:243
Sparse Core Ops, SparseCore 0:
  60.5 58.9 all-gather.2

commit v2 on v1

v2 whole, which is shorter than its diff:
```python
import jax
import jax.numpy as jnp
from jax import lax
from jax.experimental import pallas as pl
from jax.experimental.pallas import tpu as pltpu
from jax.sharding import Mesh
from jax.sharding import PartitionSpec as P

BF = jnp.bfloat16
F32 = jnp.float32
CTX = ("z", "x", "core")
HEAD = 128
TILE = 128
GROUP = 4


def _state_kernel(rate, k, v, out):
    tokens = k.shape[0]
    first = pl.program_id(0) * GROUP
    t = lax.broadcasted_iota(jnp.int32, (tokens, HEAD), 0).astype(F32)
    for h in range(GROUP):
        at = slice(h * HEAD, (h + 1) * HEAD)
        decay = jnp.exp(-rate[first + h] * (tokens - t))
        scaled = (k[:, at].astype(F32) * decay).astype(BF)
        out[at, :] = lax.dot_general(
            scaled, v[:, at], (((0,), (0,)), ((), ())), preferred_element_type=F32
        ).astype(BF)


def local_states(rate, keys, values):
    tokens, width = keys.shape
    spec = pl.BlockSpec((tokens, GROUP * HEAD), lambda h: (0, h))
    return pl.pallas_call(
        _state_kernel,
        grid=(width // (GROUP * HEAD),),
        in_specs=[pl.BlockSpec(memory_space=pltpu.SMEM), spec, spec],
        out_specs=pl.BlockSpec((GROUP * HEAD, HEAD), lambda h: (h, 0)),
        out_shape=jax.ShapeDtypeStruct((width, HEAD), BF),
        name="local_states",
    )(rate, keys, values)


def _scan_kernel(decay, states, out):
    lam = decay[0]
    blocks = states.shape[0]
    carry = jnp.zeros(states.shape[1:], F32)
    for b in range(blocks):
        out[b] = carry.astype(BF)
        carry = carry * lam + states[b].astype(F32)


def scan_states(decay, states):
    return pl.pallas_call(
        _scan_kernel,
        in_specs=[
            pl.BlockSpec(memory_space=pltpu.SMEM),
            pl.BlockSpec(memory_space=pltpu.VMEM),
        ],
        out_specs=pl.BlockSpec(memory_space=pltpu.VMEM),
        out_shape=jax.ShapeDtypeStruct(states.shape, BF),
        name="scan_states",
    )(decay, states)


def _intra_kernel(rate, q, k, v, out):
    tokens = q.shape[0]
    first = pl.program_id(0) * GROUP
    i = lax.broadcasted_iota(jnp.int32, (tokens, tokens), 0)
    j = lax.broadcasted_iota(jnp.int32, (tokens, tokens), 1)
    off = (i - j).astype(F32)
    for h in range(GROUP):
        at = slice(h * HEAD, (h + 1) * HEAD)
        r = rate[first + h]
        within = jnp.where(off >= 0.0, jnp.exp(-r * jnp.maximum(off, 0.0)), 0.0)
        scores = lax.dot_general(
            q[:, at], k[:, at], (((1,), (1,)), ((), ())), preferred_element_type=F32
        )
        out[:, at] = jnp.dot(
            (scores * within).astype(BF), v[:, at], preferred_element_type=F32
        )


def intra_part(rate, queries, keys, values):
    tokens, width = keys.shape
    spec = pl.BlockSpec((tokens, GROUP * HEAD), lambda h: (0, h))
    return pl.pallas_call(
        _intra_kernel,
        grid=(width // (GROUP * HEAD),),
        in_specs=[pl.BlockSpec(memory_space=pltpu.SMEM), spec, spec, spec],
        out_specs=spec,
        out_shape=jax.ShapeDtypeStruct((tokens, width), F32),
        name="intra_part",
    )(rate, queries, keys, values)


def _mix_kernel(rate, intra, q, prefix, mixed, squares):
    tokens = q.shape[0]
    step = pl.program_id(0)
    t = lax.broadcasted_iota(jnp.int32, (tokens, HEAD), 0).astype(F32)
    total = jnp.zeros((tokens, HEAD), F32)
    for h in range(GROUP):
        at = slice(h * HEAD, (h + 1) * HEAD)
        r = rate[step * GROUP + h]
        inter = jnp.dot(q[:, at], prefix[at, :], preferred_element_type=F32)
        value = intra[:, at] + inter * jnp.exp(-r * t)
        mixed[:, at] = value
        total += value * value

    @pl.when(step == 0)
    def _():
        squares[...] = jnp.zeros_like(squares)

    squares[...] += jnp.sum(jnp.transpose(total), axis=0, keepdims=True)


def mix_part(rate, intra, queries, prefix):
    tokens, width = queries.shape
    spec = pl.BlockSpec((tokens, GROUP * HEAD), lambda h: (0, h))
    return pl.pallas_call(
        _mix_kernel,
        grid=(width // (GROUP * HEAD),),
        in_specs=[
            pl.BlockSpec(memory_space=pltpu.SMEM),
            spec,
            spec,
            pl.BlockSpec((GROUP * HEAD, HEAD), lambda h: (h, 0)),
        ],
        out_specs=[spec, pl.BlockSpec((1, tokens), lambda h: (0, 0))],
        out_shape=[
            jax.ShapeDtypeStruct((tokens, width), F32),
            jax.ShapeDtypeStruct((1, tokens), F32),
        ],
        name="mix_part",
    )(rate, intra, queries, prefix)


def _norm_kernel(features, total, mixed, gain, gates, out):
    tokens = mixed.shape[0]
    factor = lax.rsqrt(total[...] / features + 1e-06)
    column = jnp.transpose(jnp.broadcast_to(factor, (HEAD, tokens)))
    for h in range(GROUP):
        at = slice(h * HEAD, (h + 1) * HEAD)
        scaled = mixed[:, at] * column * gain[:, at]
        out[:, at] = (scaled * jax.nn.sigmoid(gates[:, at].astype(F32))).astype(BF)


def norm_part(features, total, mixed, gain, gates):
    tokens, width = mixed.shape
    spec = pl.BlockSpec((tokens, GROUP * HEAD), lambda h: (0, h))

    def kernel(*refs):
        _norm_kernel(features, *refs)

    return pl.pallas_call(
        kernel,
        grid=(width // (GROUP * HEAD),),
        in_specs=[
            pl.BlockSpec((1, tokens), lambda h: (0, 0)),
            spec,
            pl.BlockSpec((1, GROUP * HEAD), lambda h: (0, h)),
            spec,
        ],
        out_specs=spec,
        out_shape=jax.ShapeDtypeStruct((tokens, width), BF),
        name="norm_part",
    )(total, mixed, gain, gates)


def _pick_kernel(ids, place, rows, *refs):
    outs, sems = refs[:-1], refs[-1]
    tiles = ids.shape[0]
    n_exp = len(outs)
    me_e, me_core = place[0], place[1]
    copies = []
    for k in range(n_exp):
        target = lax.rem(me_e + k, n_exp)
        tile, rank = jnp.int32(0), jnp.int32(0)
        for t in range(tiles):
            same = ids[t, 0] == target
            tile = jnp.where(same & (rank == me_core), t, tile)
            rank = rank + same.astype(jnp.int32)
        start = pl.multiple_of(tile * TILE, TILE)
        copy = pltpu.make_async_copy(
            rows.at[pl.ds(start, TILE), :], outs[k], sems.at[k]
        )
        copy.start()
        copies.append(copy)
    for copy in copies:
        copy.wait()


def pick_tiles(ids, place, rows, n_exp):
    tile = jax.ShapeDtypeStruct((TILE, rows.shape[1]), rows.dtype)
    return pl.pallas_call(
        _pick_kernel,
        in_specs=[
            pl.BlockSpec(memory_space=pltpu.SMEM),
            pl.BlockSpec(memory_space=pltpu.SMEM),
            pl.BlockSpec(memory_space=pl.ANY),
        ],
        out_specs=[pl.BlockSpec(memory_space=pl.ANY)] * n_exp,
        out_shape=[tile] * n_exp,
        scratch_shapes=[pltpu.SemaphoreType.DMA((n_exp,))],
        name="pick_tiles",
    )(ids, place, rows)


def shift(array, axis, by):
    n = lax.axis_size(axis)
    return lax.ppermute(array, axis, [(i, (i + by) % n) for i in range(n)])


def on_device(
    queries, keys, values, gates, decay_rate, norm_gain,
    moe_rows, tile_expert, row_weight, w_gate, w_up, w_down,
):
    n_exp, n_z = lax.axis_size("exp"), lax.axis_size("z")
    n_x, n_core = lax.axis_size("x"), lax.axis_size("core")
    n_ctx = n_z * n_x * n_core
    me_e, me_core = lax.axis_index("exp"), lax.axis_index("core")
    tokens, width = queries.shape
    heads = width // HEAD
    model = moe_rows.shape[1]
    tiles = tile_expert.shape[0]

    ids = tile_expert[:, 0]
    order = jnp.arange(tiles)
    earlier = (ids[None, :] == ids[:, None]) & (order[None, :] < order[:, None])
    ranks = jnp.sum(earlier.astype(jnp.int32), axis=1)

    place = jnp.stack([me_e, me_core]).astype(jnp.int32)
    picked = pick_tiles(tile_expert, place, moe_rows, n_exp)
    arrived = [shift(rows, "exp", k) if k else rows for k, rows in enumerate(picked)]

    gate_own = jnp.swapaxes(w_gate[0], 0, 1)
    up_own = jnp.swapaxes(w_up[0], 0, 1)
    gate_other = shift(gate_own, "core", 1)
    up_other = shift(up_own, "core", 1)
    units = gate_own.shape[0]
    chunk = model // n_x
    columns = model // n_ctx
    gate_other, up_other, w_down, keys_late = lax.optimization_barrier(
        (gate_other, up_other, w_down, keys)
    )

    states = local_states(decay_rate, keys_late, values)
    pieces = states.reshape(n_ctx, width // n_ctx, HEAD)
    pieces = lax.all_to_all(pieces, CTX, 0, 0, tiled=True)
    mine = lax.axis_index(CTX) * (width // n_ctx) // HEAD
    lam = jnp.exp(-decay_rate * tokens)
    pieces = scan_states(lax.dynamic_slice(lam, (mine,), (1,)), pieces)
    prefix = lax.all_to_all(pieces, CTX, 0, 0, tiled=True).reshape(width, HEAD)
    intra = intra_part(decay_rate, queries, keys, values)
    split = w_down[0].reshape(units, n_z, n_x, n_core * columns)
    split = jnp.transpose(split, (2, 0, 1, 3)).reshape(n_x, units, chunk)
    me_x = lax.axis_index("x")
    down_own = jnp.zeros((n_x, units, chunk), BF)
    for k in range(n_x):
        part = lax.dynamic_index_in_dim(split, lax.rem(me_x + k, n_x), 0)
        part = shift(part, "x", k) if k else part
        source = lax.rem(me_x + n_x - k, n_x)
        down_own = lax.dynamic_update_slice(down_own, part, (source, 0, 0))
    down_other = shift(down_own, "core", 1)
    down = jnp.stack([down_own, down_other], axis=1)

    inner = jnp.concatenate([gate_own, gate_other, up_own, up_other], axis=0)
    arrived[1], down, intra = lax.optimization_barrier((arrived[1], down, intra))
    hidden = []
    for rows in arrived:
        both = lax.dot_general(
            inner, rows, (((1,), (1,)), ((), ())), preferred_element_type=F32
        )
        half = jax.nn.silu(both[: 2 * units]) * both[2 * units :]
        hidden.append(half.astype(BF))
    turned = [hidden[(-m) % n_exp] for m in range(n_exp)]
    twice = jnp.concatenate(turned + turned, axis=1)
    rows_here = n_exp * TILE
    hidden = lax.dynamic_slice(
        twice, (0, (n_exp - me_e) * TILE), (2 * units, rows_here)
    )
    hidden = lax.all_gather(hidden, "x")
    partial = lax.dot_general(
        down.reshape(n_x * 2 * units, chunk),
        hidden.reshape(n_x * 2 * units, rows_here),
        (((0,), (0,)), ((), ())),
        preferred_element_type=F32,
    ).astype(BF)
    parts = partial.reshape(n_z * n_core, columns, n_exp, TILE)
    parts = jnp.swapaxes(parts, 1, 2).reshape(-1, columns, TILE)
    parts, prefix = lax.optimization_barrier((parts, prefix))
    parts = lax.all_to_all(parts, ("z", "core", "exp"), 0, 0, tiled=True)
    mixed, squares = mix_part(decay_rate, intra, queries, prefix)
    total = lax.psum(squares, "exp")
    attention_out = norm_part(
        float(width * n_exp), total, mixed, norm_gain[None, :], gates
    )
    parts = parts.reshape(n_z, n_core * n_exp, columns, TILE)
    summed = jnp.sum(parts.astype(F32), axis=0).astype(BF)
    summed = lax.optimization_barrier(summed)
    picked = []
    for t in range(tiles):
        slot = ranks[t] * n_exp + ids[t]
        tile = lax.dynamic_index_in_dim(summed, slot, 0, keepdims=False)
        weight = row_weight[t * TILE : (t + 1) * TILE]
        picked.append((tile.astype(F32) * weight[None, :]).astype(BF))
    moe_out = jnp.swapaxes(jnp.concatenate(picked, axis=1), 0, 1)
    return attention_out, moe_out


def solution(mesh):
    n_core, n_x = 2, 4
    grid = mesh.devices.reshape(-1, n_x, n_core, mesh.devices.shape[1])
    fine = Mesh(grid, ("z", "x", "core", "exp"))
    placed = (
        P(CTX, "exp"),
        P(CTX, "exp"),
        P(CTX, "exp"),
        P(CTX, "exp"),
        P("exp"),
        P("exp"),
        P("exp", None),
        P("exp", None),
        P("exp"),
        P("exp", None, CTX),
        P("exp", None, CTX),
        P("exp", CTX, None),
    )
    return jax.shard_map(
        on_device,
        mesh=fine,
        in_specs=placed,
        out_specs=(P(CTX, "exp"), P("exp", CTX)),
        check_vma=False,
    )
```

time: 199 us -> 245 us (1.23)
  Pallas kernels: 26.4 us -> 110 us
  blocking collectives: 51.3 us -> 11.3 us
  starting transfers between devices: 25.8 us -> 34.6 us
  waiting for transfers between devices: 46.3 us -> 41 us
  local copies, waits for them, and re-layouts: 8.64 us -> 12.1 us
  between operations: 22 us -> 19.4 us
    pallas_call x4 -> x5, Pallas kernels: 24 us -> 108 us  [the longest x1 97.1 us: pick_tiles(): pl.pallas_call(_pick_kernel, in_specs=[pl.BlockSpec(memory_space=pltpu.SM...]
    all_to_all x1 -> x0, blocking collectives: 40.2 us -> none  [on_device(): down_own = lax.all_to_all(down_own, 'z', 0, 0, tiled=True)]
    ppermute x6 -> x9, waiting for transfers between devices: 29.5 us -> 20.8 us  [shift(): return lax.ppermute(array, axis, [(i, (i + by) % n) for i in range(n)])]
    all_to_all x1, starting transfers between devices: 5.42 us -> 11.8 us  [on_device(): pieces = lax.all_to_all(pieces, CTX, 0, 0, tiled=True)]
    ppermute x6 -> x9, starting transfers between devices: 5.21 us -> 9.96 us  [shift(): return lax.ppermute(array, axis, [(i, (i + by) % n) for i in range(n)])]
    another operation x0 -> x2, local copies, waits for them, and re-layouts: none -> 3.02 us  [on_device(): split = w_down[0].reshape(units, n_z, n_x, n_core * columns)]
    dynamic_slice x1, local copies, waits for them, and re-layouts: 3.07 us -> 0.07 us  [on_device(): part = lax.dynamic_index_in_dim(split, lax.rem(me_x + k, n_x), 0)]
  transfers between devices with their start and end apart: 10 -> 13, of which waited for: 3 -> 5; matrix products, arithmetic and copies ran while one was open for 10% -> 8% of each run, Pallas kernels for 13% -> 45%
where the time goes in v2:
time: 245 us; the launch traced here: 243 us
  Pallas kernels  110 us (45%)
  waiting for transfers between devices  41 us (17%)
  starting transfers between devices  34.6 us (14%)
  between operations  19.4 us (8%)
  local copies, waits for them, and re-layouts  12.1 us (5%)
  blocking collectives  11.3 us (5%)
  matrix products  10.2 us (4%)
  other arithmetic  3.98 us (2%)
    pallas_call x1, Pallas kernels, pick_tiles(): pl.pallas_call(_pick_kernel, in_specs=[pl.BlockSpec(memory_space=pltpu.SM...  97.1 us
    ppermute x9, waiting for transfers between devices, shift(): return lax.ppermute(array, axis, [(i, (i + by) % n) for i in range(n)])  20.8 us
    all_to_all x1, starting transfers between devices, on_device(): pieces = lax.all_to_all(pieces, CTX, 0, 0, tiled=True)  11.8 us
    all_to_all x1, waiting for transfers between devices, on_device(): pieces = lax.all_to_all(pieces, CTX, 0, 0, tiled=True)  11.3 us
    psum x1, blocking collectives, on_device(): total = lax.psum(squares, 'exp')  11.3 us
    ppermute x9, starting transfers between devices, shift(): return lax.ppermute(array, axis, [(i, (i + by) % n) for i in range(n)])  9.96 us
    all_to_all x1, waiting for transfers between devices, on_device(): prefix = lax.all_to_all(pieces, CTX, 0, 0, tiled=True).reshape(width, HEAD)  8.2 us
    dot_general x4, matrix products, on_device(): lax.dot_general(inner, rows, (((1,), (1,)), ((), ())), preferred_element_...  7.7 us
  transfers between devices with their start and end apart: 13, of which 5 were waited for; matrix products, arithmetic and copies ran while one was open for 8% of the time, Pallas kernels for 45%

profile of v2, /device:TPU:6, one launch (start us, length us, event | category | flops | bytes accessed | tf_op | source)
XLA Modules:
  0.0 242.7 jit_solution(11454280905787666181)
XLA Ops:
  7.8 1.3 copy.19.ids
  9.8 97.1 %pick_tiles.1 = (bf16[128,3072]{1,0:T(8,128)(2,1)}, bf16[128,3072]{1,0:T(8,128)(2,1)}, bf16[128,3072]{1,0:T(8,128)(2,1)}, bf16[128,3072]{1,0:T(8,128)(2,1)}) custom-call(s32[4,1]{1,0:T(4,128)} %copy.19.ids, s32[2]{0:T(128)} %pad_add_fusion.place, bf16[512,3072]{1,0:T(8,128)(2,1)} %rows.1), custom_call_target="tpu_custom_call" | custom-call | tf_op jit(solution)/shard_map/pick_tiles/pallas_call | solution.py:194
  106.9 1.7 collective-permute-start
  108.6 1.7 collective-permute-start.7
  110.2 2.0 collective-permute-start.8
  112.2 3.3 %intra_part.1.intra = f32[256,1024]{1,0:T(8,128)} custom-call(f32[8]{0:T(128)} %rate.5, bf16[256,1024]{1,0:T(8,128)(2,1)} %q.3, bf16[256,1024]{1,0:T(8,128)(2,1)} %k.2, bf16[256,1024]{1,0:T(8,128)(2,1)} %v.3), custom_call_target="tpu_custom_call" | custom-call | tf_op jit(solution)/shard_map/intra_part/pallas_call | solution.py:86
  115.5 1.0 copy-done.3
  116.6 0.9 copy-done.4
  117.5 2.9 %reshape_squeeze.3 = bf16[144,8,4,96]{3,2,1,0:T(4,128)(2,1)S(1)} reshape(bf16[1,144,3072]{2,1,0:T(8,128)(2,1)} %param.23) | data formatting | bytes 1769472 | tf_op jit(solution)/shard_map/reshape;squeeze | solution.py:254
  120.5 1.0 reshape.57
  122.2 2.4 collective-permute-start.4
  124.6 1.9 pad_maximum_fusion
  126.6 1.1 fusion.16
  127.7 16.7 %collective-permute-done.7 = bf16[128,3072]{1,0:T(8,128)(2,1)} collective-permute-done((bf16[128,3072]{1,0:T(8,128)(2,1)}, bf16[128,3072]{1,0:T(8,128)(2,1)}, u32[]{:S(2)}, u32[]{:S(2)}) %collective-permute-start.7) | collective-permute-done | bytes 786464 | tf_op jit(solution)/shard_map/ppermute | solution.py:210
  144.4 0.8 collective-permute-start.5
  145.2 2.2 fusion.17
  147.5 4.0 %collective-permute-done.5 = bf16[1,144,768]{2,1,0:T(8,128)(2,1)S(1)} collective-permute-done((bf16[1,144,768]{2,1,0:T(8,128)(2,1)S(1)}, bf16[1,144,768]{2,1,0:T(8,128)(2,1)S(1)}, u32[]{:S(2)}, u32[]{:S(2)}) %collective-permute-start.5) | collective-permute-done | bytes 221216 | tf_op jit(solution)/shard_map/ppermute | solution.py:210
  152.0 2.2 fusion.18
  154.5 2.2 fusion.19
  156.9 0.7 constant_dynamic-slice_fusion
  157.6 2.4 local_states.1
  160.0 11.8 %all-to-all-start = ((bf16[64,16,128]{2,1,0:T(8,128)(2,1)}), bf16[64,16,128]{2,1,0:T(8,128)(2,1)S(1)}, u32[]{:S(2)}, u32[]{:S(2)}) async-start(bf16[64,16,128]{2,1,0:T(8,128)(2,1)} %bitcast.62), calls=%async_computation | async-start | bytes 524288 | tf_op jit(solution)/shard_map/all_to_all | solution.py:248
  172.4 11.3 %all-to-all-done.states = bf16[64,16,128]{2,1,0:T(8,128)(2,1)S(1)} async-done(((bf16[64,16,128]{2,1,0:T(8,128)(2,1)}), bf16[64,16,128]{2,1,0:T(8,128)(2,1)S(1)}, u32[]{:S(2)}, u32[]{:S(2)}) %all-to-all-start) | async-done | bytes 262176 | tf_op jit(solution)/shard_map/all_to_all | solution.py:248
  184.5 2.4 scan_states.1
  186.9 6.0 %all-to-all-start.1 = ((bf16[64,16,128]{2,1,0:T(8,128)(2,1)}), bf16[64,16,128]{2,1,0:T(8,128)(2,1)S(1)}, u32[]{:S(2)}, u32[]{:S(2)}) async-start(bf16[64,16,128]{2,1,0:T(8,128)(2,1)} %scan_states.1), calls=%async_computation.1 | async-start | bytes 524288 | tf_op jit(solution)/shard_map/all_to_all | solution.py:252
  193.0 2.5 %convolution_convert_fusion = bf16[768,512]{1,0:T(8,128)(2,1)S(1)} fusion(bf16[1152,768]{1,0:T(8,128)(2,1)S(1)} %bitcast.61, bf16[1152,512]{1,0:T(8,128)(2,1)} %all-gather.3.cloned.1.call-done), kind=kOutput, calls=%fused_computation.2 | convolution fusion | flops 906362880 | bytes 3735552 | tf_op jit(solution)/shard_map/dot_general | solution.py:282
  195.7 1.0 copy.22
  196.7 8.2 %all-to-all-done.1 = bf16[64,16,128]{2,1,0:T(8,128)(2,1)S(1)} async-done(((bf16[64,16,128]{2,1,0:T(8,128)(2,1)}), bf16[64,16,128]{2,1,0:T(8,128)(2,1)S(1)}, u32[]{:S(2)}, u32[]{:S(2)}) %all-to-all-start.1) | async-done | bytes 262176 | tf_op jit(solution)/shard_map/all_to_all | solution.py:252
  204.9 6.8 %all-to-all-start.2 = ((bf16[64,48,128]{2,1,0:T(8,128)(2,1)}), bf16[64,48,128]{2,1,0:T(8,128)(2,1)S(1)}, u32[]{:S(2)}, u32[]{:S(2)}) async-start(bf16[64,48,128]{2,1,0:T(8,128)(2,1)} %bitcast.14), calls=%async_computation.2 | async-start | bytes 1572864 | tf_op jit(solution)/shard_map/all_to_all | solution.py:291
  218.2 2.6 %mix_part.1 = (f32[256,1024]{1,0:T(8,128)}, f32[1,256]{1,0:T(1,128)}) custom-call(f32[8]{0:T(128)} %rate.5, f32[256,1024]{1,0:T(8,128)} %intra_part.1.intra, bf16[256,1024]{1,0:T(8,128)(2,1)} %q.3, bf16[1024,128]{1,0:T(8,128)(2,1)} %bitcast.63), custom_call_target="tpu_custom_call" | custom-call | tf_op jit(solution)/shard_map/mix_part/pallas_call | solution.py:119
  220.9 11.3 %psum.7.refs_0_ = f32[1,256]{1,0:T(1,128)} all-reduce(f32[1,256]{1,0:T(1,128)} %get-tuple-element.29), channel_id=1, replica_groups=mesh['z'=8,'x'=4,'core'=2,'exp'=4] {'exp'}, use_global_device_ids=true, to_apply=%region_0.0 | all-reduce | flops 256 | bytes 2048 | tf_op jit(solution)/shard_map/psum | solution.py:293
  232.1 2.3 norm_part.1
  (57 shorter events, 7.5 us)
Async XLA Ops:
  7.2 185.8 %all-gather.3.cloned.1.call-start = ((), (), s32[]{:S(2)}) async-start(), calls=%async_computation.3 | async-start | bytes 1474560 | tf_op jit(solution)/shard_map/all_gather | solution.py:281
  7.2 108.3 %collective-permute-start.1 = (bf16[144,3072]{1,0:T(8,128)(2,1)}, bf16[144,3072]{1,0:T(8,128)(2,1)S(1)}, u32[]{:S(2)}, u32[]{:S(2)}) collective-permute-start(bf16[144,3072]{1,0:T(8,128)(2,1)} %bitcast.67), channel_id=1, source_target_pairs={{0,4},{4,0},{1,5},{5,1},{2,6},{6,2},{3,7},{7,3},{8,12},{12,8},{9,1... | collective-permute-start | bytes 2654216 | tf_op jit(solution)/shard_map/ppermute | solution.py:210
  7.3 108.2 %collective-permute-start.2 = (bf16[144,3072]{1,0:T(8,128)(2,1)}, bf16[144,3072]{1,0:T(8,128)(2,1)S(1)}, u32[]{:S(2)}, u32[]{:S(2)}) collective-permute-start(bf16[144,3072]{1,0:T(8,128)(2,1)} %bitcast.65), channel_id=1, source_target_pairs={{0,4},{4,0},{1,5},{5,1},{2,6},{6,2},{3,7},{7,3},{8,12},{12,8},{9,1... | collective-permute-start | bytes 2654216 | tf_op jit(solution)/shard_map/ppermute | solution.py:210
  106.9 47.5 %collective-permute-start = (bf16[128,3072]{1,0:T(8,128)(2,1)}, bf16[128,3072]{1,0:T(8,128)(2,1)}, u32[]{:S(2)}, u32[]{:S(2)}) collective-permute-start(bf16[128,3072]{1,0:T(8,128)(2,1)} %get-tuple-element.17), channel_id=1, source_target_pairs={{0,1},{1,2},{2,3},{3,0},{4,5},{5,6},{6,7},{7,4},{8,9},{9,10},{10,1... | collective-permute-start | bytes 2359304 | tf_op jit(solution)/shard_map/ppermute | solution.py:210
  108.6 35.8 %collective-permute-start.7 = (bf16[128,3072]{1,0:T(8,128)(2,1)}, bf16[128,3072]{1,0:T(8,128)(2,1)}, u32[]{:S(2)}, u32[]{:S(2)}) collective-permute-start(bf16[128,3072]{1,0:T(8,128)(2,1)} %get-tuple-element.24), channel_id=1, source_target_pairs={{0,3},{1,0},{2,1},{3,2},{4,7},{5,4},{6,5},{7,6},{8,11},{9,8},{10,9... | collective-permute-start | bytes 2359304 | tf_op jit(solution)/shard_map/ppermute | solution.py:210
  110.2 41.7 %collective-permute-start.8 = (bf16[128,3072]{1,0:T(8,128)(2,1)}, bf16[128,3072]{1,0:T(8,128)(2,1)}, u32[]{:S(2)}, u32[]{:S(2)}) collective-permute-start(bf16[128,3072]{1,0:T(8,128)(2,1)} %get-tuple-element.25), channel_id=1, source_target_pairs={{0,2},{1,3},{2,0},{3,1},{4,6},{5,7},{6,4},{7,5},{8,10},{9,11},{10,... | collective-permute-start | bytes 2359304 | tf_op jit(solution)/shard_map/ppermute | solution.py:210
  115.5 1.0 copy-start.3
  116.6 0.9 copy-start.4
  120.3 4.3 %copy-start.2 = (bf16[1,3072,144]{1,2,0:T(8,128)(2,1)S(1)}, bf16[1,3072,144]{1,2,0:T(8,128)(2,1)}, u32[]{:S(2)}) copy-start(bf16[1,3072,144]{1,2,0:T(8,128)(2,1)} %param.22) | copy-start | bytes 2654212
  121.6 25.8 %collective-permute-start.3 = (bf16[1,144,768]{2,1,0:T(8,128)(2,1)S(1)}, bf16[1,144,768]{2,1,0:T(8,128)(2,1)S(1)}, u32[]{:S(2)}, u32[]{:S(2)}) collective-permute-start(bf16[1,144,768]{2,1,0:T(8,128)(2,1)S(1)} %get-tuple-element.42), channel_id=1, source_target_pairs={{0,8},{8,16},{16,24},{24,0},{1,9},{9,17},{17,25},{25,1},{2,10},{10... | collective-permute-start | bytes 663560 | tf_op jit(solution)/shard_map/ppermute | solution.py:210
  122.2 4.4 %copy-start.5 = (bf16[128,3072]{1,0:T(8,128)(2,1)S(1)}, bf16[128,3072]{1,0:T(8,128)(2,1)}, u32[]{:S(2)}) copy-start(bf16[128,3072]{1,0:T(8,128)(2,1)} %get-tuple-element.23) | copy-start | bytes 2359300
  122.2 25.3 %collective-permute-start.4 = (bf16[1,144,768]{2,1,0:T(8,128)(2,1)S(1)}, bf16[1,144,768]{2,1,0:T(8,128)(2,1)S(1)}, u32[]{:S(2)}, u32[]{:S(2)}) collective-permute-start(bf16[1,144,768]{2,1,0:T(8,128)(2,1)S(1)} %get-tuple-element.41), channel_id=1, source_target_pairs={{0,16},{8,24},{16,0},{24,8},{1,17},{9,25},{17,1},{25,9},{2,18},{10... | collective-permute-start | bytes 663560 | tf_op jit(solution)/shard_map/ppermute | solution.py:210
  144.4 7.1 %collective-permute-start.5 = (bf16[1,144,768]{2,1,0:T(8,128)(2,1)S(1)}, bf16[1,144,768]{2,1,0:T(8,128)(2,1)S(1)}, u32[]{:S(2)}, u32[]{:S(2)}) collective-permute-start(bf16[1,144,768]{2,1,0:T(8,128)(2,1)S(1)} %get-tuple-element.40), channel_id=1, source_target_pairs={{0,24},{8,0},{16,8},{24,16},{1,25},{9,1},{17,9},{25,17},{2,26},{10... | collective-permute-start | bytes 663560 | tf_op jit(solution)/shard_map/ppermute | solution.py:210
  151.5 2.7 %collective-permute-start.6 = (bf16[4,144,768]{2,1,0:T(8,128)(2,1)S(1)}, bf16[4,144,768]{2,1,0:T(8,128)(2,1)S(1)}, u32[]{:S(2)}, u32[]{:S(2)}) collective-permute-start(bf16[4,144,768]{2,1,0:T(8,128)(2,1)S(1)} %constant_dynamic-update-slice_fusion.8), channel_id=1, source_target_pairs={{0,4},{4,0},{1,5},{5,1},{2,6},{6,2},{3,7},{7,3},{8,12},{12,8},{9,1... | collective-permute-start | bytes 2654216 | tf_op jit(solution)/shard_map/ppermute | solution.py:210
  154.4 17.4 %copy-start.7 = (f32[8]{0:T(128)S(1)}, f32[8]{0:T(128)}, u32[]{:S(2)}) copy-start(f32[8]{0:T(128)} %rate.5) | copy-start | bytes 100
  160.0 23.8 %all-to-all-start = ((bf16[64,16,128]{2,1,0:T(8,128)(2,1)}), bf16[64,16,128]{2,1,0:T(8,128)(2,1)S(1)}, u32[]{:S(2)}, u32[]{:S(2)}) async-start(bf16[64,16,128]{2,1,0:T(8,128)(2,1)} %bitcast.62), calls=%async_computation | async-start | bytes 524288 | tf_op jit(solution)/shard_map/all_to_all | solution.py:248
  183.8 0.7 copy-start
  186.9 18.0 %all-to-all-start.1 = ((bf16[64,16,128]{2,1,0:T(8,128)(2,1)}), bf16[64,16,128]{2,1,0:T(8,128)(2,1)S(1)}, u32[]{:S(2)}, u32[]{:S(2)}) async-start(bf16[64,16,128]{2,1,0:T(8,128)(2,1)} %scan_states.1), calls=%async_computation.1 | async-start | bytes 524288 | tf_op jit(solution)/shard_map/all_to_all | solution.py:252
  195.4 16.3 %copy-start.6 = (s32[4,1]{0,1:T(1,128)S(1)}, s32[4,1]{0,1:T(1,128)}, u32[]{:S(2)}) copy-start(s32[4,1]{0,1:T(1,128)} %param.19) | copy-start | bytes 52
  195.5 22.7 %copy-start.8 = (f32[512]{0:T(512)S(1)}, f32[512]{0:T(512)}, u32[]{:S(2)}) copy-start(f32[512]{0:T(512)} %param.20) | copy-start | bytes 6148
  204.9 13.3 %copy-start.1 = (bf16[64,16,128]{2,1,0:T(8,128)(2,1)}, bf16[64,16,128]{2,1,0:T(8,128)(2,1)S(1)}, u32[]{:S(2)}) copy-start(bf16[64,16,128]{2,1,0:T(8,128)(2,1)S(1)} %all-to-all-done.1) | copy-start | bytes 786436
  204.9 30.2 %all-to-all-start.2 = ((bf16[64,48,128]{2,1,0:T(8,128)(2,1)}), bf16[64,48,128]{2,1,0:T(8,128)(2,1)S(1)}, u32[]{:S(2)}, u32[]{:S(2)}) async-start(bf16[64,48,128]{2,1,0:T(8,128)(2,1)} %bitcast.14), calls=%async_computation.2 | async-start | bytes 1572864 | tf_op jit(solution)/shard_map/all_to_all | solution.py:291
Sparse Core Ops, SparseCore 0:
  157.7 31.2 all-gather.2

commit v3 on v2

--- a/solution.py
+++ b/solution.py
@@ -167,29 +167,34 @@
 
 
 def _pick_kernel(ids, place, rows, *refs):
-    outs, sems = refs[:-1], refs[-1]
+    n_exp = place[2]
+    outs, held, into, out_of = refs[:-3], refs[-3], refs[-2], refs[-1]
     tiles = ids.shape[0]
-    n_exp = len(outs)
-    me_e, me_core = place[0], place[1]
-    copies = []
-    for k in range(n_exp):
-        target = lax.rem(me_e + k, n_exp)
+    loads = []
+    for k in range(len(outs)):
+        target = lax.rem(place[0] + k + 1, n_exp)
         tile, rank = jnp.int32(0), jnp.int32(0)
         for t in range(tiles):
             same = ids[t, 0] == target
-            tile = jnp.where(same & (rank == me_core), t, tile)
+            tile = jnp.where(same & (rank == place[1]), t, tile)
             rank = rank + same.astype(jnp.int32)
         start = pl.multiple_of(tile * TILE, TILE)
-        copy = pltpu.make_async_copy(
-            rows.at[pl.ds(start, TILE), :], outs[k], sems.at[k]
+        load = pltpu.make_async_copy(
+            rows.at[pl.ds(start, TILE), :], held.at[k], into.at[k]
         )
-        copy.start()
-        copies.append(copy)
-    for copy in copies:
-        copy.wait()
-
-
-def pick_tiles(ids, place, rows, n_exp):
+        load.start()
+        loads.append(load)
+    stores = []
+    for k, load in enumerate(loads):
+        load.wait()
+        store = pltpu.make_async_copy(held.at[k], outs[k], out_of.at[k])
+        store.start()
+        stores.append(store)
+    for store in stores:
+        store.wait()
+
+
+def pick_tiles(ids, place, rows, count):
     tile = jax.ShapeDtypeStruct((TILE, rows.shape[1]), rows.dtype)
     return pl.pallas_call(
         _pick_kernel,
@@ -198,9 +203,13 @@
             pl.BlockSpec(memory_space=pltpu.SMEM),
             pl.BlockSpec(memory_space=pl.ANY),
         ],
-        out_specs=[pl.BlockSpec(memory_space=pl.ANY)] * n_exp,
-        out_shape=[tile] * n_exp,
-        scratch_shapes=[pltpu.SemaphoreType.DMA((n_exp,))],
+        out_specs=[pl.BlockSpec(memory_space=pl.ANY)] * count,
+        out_shape=[tile] * count,
+        scratch_shapes=[
+            pltpu.VMEM((count, TILE, rows.shape[1]), rows.dtype),
+            pltpu.SemaphoreType.DMA((count,)),
+            pltpu.SemaphoreType.DMA((count,)),
+        ],
         name="pick_tiles",
     )(ids, place, rows)
 
@@ -228,9 +237,10 @@
     earlier = (ids[None, :] == ids[:, None]) & (order[None, :] < order[:, None])
     ranks = jnp.sum(earlier.astype(jnp.int32), axis=1)
 
-    place = jnp.stack([me_e, me_core]).astype(jnp.int32)
+    place = jnp.stack([me_e, me_core, n_exp]).astype(jnp.int32)
     picked = pick_tiles(tile_expert, place, moe_rows, n_exp)
-    arrived = [shift(rows, "exp", k) if k else rows for k, rows in enumerate(picked)]
+    arrived = [picked[-1]]
+    arrived += [shift(picked[k - 1], "exp", k) for k in range(1, n_exp)]
 
     gate_own = jnp.swapaxes(w_gate[0], 0, 1)
     up_own = jnp.swapaxes(w_up[0], 0, 1)
@@ -249,6 +259,7 @@
     mine = lax.axis_index(CTX) * (width // n_ctx) // HEAD
     lam = jnp.exp(-decay_rate * tokens)
     pieces = scan_states(lax.dynamic_slice(lam, (mine,), (1,)), pieces)
+    arrived[2], pieces = lax.optimization_barrier((arrived[2], pieces))
     prefix = lax.all_to_all(pieces, CTX, 0, 0, tiled=True).reshape(width, HEAD)
     intra = intra_part(decay_rate, queries, keys, values)
     split = w_down[0].reshape(units, n_z, n_x, n_core * columns)
@@ -265,28 +276,30 @@
 
     inner = jnp.concatenate([gate_own, gate_other, up_own, up_other], axis=0)
     arrived[1], down, intra = lax.optimization_barrier((arrived[1], down, intra))
-    hidden = []
-    for rows in arrived:
-        both = lax.dot_general(
-            inner, rows, (((1,), (1,)), ((), ())), preferred_element_type=F32
-        )
-        half = jax.nn.silu(both[: 2 * units]) * both[2 * units :]
-        hidden.append(half.astype(BF))
-    turned = [hidden[(-m) % n_exp] for m in range(n_exp)]
-    twice = jnp.concatenate(turned + turned, axis=1)
-    rows_here = n_exp * TILE
-    hidden = lax.dynamic_slice(
-        twice, (0, (n_exp - me_e) * TILE), (2 * units, rows_here)
-    )
-    hidden = lax.all_gather(hidden, "x")
-    partial = lax.dot_general(
-        down.reshape(n_x * 2 * units, chunk),
-        hidden.reshape(n_x * 2 * units, rows_here),
-        (((0,), (0,)), ((), ())),
-        preferred_element_type=F32,
-    ).astype(BF)
-    parts = partial.reshape(n_z * n_core, columns, n_exp, TILE)
-    parts = jnp.swapaxes(parts, 1, 2).reshape(-1, columns, TILE)
+    down = down.reshape(n_x * 2 * units, chunk)
+    parts = jnp.zeros((n_z * n_core, n_exp, columns, TILE), BF)
+    for pair in ((0, 1), (3, 2)):
+        hidden = []
+        for k in pair:
+            both = lax.dot_general(
+                inner, arrived[k], (((1,), (1,)), ((), ())), preferred_element_type=F32
+            )
+            half = jax.nn.silu(both[: 2 * units]) * both[2 * units :]
+            hidden.append(half.astype(BF))
+        hidden = lax.all_gather(jnp.concatenate(hidden, axis=1), "x")
+        partial = lax.dot_general(
+            down,
+            hidden.reshape(n_x * 2 * units, len(pair) * TILE),
+            (((0,), (0,)), ((), ())),
+            preferred_element_type=F32,
+        ).astype(BF)
+        partial = partial.reshape(n_z * n_core, 1, columns, len(pair) * TILE)
+        for i, k in enumerate(pair):
+            source = lax.rem(me_e + n_exp - k, n_exp)
+            parts = lax.dynamic_update_slice(
+                parts, partial[..., i * TILE : (i + 1) * TILE], (0, source, 0, 0)
+            )
+    parts = parts.reshape(-1, columns, TILE)
     parts, prefix = lax.optimization_barrier((parts, prefix))
     parts = lax.all_to_all(parts, ("z", "core", "exp"), 0, 0, tiled=True)
     mixed, squares = mix_part(decay_rate, intra, queries, prefix)

time: 245 us -> 150 us (0.61)
  Pallas kernels: 110 us -> 17.1 us
  waiting for transfers between devices: 41 us -> 10.8 us
  blocking collectives: 11.3 us -> 38.6 us
  between operations: 19.4 us -> 5.93 us
  starting transfers between devices: 34.6 us -> 42.9 us
  other arithmetic: 3.98 us -> 8.8 us
    pallas_call x1, Pallas kernels: 97.1 us -> 3.76 us  [pick_tiles(): pl.pallas_call(_pick_kernel, in_specs=[pl.BlockSpec(memory_space=pltpu.SM...]
    all_gather x0 -> x2, blocking collectives: none -> 27.4 us  [on_device(): hidden = lax.all_gather(jnp.concatenate(hidden, axis=1), 'x')]
    all_to_all x1, waiting for transfers between devices: 11.3 us -> 0.01 us  [on_device(): pieces = lax.all_to_all(pieces, CTX, 0, 0, tiled=True)]
    ppermute x9, waiting for transfers between devices: 20.8 us -> 10.1 us  [shift(): return lax.ppermute(array, axis, [(i, (i + by) % n) for i in range(n)])]
    all_to_all x1, waiting for transfers between devices: 8.2 us -> 0.01 us  [on_device(): prefix = lax.all_to_all(pieces, CTX, 0, 0, tiled=True).reshape(width, HEAD)]
    all_to_all x1, starting transfers between devices: 6.02 us -> 12 us  [on_device(): prefix = lax.all_to_all(pieces, CTX, 0, 0, tiled=True).reshape(width, HEAD)]
    dynamic_update_slice x0 -> x4, local copies, waits for them, and re-layouts: none -> 2.93 us  [on_device(): lax.dynamic_update_slice(parts, partial[..., i * TILE:(i + 1) * TILE], (0...]
    unnamed x22 -> x15, local copies, waits for them, and re-layouts: 4.06 us -> 1.35 us
  transfers between devices with their start and end apart: 13 -> 12, of which waited for: 5 -> 3; matrix products, arithmetic and copies ran while one was open for 8% -> 22% of each run, Pallas kernels for 45% -> 12%
where the time goes in v3:
time: 150 us; the launch traced here: 148 us
  starting transfers between devices  42.9 us (29%)
  blocking collectives  38.6 us (26%)
  Pallas kernels  17.1 us (11%)
  local copies, waits for them, and re-layouts  13.3 us (9%)
  waiting for transfers between devices  10.8 us (7%)
  matrix products  10.6 us (7%)
  other arithmetic  8.8 us (6%)
  between operations  5.93 us (4%)
    all_gather x2, blocking collectives, on_device(): hidden = lax.all_gather(jnp.concatenate(hidden, axis=1), 'x')  27.4 us
    all_to_all x1, starting transfers between devices, on_device(): pieces = lax.all_to_all(pieces, CTX, 0, 0, tiled=True)  12.2 us
    all_to_all x1, starting transfers between devices, on_device(): prefix = lax.all_to_all(pieces, CTX, 0, 0, tiled=True).reshape(width, HEAD)  12 us
    psum x1, blocking collectives, on_device(): total = lax.psum(squares, 'exp')  11.3 us
    ppermute x9, waiting for transfers between devices, shift(): return lax.ppermute(array, axis, [(i, (i + by) % n) for i in range(n)])  10.1 us
    ppermute x9, starting transfers between devices, shift(): return lax.ppermute(array, axis, [(i, (i + by) % n) for i in range(n)])  9.66 us
    dot_general x4, matrix products, on_device(): lax.dot_general(inner, arrived[k], (((1,), (1,)), ((), ())), preferred_el...  9.18 us
    all_to_all x1, starting transfers between devices, on_device(): parts = lax.all_to_all(parts, ('z', 'core', 'exp'), 0, 0, tiled=True)  9.08 us
  transfers between devices with their start and end apart: 12, of which 3 were waited for; matrix products, arithmetic and copies ran while one was open for 22% of the time, Pallas kernels for 12%

profile of v3, /device:TPU:6, one launch (start us, length us, event | category | flops | bytes accessed | tf_op | source)
XLA Modules:
  0.0 148.1 jit_solution(13157537299605219466)
XLA Ops:
  1.2 1.3 copy.22.ids
  3.2 3.8 %pick_tiles.1 = (bf16[128,3072]{1,0:T(8,128)(2,1)}, bf16[128,3072]{1,0:T(8,128)(2,1)}, bf16[128,3072]{1,0:T(8,128)(2,1)}, bf16[128,3072]{1,0:T(8,128)(2,1)}) custom-call(s32[4,1]{1,0:T(4,128)} %copy.22.ids, s32[3]{0:T(128)} %pad_add_fusion.place, bf16[512,3072]{1,0:T(8,128)(2,1)} %rows.1), custom_call_target="tpu_custom_call" | custom-call | tf_op jit(solution)/shard_map/pick_tiles/pallas_call | solution.py:199
  7.0 3.3 %collective-permute-start.8 = (bf16[128,3072]{1,0:T(8,128)(2,1)}, bf16[128,3072]{1,0:T(8,128)(2,1)}, u32[]{:S(2)}, u32[]{:S(2)}) collective-permute-start(bf16[128,3072]{1,0:T(8,128)(2,1)} %get-tuple-element.28), channel_id=1, source_target_pairs={{0,2},{1,3},{2,0},{3,1},{4,6},{5,7},{6,4},{7,5},{8,10},{9,11},{10,... | collective-permute-start | bytes 2359304 | tf_op jit(solution)/shard_map/ppermute | solution.py:219
  10.2 1.1 collective-permute-start.7
  11.3 1.0 collective-permute-start
  13.5 3.3 %intra_part.1.intra = f32[256,1024]{1,0:T(8,128)} custom-call(f32[8]{0:T(128)} %rate.5, bf16[256,1024]{1,0:T(8,128)(2,1)} %q.3, bf16[256,1024]{1,0:T(8,128)(2,1)} %k.2, bf16[256,1024]{1,0:T(8,128)(2,1)} %v.3), custom_call_target="tpu_custom_call" | custom-call | tf_op jit(solution)/shard_map/intra_part/pallas_call | solution.py:86
  16.8 2.8 %local_states.1 = bf16[1024,128]{1,0:T(8,128)(2,1)} custom-call(f32[8]{0:T(128)} %rate.5, bf16[256,1024]{1,0:T(8,128)(2,1)} %k.2, bf16[256,1024]{1,0:T(8,128)(2,1)} %v.3), custom_call_target="tpu_custom_call" | custom-call | tf_op jit(solution)/shard_map/local_states/pallas_call | solution.py:33
  19.6 12.2 %all-to-all-start = ((bf16[64,16,128]{2,1,0:T(8,128)(2,1)}), bf16[64,16,128]{2,1,0:T(8,128)(2,1)}, u32[]{:S(2)}, u32[]{:S(2)}) async-start(bf16[64,16,128]{2,1,0:T(8,128)(2,1)} %bitcast.70), calls=%async_computation | async-start | bytes 524288 | tf_op jit(solution)/shard_map/all_to_all | solution.py:258
  31.8 1.1 reshape_squeeze.3
  33.1 1.0 reshape.63
  34.1 1.0 broadcast_in_dim.6
  36.3 2.4 %collective-permute-start.4 = (bf16[1,144,768]{2,1,0:T(8,128)(2,1)S(1)}, bf16[1,144,768]{2,1,0:T(8,128)(2,1)S(1)}, u32[]{:S(2)}, u32[]{:S(2)}) collective-permute-start(bf16[1,144,768]{2,1,0:T(8,128)(2,1)S(1)} %get-tuple-element.37), channel_id=1, source_target_pairs={{0,16},{8,24},{16,0},{24,8},{1,17},{9,25},{17,1},{25,9},{2,18},{10... | collective-permute-start | bytes 663560 | tf_op jit(solution)/shard_map/ppermute | solution.py:219
  38.7 2.2 %pad_maximum_fusion = bf16[576,3072]{1,0:T(8,128)(2,1)S(1)} fusion(bf16[144,3072]{1,0:T(8,128)(2,1)} %copy-done.2, bf16[144,3072]{1,0:T(8,128)(2,1)} %bitcast.72, bf16[144,3072]{1,0:T(8,128)(2,1)} %copy-done.1, bf16[144,3072]{1,0:T(8,128)(2,1)} %bitcast.74), kind=kLoop, calls=%fused_computation | loop fusion | flops 14155776 | bytes 7077888 | tf_op jit(solution)/shard_map/concatenate | solution.py:277
  41.0 1.8 %fusion.12 = f32[576,128]{1,0:T(8,128)} fusion(bf16[576,3072]{1,0:T(8,128)(2,1)S(1)} %pad_maximum_fusion, bf16[128,3072]{1,0:T(8,128)(2,1)S(1)} %copy-done.4), kind=kOutput, calls=%fused_computation.43 | convolution fusion | flops 452984832 | bytes 4620288 | tf_op jit(solution)/shard_map/dot_general | solution.py:284
  42.7 3.7 %collective-permute-done.7 = bf16[128,3072]{1,0:T(8,128)(2,1)} collective-permute-done((bf16[128,3072]{1,0:T(8,128)(2,1)}, bf16[128,3072]{1,0:T(8,128)(2,1)}, u32[]{:S(2)}, u32[]{:S(2)}) %collective-permute-start.7) | collective-permute-done | bytes 786464 | tf_op jit(solution)/shard_map/ppermute | solution.py:219
  46.5 2.2 %fusion.14 = f32[576,128]{1,0:T(8,128)S(1)} fusion(bf16[576,3072]{1,0:T(8,128)(2,1)S(1)} %pad_maximum_fusion, bf16[128,3072]{1,0:T(8,128)(2,1)} %collective-permute-done.7), kind=kOutput, calls=%fused_computation.45 | convolution fusion | flops 452984832 | bytes 4620288 | tf_op jit(solution)/shard_map/dot_general | solution.py:284
  49.4 0.8 collective-permute-start.5
  51.6 6.3 %collective-permute-done.5 = bf16[1,144,768]{2,1,0:T(8,128)(2,1)S(1)} collective-permute-done((bf16[1,144,768]{2,1,0:T(8,128)(2,1)S(1)}, bf16[1,144,768]{2,1,0:T(8,128)(2,1)S(1)}, u32[]{:S(2)}, u32[]{:S(2)}) %collective-permute-start.5) | collective-permute-done | bytes 221216 | tf_op jit(solution)/shard_map/ppermute | solution.py:219
  58.7 2.4 %scan_states.1 = bf16[64,16,128]{2,1,0:T(8,128)(2,1)} custom-call(f32[1]{0:T(128)} %dynamic_slice.33.decay, bf16[64,16,128]{2,1,0:T(8,128)(2,1)} %all-to-all-done.states), custom_call_target="tpu_custom_call" | custom-call | tf_op jit(solution)/shard_map/scan_states/pallas_call | solution.py:53
  61.1 2.9 %fusion.15 = f32[576,128]{1,0:T(8,128)} fusion(bf16[576,3072]{1,0:T(8,128)(2,1)S(1)} %pad_maximum_fusion, bf16[128,3072]{1,0:T(8,128)(2,1)} %collective-permute-done.8), kind=kOutput, calls=%fused_computation.46 | convolution fusion | flops 452984832 | bytes 4620288 | tf_op jit(solution)/shard_map/dot_general | solution.py:284
  64.1 12.0 %all-to-all-start.1 = ((bf16[64,16,128]{2,1,0:T(8,128)(2,1)}), bf16[64,16,128]{2,1,0:T(8,128)(2,1)}, u32[]{:S(2)}, u32[]{:S(2)}) async-start(bf16[64,16,128]{2,1,0:T(8,128)(2,1)} %scan_states.1), calls=%async_computation.1 | async-start | bytes 524288 | tf_op jit(solution)/shard_map/all_to_all | solution.py:263
  76.1 1.0 fusion
  77.1 0.9 pad_maximum_fusion.3
  78.0 14.0 %all-gather.1 = bf16[1152,256]{1,0:T(8,128)(2,1)S(1)} all-gather(bf16[288,256]{1,0:T(8,128)(2,1)S(1)} %pad_maximum_fusion.3), channel_id=3, replica_groups=mesh['z'=8,'x'=4,'core'=2,'exp'=4] {'x'}, dimensions={0}, use_global_device_ids=true | all-gather | bytes 737280 | tf_op jit(solution)/shard_map/all_gather | solution.py:289
  92.0 1.6 %pad_maximum_fusion.1 = bf16[4,2,144,768]{3,2,1,0:T(8,128)(2,1)S(1)} fusion(bf16[4,1,144,768]{3,2,1,0:T(8,128)(2,1)} %bitcast.9, bf16[4,1,144,768]{3,2,1,0:T(8,128)(2,1)} %bitcast.8), kind=kLoop, calls=%fused_computation.1 | loop fusion | flops 884736 | bytes 3538944 | tf_op jit(solution)/shard_map/stack | solution.py:275
  93.6 2.2 %fusion.13 = f32[576,128]{1,0:T(8,128)S(1)} fusion(bf16[576,3072]{1,0:T(8,128)(2,1)S(1)} %pad_maximum_fusion, bf16[128,3072]{1,0:T(8,128)(2,1)} %collective-permute-done), kind=kOutput, calls=%fused_computation.44 | convolution fusion | flops 452984832 | bytes 4620288 | tf_op jit(solution)/shard_map/dot_general | solution.py:284
  96.0 13.4 %all-gather = bf16[1152,256]{1,0:T(8,128)(2,1)S(1)} all-gather(bf16[288,256]{1,0:T(8,128)(2,1)S(1)} %pad_maximum_fusion.2), channel_id=2, replica_groups=mesh['z'=8,'x'=4,'core'=2,'exp'=4] {'x'}, dimensions={0}, use_global_device_ids=true | all-gather | bytes 737280 | tf_op jit(solution)/shard_map/all_gather | solution.py:289
  110.9 1.0 broadcast_in_dim.7
  114.8 9.1 %all-to-all-start.2 = ((bf16[64,48,128]{2,1,0:T(8,128)(2,1)}), bf16[64,48,128]{2,1,0:T(8,128)(2,1)S(1)}, u32[]{:S(2)}, u32[]{:S(2)}) async-start(bf16[64,48,128]{2,1,0:T(8,128)(2,1)} %bitcast.20), calls=%async_computation.2 | async-start | bytes 1572864 | tf_op jit(solution)/shard_map/all_to_all | solution.py:304
  130.5 2.6 %mix_part.1 = (f32[256,1024]{1,0:T(8,128)}, f32[1,256]{1,0:T(1,128)}) custom-call(f32[8]{0:T(128)} %rate.5, f32[256,1024]{1,0:T(8,128)} %intra_part.1.intra, bf16[256,1024]{1,0:T(8,128)(2,1)} %q.3, bf16[1024,128]{1,0:T(8,128)(2,1)} %bitcast.21.prefix), custom_call_target="tpu_custom_call" | custom-call | tf_op jit(solution)/shard_map/mix_part/pallas_call | solution.py:119
  133.1 11.3 %psum.7.refs_0_ = f32[1,256]{1,0:T(1,128)} all-reduce(f32[1,256]{1,0:T(1,128)} %get-tuple-element.33), channel_id=1, replica_groups=mesh['z'=8,'x'=4,'core'=2,'exp'=4] {'exp'}, use_global_device_ids=true, to_apply=%region_0.0 | all-reduce | flops 256 | bytes 2048 | tf_op jit(solution)/shard_map/psum | solution.py:306
  144.3 2.3 %norm_part.1 = bf16[256,1024]{1,0:T(8,128)(2,1)} custom-call(f32[1,256]{1,0:T(1,128)} %psum.7.refs_0_, f32[256,1024]{1,0:T(8,128)} %get-tuple-element.34.refs_1_, f32[1,1024]{1,0:T(1,128)} %bitcast.80, bf16[256,1024]{1,0:T(8,128)(2,1)} %refs_3_.1), custom_call_target="tpu_custom_call" | custom-call | tf_op jit(solution)/shard_map/norm_part/pallas_call | solution.py:154
  (52 shorter events, 14.2 us)
Async XLA Ops:
  0.6 16.2 %collective-permute-start.1 = (bf16[144,3072]{1,0:T(8,128)(2,1)}, bf16[144,3072]{1,0:T(8,128)(2,1)S(1)}, u32[]{:S(2)}, u32[]{:S(2)}) collective-permute-start(bf16[144,3072]{1,0:T(8,128)(2,1)} %bitcast.73), channel_id=1, source_target_pairs={{0,4},{4,0},{1,5},{5,1},{2,6},{6,2},{3,7},{7,3},{8,12},{12,8},{9,1... | collective-permute-start | bytes 2654216 | tf_op jit(solution)/shard_map/ppermute | solution.py:219
  0.7 16.1 %collective-permute-start.2 = (bf16[144,3072]{1,0:T(8,128)(2,1)}, bf16[144,3072]{1,0:T(8,128)(2,1)S(1)}, u32[]{:S(2)}, u32[]{:S(2)}) collective-permute-start(bf16[144,3072]{1,0:T(8,128)(2,1)} %bitcast.71), channel_id=1, source_target_pairs={{0,4},{4,0},{1,5},{5,1},{2,6},{6,2},{3,7},{7,3},{8,12},{12,8},{9,1... | collective-permute-start | bytes 2654216 | tf_op jit(solution)/shard_map/ppermute | solution.py:219
  3.2 28.6 %copy-start.3 = (bf16[1,144,3072]{2,1,0:T(8,128)(2,1)S(1)}, bf16[1,144,3072]{2,1,0:T(8,128)(2,1)}, u32[]{:S(2)}) copy-start(bf16[1,144,3072]{2,1,0:T(8,128)(2,1)} %param.23) | copy-start | bytes 2654212
  7.0 54.2 %collective-permute-start.8 = (bf16[128,3072]{1,0:T(8,128)(2,1)}, bf16[128,3072]{1,0:T(8,128)(2,1)}, u32[]{:S(2)}, u32[]{:S(2)}) collective-permute-start(bf16[128,3072]{1,0:T(8,128)(2,1)} %get-tuple-element.28), channel_id=1, source_target_pairs={{0,2},{1,3},{2,0},{3,1},{4,6},{5,7},{6,4},{7,5},{8,10},{9,11},{10,... | collective-permute-start | bytes 2359304 | tf_op jit(solution)/shard_map/ppermute | solution.py:219
  10.2 36.2 %collective-permute-start.7 = (bf16[128,3072]{1,0:T(8,128)(2,1)}, bf16[128,3072]{1,0:T(8,128)(2,1)}, u32[]{:S(2)}, u32[]{:S(2)}) collective-permute-start(bf16[128,3072]{1,0:T(8,128)(2,1)} %get-tuple-element.27), channel_id=1, source_target_pairs={{0,3},{1,0},{2,1},{3,2},{4,7},{5,4},{6,5},{7,6},{8,11},{9,8},{10,9... | collective-permute-start | bytes 2359304 | tf_op jit(solution)/shard_map/ppermute | solution.py:219
  11.3 82.3 %collective-permute-start = (bf16[128,3072]{1,0:T(8,128)(2,1)}, bf16[128,3072]{1,0:T(8,128)(2,1)}, u32[]{:S(2)}, u32[]{:S(2)}) collective-permute-start(bf16[128,3072]{1,0:T(8,128)(2,1)} %get-tuple-element.19), channel_id=1, source_target_pairs={{0,1},{1,2},{2,3},{3,0},{4,5},{5,6},{6,7},{7,4},{8,9},{9,10},{10,1... | collective-permute-start | bytes 2359304 | tf_op jit(solution)/shard_map/ppermute | solution.py:219
  16.8 15.0 %copy-start.1 = (bf16[144,3072]{1,0:T(8,128)(2,1)}, bf16[144,3072]{1,0:T(8,128)(2,1)S(1)}, u32[]{:S(2)}) copy-start(bf16[144,3072]{1,0:T(8,128)(2,1)S(1)} %collective-permute-done.1) | copy-start | bytes 2654212
  16.8 2.8 %copy-start.2 = (bf16[144,3072]{1,0:T(8,128)(2,1)}, bf16[144,3072]{1,0:T(8,128)(2,1)S(1)}, u32[]{:S(2)}) copy-start(bf16[144,3072]{1,0:T(8,128)(2,1)S(1)} %collective-permute-done.2) | copy-start | bytes 2654212
  19.6 39.1 %all-to-all-start = ((bf16[64,16,128]{2,1,0:T(8,128)(2,1)}), bf16[64,16,128]{2,1,0:T(8,128)(2,1)}, u32[]{:S(2)}, u32[]{:S(2)}) async-start(bf16[64,16,128]{2,1,0:T(8,128)(2,1)} %bitcast.70), calls=%async_computation | async-start | bytes 524288 | tf_op jit(solution)/shard_map/all_to_all | solution.py:258
  35.8 14.4 %collective-permute-start.3 = (bf16[1,144,768]{2,1,0:T(8,128)(2,1)S(1)}, bf16[1,144,768]{2,1,0:T(8,128)(2,1)S(1)}, u32[]{:S(2)}, u32[]{:S(2)}) collective-permute-start(bf16[1,144,768]{2,1,0:T(8,128)(2,1)S(1)} %get-tuple-element.38), channel_id=1, source_target_pairs={{0,8},{8,16},{16,24},{24,0},{1,9},{9,17},{17,25},{25,1},{2,10},{10... | collective-permute-start | bytes 663560 | tf_op jit(solution)/shard_map/ppermute | solution.py:219
  36.3 4.6 %copy-start.4 = (bf16[128,3072]{1,0:T(8,128)(2,1)S(1)}, bf16[128,3072]{1,0:T(8,128)(2,1)}, u32[]{:S(2)}) copy-start(bf16[128,3072]{1,0:T(8,128)(2,1)} %get-tuple-element.25) | copy-start | bytes 2359300
  36.3 14.6 %collective-permute-start.4 = (bf16[1,144,768]{2,1,0:T(8,128)(2,1)S(1)}, bf16[1,144,768]{2,1,0:T(8,128)(2,1)S(1)}, u32[]{:S(2)}, u32[]{:S(2)}) collective-permute-start(bf16[1,144,768]{2,1,0:T(8,128)(2,1)S(1)} %get-tuple-element.37), channel_id=1, source_target_pairs={{0,16},{8,24},{16,0},{24,8},{1,17},{9,25},{17,1},{25,9},{2,18},{10... | collective-permute-start | bytes 663560 | tf_op jit(solution)/shard_map/ppermute | solution.py:219
  49.4 8.6 %collective-permute-start.5 = (bf16[1,144,768]{2,1,0:T(8,128)(2,1)S(1)}, bf16[1,144,768]{2,1,0:T(8,128)(2,1)S(1)}, u32[]{:S(2)}, u32[]{:S(2)}) collective-permute-start(bf16[1,144,768]{2,1,0:T(8,128)(2,1)S(1)} %get-tuple-element.36), channel_id=1, source_target_pairs={{0,24},{8,0},{16,8},{24,16},{1,25},{9,1},{17,9},{25,17},{2,26},{10... | collective-permute-start | bytes 663560 | tf_op jit(solution)/shard_map/ppermute | solution.py:219
  58.7 33.3 %collective-permute-start.6 = (bf16[4,144,768]{2,1,0:T(8,128)(2,1)}, bf16[4,144,768]{2,1,0:T(8,128)(2,1)}, u32[]{:S(2)}, u32[]{:S(2)}) collective-permute-start(bf16[4,144,768]{2,1,0:T(8,128)(2,1)} %constant_dynamic-update-slice_fusion), channel_id=1, source_target_pairs={{0,4},{4,0},{1,5},{5,1},{2,6},{6,2},{3,7},{7,3},{8,12},{12,8},{9,1... | collective-permute-start | bytes 2654216 | tf_op jit(solution)/shard_map/ppermute | solution.py:219
  64.1 50.8 %all-to-all-start.1 = ((bf16[64,16,128]{2,1,0:T(8,128)(2,1)}), bf16[64,16,128]{2,1,0:T(8,128)(2,1)}, u32[]{:S(2)}, u32[]{:S(2)}) async-start(bf16[64,16,128]{2,1,0:T(8,128)(2,1)} %scan_states.1), calls=%async_computation.1 | async-start | bytes 524288 | tf_op jit(solution)/shard_map/all_to_all | solution.py:263
  93.6 2.3 %copy-start = (f32[576,128]{1,0:T(8,128)S(1)}, f32[576,128]{1,0:T(8,128)}, u32[]{:S(2)}) copy-start(f32[576,128]{1,0:T(8,128)} %fusion.12) | copy-start | bytes 884740
  110.8 13.1 %copy-start.5 = (s32[4,1]{0,1:T(1,128)S(1)}, s32[4,1]{0,1:T(1,128)}, u32[]{:S(2)}) copy-start(s32[4,1]{0,1:T(1,128)} %param.19) | copy-start | bytes 52
  110.8 19.6 %copy-start.6 = (f32[512]{0:T(512)S(1)}, f32[512]{0:T(512)}, u32[]{:S(2)}) copy-start(f32[512]{0:T(512)} %param.20) | copy-start | bytes 6148
  114.8 32.5 %all-to-all-start.2 = ((bf16[64,48,128]{2,1,0:T(8,128)(2,1)}), bf16[64,48,128]{2,1,0:T(8,128)(2,1)S(1)}, u32[]{:S(2)}, u32[]{:S(2)}) async-start(bf16[64,48,128]{2,1,0:T(8,128)(2,1)} %bitcast.20), calls=%async_computation.2 | async-start | bytes 1572864 | tf_op jit(solution)/shard_map/all_to_all | solution.py:304

commit v4 on v3

--- a/solution.py
+++ b/solution.py
@@ -1,3 +1,5 @@
+import functools
+
 import jax
 import jax.numpy as jnp
 from jax import lax
@@ -12,6 +14,7 @@
 HEAD = 128
 TILE = 128
 GROUP = 4
+LAST = 1
 
 
 def _state_kernel(rate, k, v, out):
@@ -40,18 +43,19 @@
     )(rate, keys, values)
 
 
-def _scan_kernel(decay, states, out):
-    lam = decay[0]
-    blocks = states.shape[0]
-    carry = jnp.zeros(states.shape[1:], F32)
+def _scan_kernel(tokens, heads, rate, states, out):
+    blocks, rows, width = states.shape
+    mine = lax.axis_index(CTX) * heads // blocks
+    lam = jnp.exp(jnp.full((rows, width), -rate[mine] * tokens, F32))
+    carry = jnp.zeros((rows, width), F32)
     for b in range(blocks):
         out[b] = carry.astype(BF)
         carry = carry * lam + states[b].astype(F32)
 
 
-def scan_states(decay, states):
-    return pl.pallas_call(
-        _scan_kernel,
+def scan_states(tokens, rate, states):
+    return pl.pallas_call(
+        functools.partial(_scan_kernel, tokens, rate.shape[0]),
         in_specs=[
             pl.BlockSpec(memory_space=pltpu.SMEM),
             pl.BlockSpec(memory_space=pltpu.VMEM),
@@ -59,7 +63,7 @@
         out_specs=pl.BlockSpec(memory_space=pltpu.VMEM),
         out_shape=jax.ShapeDtypeStruct(states.shape, BF),
         name="scan_states",
-    )(decay, states)
+    )(rate, states)
 
 
 def _intra_kernel(rate, q, k, v, out):
@@ -166,27 +170,33 @@
     )(total, mixed, gain, gates)
 
 
-def _pick_kernel(ids, place, rows, *refs):
-    n_exp = place[2]
+def _pick_kernel(ids, rows, *refs):
     outs, held, into, out_of = refs[:-3], refs[-3], refs[-2], refs[-1]
-    tiles = ids.shape[0]
+    n_exp, me_e, me_core = lax.axis_size("exp"), lax.axis_index("exp"), lax.axis_index("core")
+    tiles, half = ids.shape[0], TILE // 2
     loads = []
     for k in range(len(outs)):
-        target = lax.rem(place[0] + k + 1, n_exp)
-        tile, rank = jnp.int32(0), jnp.int32(0)
+        target = lax.rem(me_e + k + 1, n_exp)
+        seen = jnp.int32(0)
+        tile = [jnp.int32(0), jnp.int32(0)]
         for t in range(tiles):
-            same = ids[t, 0] == target
-            tile = jnp.where(same & (rank == place[1]), t, tile)
-            rank = rank + same.astype(jnp.int32)
-        start = pl.multiple_of(tile * TILE, TILE)
-        load = pltpu.make_async_copy(
-            rows.at[pl.ds(start, TILE), :], held.at[k], into.at[k]
-        )
-        load.start()
-        loads.append(load)
+            same = ids[t] == target
+            for rank in range(2):
+                tile[rank] = jnp.where(same & (seen == rank), t, tile[rank])
+            seen = seen + same.astype(jnp.int32)
+        for rank in range(2):
+            start = pl.multiple_of(tile[rank] * TILE + me_core * half, half)
+            load = pltpu.make_async_copy(
+                rows.at[pl.ds(start, half), :],
+                held.at[k, pl.ds(rank * half, half), :],
+                into.at[k, rank],
+            )
+            load.start()
+            loads.append(load)
     stores = []
-    for k, load in enumerate(loads):
-        load.wait()
+    for k in range(len(outs)):
+        loads[2 * k].wait()
+        loads[2 * k + 1].wait()
         store = pltpu.make_async_copy(held.at[k], outs[k], out_of.at[k])
         store.start()
         stores.append(store)
@@ -194,12 +204,11 @@
         store.wait()
 
 
-def pick_tiles(ids, place, rows, count):
+def pick_tiles(ids, rows, count):
     tile = jax.ShapeDtypeStruct((TILE, rows.shape[1]), rows.dtype)
     return pl.pallas_call(
         _pick_kernel,
         in_specs=[
-            pl.BlockSpec(memory_space=pltpu.SMEM),
             pl.BlockSpec(memory_space=pltpu.SMEM),
             pl.BlockSpec(memory_space=pl.ANY),
         ],
@@ -207,11 +216,117 @@
         out_shape=[tile] * count,
         scratch_shapes=[
             pltpu.VMEM((count, TILE, rows.shape[1]), rows.dtype),
+            pltpu.SemaphoreType.DMA((count, 2)),
             pltpu.SemaphoreType.DMA((count,)),
-            pltpu.SemaphoreType.DMA((count,)),
         ],
         name="pick_tiles",
-    )(ids, place, rows)
+    )(ids, rows)
+
+
+def _hidden_kernel(count, *refs):
+    rows, weights = refs[:count], refs[count : count + 4]
+    held, out = refs[-1], refs[-2]
+    gate_own, gate_other, up_own, up_other = weights
+    units = gate_own.shape[0]
+    for i in range(count):
+        held[i * TILE : (i + 1) * TILE, :] = rows[i][...]
+    x = held[...]
+    for i, (gate, up) in enumerate(((gate_own, up_own), (gate_other, up_other))):
+        dims = (((1,), (1,)), ((), ()))
+        g = lax.dot_general(gate[...], x, dims, preferred_element_type=F32)
+        u = lax.dot_general(up[...], x, dims, preferred_element_type=F32)
+        out[i * units : (i + 1) * units, :] = (jax.nn.silu(g) * u).astype(BF)
+
+
+def hidden_part(rows, weights):
+    count, units, model = len(rows), weights[0].shape[0], weights[0].shape[1]
+    vmem = pl.BlockSpec(memory_space=pltpu.VMEM)
+    return pl.pallas_call(
+        functools.partial(_hidden_kernel, count),
+        in_specs=[vmem] * (count + 4),
+        out_specs=vmem,
+        out_shape=jax.ShapeDtypeStruct((2 * units, count * TILE), BF),
+        scratch_shapes=[pltpu.VMEM((count * TILE, model), BF)],
+        compiler_params=pltpu.CompilerParams(vmem_limit_bytes=40 << 20),
+        name="hidden_part",
+    )(*rows, *weights)
+
+
+def _down_kernel(groups, own, other, hidden, out):
+    n_exp, me_e = lax.axis_size("exp"), lax.axis_index("exp")
+    n_x = len(own)
+    units = own[0].shape[0]
+    blocks, columns = out.shape[0], out.shape[2]
+    for slots, held in zip(groups, hidden):
+        total = None
+        for k in range(n_x):
+            for i, part in enumerate((own[k], other[k])):
+                h = held[k][i * units : (i + 1) * units, :]
+                term = lax.dot_general(
+                    part[...], h, (((0,), (0,)), ((), ())), preferred_element_type=F32
+                )
+                total = term if total is None else total + term
+        total = total.astype(BF)
+        for i, slot in enumerate(slots):
+            home = lax.rem(me_e + n_exp - slot, n_exp)
+            block = total[:, i * TILE : (i + 1) * TILE]
+            out[:, home] = block.reshape(blocks, columns, TILE)
+
+
+def down_part(groups, own, other, hidden, blocks, columns):
+    n_x = len(own)
+    n_slots = sum(len(slots) for slots in groups)
+    vmem = pl.BlockSpec(memory_space=pltpu.VMEM)
+
+    def kernel(*refs):
+        held = [
+            refs[n_x * (2 + g) : n_x * (3 + g)] for g in range(len(groups))
+        ]
+        _down_kernel(groups, refs[:n_x], refs[n_x : 2 * n_x], held, refs[-1])
+
+    flat = [piece for held in hidden for piece in held]
+    return pl.pallas_call(
+        kernel,
+        in_specs=[vmem] * (2 * n_x + len(flat)),
+        out_specs=vmem,
+        out_shape=jax.ShapeDtypeStruct((blocks, n_slots, columns, TILE), BF),
+        compiler_params=pltpu.CompilerParams(vmem_limit_bytes=40 << 20),
+        name="down_part",
+    )(*own, *other, *flat)
+
+
+def _finish_kernel(ids, parts, weight, out):
+    n_z, n_core, n_exp, columns, _ = parts.shape
+    tiles, half = ids.shape[0], TILE // 2
+    low = lax.broadcasted_iota(jnp.int32, (columns, TILE), 1) < half
+    for t in range(tiles):
+        rank = jnp.int32(0)
+        for earlier in range(t):
+            rank = rank + (ids[earlier] == ids[t]).astype(jnp.int32)
+        sums = []
+        for core in range(n_core):
+            total = jnp.zeros((columns, TILE), F32)
+            for z in range(n_z):
+                total = total + parts[z, core, ids[t]].astype(F32)
+            sums.append(total.astype(BF).astype(F32))
+        first, second = sums
+        zero = jnp.where(low, first, pltpu.roll(second, half, 1))
+        one = jnp.where(low, pltpu.roll(first, half, 1), second)
+        rows = jnp.where(rank == 0, zero, one)
+        at = slice(t * TILE, (t + 1) * TILE)
+        out[:, at] = (rows * weight[:, at]).astype(BF)
+
+
+def finish_part(ids, parts, weight):
+    columns = parts.shape[3]
+    vmem = pl.BlockSpec(memory_space=pltpu.VMEM)
+    return pl.pallas_call(
+        _finish_kernel,
+        in_specs=[pl.BlockSpec(memory_space=pltpu.SMEM), vmem, vmem],
+        out_specs=vmem,
+        out_shape=jax.ShapeDtypeStruct((columns, weight.shape[1]), BF),
+        name="finish_part",
+    )(ids, parts, weight)
 
 
 def shift(array, axis, by):
@@ -226,29 +341,21 @@
     n_exp, n_z = lax.axis_size("exp"), lax.axis_size("z")
     n_x, n_core = lax.axis_size("x"), lax.axis_size("core")
     n_ctx = n_z * n_x * n_core
-    me_e, me_core = lax.axis_index("exp"), lax.axis_index("core")
     tokens, width = queries.shape
-    heads = width // HEAD
     model = moe_rows.shape[1]
-    tiles = tile_expert.shape[0]
-
     ids = tile_expert[:, 0]
-    order = jnp.arange(tiles)
-    earlier = (ids[None, :] == ids[:, None]) & (order[None, :] < order[:, None])
-    ranks = jnp.sum(earlier.astype(jnp.int32), axis=1)
-
-    place = jnp.stack([me_e, me_core, n_exp]).astype(jnp.int32)
-    picked = pick_tiles(tile_expert, place, moe_rows, n_exp)
-    arrived = [picked[-1]]
-    arrived += [shift(picked[k - 1], "exp", k) for k in range(1, n_exp)]
+    columns = model // n_ctx
+    chunk = model // n_x
 
     gate_own = jnp.swapaxes(w_gate[0], 0, 1)
     up_own = jnp.swapaxes(w_up[0], 0, 1)
     gate_other = shift(gate_own, "core", 1)
     up_other = shift(up_own, "core", 1)
     units = gate_own.shape[0]
-    chunk = model // n_x
-    columns = model // n_ctx
+
+    picked = pick_tiles(ids, moe_rows, n_exp)
+    arrived = [picked[-1]]
+    arrived += [shift(picked[k - 1], "exp", k) for k in range(1, n_exp)]
     gate_other, up_other, w_down, keys_late = lax.optimization_barrier(
         (gate_other, up_other, w_down, keys)
     )
@@ -256,67 +363,45 @@
     states = local_states(decay_rate, keys_late, values)
     pieces = states.reshape(n_ctx, width // n_ctx, HEAD)
     pieces = lax.all_to_all(pieces, CTX, 0, 0, tiled=True)
-    mine = lax.axis_index(CTX) * (width // n_ctx) // HEAD
-    lam = jnp.exp(-decay_rate * tokens)
-    pieces = scan_states(lax.dynamic_slice(lam, (mine,), (1,)), pieces)
-    arrived[2], pieces = lax.optimization_barrier((arrived[2], pieces))
+    pieces = scan_states(float(tokens), decay_rate, pieces)
+    arrived[LAST], pieces = lax.optimization_barrier((arrived[LAST], pieces))
     prefix = lax.all_to_all(pieces, CTX, 0, 0, tiled=True).reshape(width, HEAD)
     intra = intra_part(decay_rate, queries, keys, values)
+
     split = w_down[0].reshape(units, n_z, n_x, n_core * columns)
     split = jnp.transpose(split, (2, 0, 1, 3)).reshape(n_x, units, chunk)
     me_x = lax.axis_index("x")
-    down_own = jnp.zeros((n_x, units, chunk), BF)
+    down_own, down_other = [], []
     for k in range(n_x):
-        part = lax.dynamic_index_in_dim(split, lax.rem(me_x + k, n_x), 0)
+        part = lax.dynamic_index_in_dim(
+            split, lax.rem(me_x + k, n_x), 0, keepdims=False
+        )
         part = shift(part, "x", k) if k else part
-        source = lax.rem(me_x + n_x - k, n_x)
-        down_own = lax.dynamic_update_slice(down_own, part, (source, 0, 0))
-    down_other = shift(down_own, "core", 1)
-    down = jnp.stack([down_own, down_other], axis=1)
-
-    inner = jnp.concatenate([gate_own, gate_other, up_own, up_other], axis=0)
-    arrived[1], down, intra = lax.optimization_barrier((arrived[1], down, intra))
-    down = down.reshape(n_x * 2 * units, chunk)
-    parts = jnp.zeros((n_z * n_core, n_exp, columns, TILE), BF)
-    for pair in ((0, 1), (3, 2)):
-        hidden = []
-        for k in pair:
-            both = lax.dot_general(
-                inner, arrived[k], (((1,), (1,)), ((), ())), preferred_element_type=F32
-            )
-            half = jax.nn.silu(both[: 2 * units]) * both[2 * units :]
-            hidden.append(half.astype(BF))
-        hidden = lax.all_gather(jnp.concatenate(hidden, axis=1), "x")
-        partial = lax.dot_general(
-            down,
-            hidden.reshape(n_x * 2 * units, len(pair) * TILE),
-            (((0,), (0,)), ((), ())),
-            preferred_element_type=F32,
-        ).astype(BF)
-        partial = partial.reshape(n_z * n_core, 1, columns, len(pair) * TILE)
-        for i, k in enumerate(pair):
-            source = lax.rem(me_e + n_exp - k, n_exp)
-            parts = lax.dynamic_update_slice(
-                parts, partial[..., i * TILE : (i + 1) * TILE], (0, source, 0, 0)
-            )
+        down_own.append(part)
+        down_other.append(shift(part, "core", 1))
+    arrived[LAST], intra, *down_other = lax.optimization_barrier(
+        (arrived[LAST], intra, *down_other)
+    )
+
+    weights = (gate_own, gate_other, up_own, up_other)
+    early = [k for k in range(n_exp) if k != LAST]
+    groups = [early, [LAST]]
+    hidden = []
+    for slots in groups:
+        mine = hidden_part([arrived[k] for k in slots], weights)
+        hidden.append([mine] + [shift(mine, "x", k) for k in range(1, n_x)])
+    hidden[-1][0], prefix = lax.optimization_barrier((hidden[-1][0], prefix))
+    parts = down_part(groups, down_own, down_other, hidden, n_z * n_core, columns)
     parts = parts.reshape(-1, columns, TILE)
-    parts, prefix = lax.optimization_barrier((parts, prefix))
     parts = lax.all_to_all(parts, ("z", "core", "exp"), 0, 0, tiled=True)
+    parts = parts.reshape(n_z, n_core, n_exp, columns, TILE)
+
     mixed, squares = mix_part(decay_rate, intra, queries, prefix)
     total = lax.psum(squares, "exp")
     attention_out = norm_part(
         float(width * n_exp), total, mixed, norm_gain[None, :], gates
     )
-    parts = parts.reshape(n_z, n_core * n_exp, columns, TILE)
-    summed = jnp.sum(parts.astype(F32), axis=0).astype(BF)
-    summed = lax.optimization_barrier(summed)
-    picked = []
-    for t in range(tiles):
-        slot = ranks[t] * n_exp + ids[t]
-        tile = lax.dynamic_index_in_dim(summed, slot, 0, keepdims=False)
-        weight = row_weight[t * TILE : (t + 1) * TILE]
-        picked.append((tile.astype(F32) * weight[None, :]).astype(BF))
-    moe_out = jnp.swapaxes(jnp.concatenate(picked, axis=1), 0, 1)
+    moe_out = jnp.swapaxes(finish_part(ids, parts, row_weight[None, :]), 0, 1)
     return attention_out, moe_out
 
 

time: 150 us -> 129 us (0.86)
  blocking collectives: 38.6 us -> 11.2 us
  Pallas kernels: 17.1 us -> 31.7 us
  starting transfers between devices: 42.9 us -> 56.1 us
  matrix products: 10.6 us -> 0 us
  other arithmetic: 8.8 us -> 0 us
  between operations: 5.93 us -> 0.77 us
  waiting for transfers between devices: 10.8 us -> 13.6 us
    all_gather x2 -> x0, blocking collectives: 27.4 us -> none  [on_device(): hidden = lax.all_gather(jnp.concatenate(hidden, axis=1), 'x')]
    pallas_call x1 -> x5, Pallas kernels: 2.44 us -> 16.7 us  [the longest x2 7.75 us: hidden_part(): pl.pallas_call(functools.partial(_hidden_kernel, count), in_specs=[vmem]...]
    dot_general x6 -> x0, matrix products: 10.6 us -> none  [the longest x4 9.18 us: on_device(): lax.dot_general(inner, arrived[k], (((1,), (1,)), ((), ())), preferred_el...]
    ppermute x9 -> x18, starting transfers between devices: 9.66 us -> 18.9 us  [shift(): return lax.ppermute(array, axis, [(i, (i + by) % n) for i in range(n)])]
    all_to_all x1, waiting for transfers between devices: 0.7 us -> 7.35 us  [on_device(): parts = lax.all_to_all(parts, ('z', 'core', 'exp'), 0, 0, tiled=True)]
    all_to_all x1, starting transfers between devices: 9.08 us -> 14.8 us  [on_device(): parts = lax.all_to_all(parts, ('z', 'core', 'exp'), 0, 0, tiled=True)]
    dynamic_update_slice x7 -> x0, local copies, waits for them, and re-layouts: 5.05 us -> none  [the longest x4 2.93 us: on_device(): lax.dynamic_update_slice(parts, partial[..., i * TILE:(i + 1) * TILE], (0...]
    ppermute x9 -> x18, waiting for transfers between devices: 10.1 us -> 5.17 us  [shift(): return lax.ppermute(array, axis, [(i, (i + by) % n) for i in range(n)])]
  transfers between devices with their start and end apart: 12 -> 21, of which waited for: 3 -> 5; matrix products, arithmetic and copies ran while one was open for 22% -> 6% of each run, Pallas kernels for 12% -> 19%
where the time goes in v4:
time: 129 us; the launch traced here: 127 us
  starting transfers between devices  56.1 us (43%)
  Pallas kernels  31.7 us (25%)
  local copies, waits for them, and re-layouts  14.1 us (11%)
  waiting for transfers between devices  13.6 us (11%)
  blocking collectives  11.2 us (9%)
    ppermute x18, starting transfers between devices, shift(): return lax.ppermute(array, axis, [(i, (i + by) % n) for i in range(n)])  18.9 us
    all_to_all x1, starting transfers between devices, on_device(): parts = lax.all_to_all(parts, ('z', 'core', 'exp'), 0, 0, tiled=True)  14.8 us
    all_to_all x1, starting transfers between devices, on_device(): pieces = lax.all_to_all(pieces, CTX, 0, 0, tiled=True)  12.2 us
    psum x1, blocking collectives, on_device(): total = lax.psum(squares, 'exp')  11.2 us
    all_to_all x1, starting transfers between devices, on_device(): prefix = lax.all_to_all(pieces, CTX, 0, 0, tiled=True).reshape(width, HEAD)  10.2 us
    pallas_call x2, Pallas kernels, hidden_part(): pl.pallas_call(functools.partial(_hidden_kernel, count), in_specs=[vmem]...  7.75 us
    all_to_all x1, waiting for transfers between devices, on_device(): parts = lax.all_to_all(parts, ('z', 'core', 'exp'), 0, 0, tiled=True)  7.35 us
    unnamed x20, local copies, waits for them, and re-layouts  6.23 us
  transfers between devices with their start and end apart: 21, of which 5 were waited for; matrix products, arithmetic and copies ran while one was open for 6% of the time, Pallas kernels for 19%

profile of v4, /device:TPU:6, one launch (start us, length us, event | category | flops | bytes accessed | tf_op | source)
XLA Modules:
  0.0 127.4 jit_solution(2373096970598622136)
XLA Ops:
  1.2 4.4 %pick_tiles.1 = (bf16[128,3072]{1,0:T(8,128)(2,1)}, bf16[128,3072]{1,0:T(8,128)(2,1)}, bf16[128,3072]{1,0:T(8,128)(2,1)}, bf16[128,3072]{1,0:T(8,128)(2,1)}) custom-call(s32[4]{0:T(128)} %bitcast.37, bf16[512,3072]{1,0:T(8,128)(2,1)} %rows.1), custom_call_target="tpu_custom_call" | custom-call | tf_op jit(solution)/shard_map/pick_tiles/pallas_call | solution.py:209
  5.7 1.7 %collective-permute-start = (bf16[128,3072]{1,0:T(8,128)(2,1)}, bf16[128,3072]{1,0:T(8,128)(2,1)}, u32[]{:S(2)}, u32[]{:S(2)}) collective-permute-start(bf16[128,3072]{1,0:T(8,128)(2,1)} %get-tuple-element.22), channel_id=1, source_target_pairs={{0,1},{1,2},{2,3},{3,0},{4,5},{5,6},{6,7},{7,4},{8,9},{9,10},{10,1... | collective-permute-start | bytes 2359304 | tf_op jit(solution)/shard_map/ppermute | solution.py:334
  7.3 2.9 %collective-permute-start.10 = (bf16[128,3072]{1,0:T(8,128)(2,1)}, bf16[128,3072]{1,0:T(8,128)(2,1)}, u32[]{:S(2)}, u32[]{:S(2)}) collective-permute-start(bf16[128,3072]{1,0:T(8,128)(2,1)} %get-tuple-element.39), channel_id=1, source_target_pairs={{0,2},{1,3},{2,0},{3,1},{4,6},{5,7},{6,4},{7,5},{8,10},{9,11},{10,... | collective-permute-start | bytes 2359304 | tf_op jit(solution)/shard_map/ppermute | solution.py:334
  10.2 1.3 %collective-permute-start.11 = (bf16[128,3072]{1,0:T(8,128)(2,1)}, bf16[128,3072]{1,0:T(8,128)(2,1)}, u32[]{:S(2)}, u32[]{:S(2)}) collective-permute-start(bf16[128,3072]{1,0:T(8,128)(2,1)} %get-tuple-element.40), channel_id=1, source_target_pairs={{0,3},{1,0},{2,1},{3,2},{4,7},{5,4},{6,5},{7,6},{8,11},{9,8},{10,9... | collective-permute-start | bytes 2359304 | tf_op jit(solution)/shard_map/ppermute | solution.py:334
  11.6 2.4 %local_states.1 = bf16[1024,128]{1,0:T(8,128)(2,1)} custom-call(f32[8]{0:T(128)} %rate.7, bf16[256,1024]{1,0:T(8,128)(2,1)} %k.2, bf16[256,1024]{1,0:T(8,128)(2,1)} %v.3), custom_call_target="tpu_custom_call" | custom-call | tf_op jit(solution)/shard_map/local_states/pallas_call | solution.py:36
  14.0 12.2 %all-to-all-start = ((bf16[64,16,128]{2,1,0:T(8,128)(2,1)}), bf16[64,16,128]{2,1,0:T(8,128)(2,1)}, u32[]{:S(2)}, u32[]{:S(2)}) async-start(bf16[64,16,128]{2,1,0:T(8,128)(2,1)} %bitcast.33), calls=%async_computation | async-start | bytes 524288 | tf_op jit(solution)/shard_map/all_to_all | solution.py:365
  26.2 2.2 %reshape_squeeze.3 = bf16[144,8,4,96]{3,2,1,0:T(4,128)(2,1)} reshape(bf16[1,144,3072]{2,1,0:T(8,128)(2,1)S(1)} %copy-done.9) | data formatting | bytes 1769472 | tf_op jit(solution)/shard_map/reshape;squeeze | solution.py:371
  28.3 1.4 %copy.14 = bf16[4,144,8,96]{3,2,1,0:T(8,128)(2,1)S(1)} copy(bf16[4,144,8,96]{3,0,2,1:T(4,128)(2,1)} %bitcast.31) | data formatting | bytes 1769472 | tf_op jit(solution)/shard_map/transpose | solution.py:372
  29.8 1.9 %reshape.20 = bf16[4,144,768]{2,1,0:T(8,128)(2,1)} reshape(bf16[4,144,8,96]{3,2,1,0:T(8,128)(2,1)S(1)} %copy.14) | data formatting | bytes 1769472 | tf_op jit(solution)/shard_map/reshape | solution.py:372
  31.7 2.4 %dynamic-slice_bitcast_fusion = (bf16[144,768]{1,0:T(8,128)(2,1)}, bf16[144,768]{1,0:T(8,128)(2,1)}, bf16[144,768]{1,0:T(8,128)(2,1)}, bf16[144,768]{1,0:T(8,128)(2,1)}) fusion(bf16[4,144,768]{2,1,0:T(8,128)(2,1)} %reshape.20, s32[]{:T(128)S(6)} %select_n.16, s32[]{:T(128)S(6)} %select_n.15, s32[]{:T(128)S(6)} %select_n.14, s32[]{:T(128)S(6)} %select_n.13), kind=kLoop, calls=%fused_computation | loop fusion | bytes 1769488 | tf_op jit(solution)/shard_map/jit(dynamic_index_in_dim)/squeeze | solution.py:376
  34.6 2.4 %collective-permute-start.6 = (bf16[144,768]{1,0:T(8,128)(2,1)}, bf16[144,768]{1,0:T(8,128)(2,1)}, u32[]{:S(2)}, u32[]{:S(2)}) collective-permute-start(bf16[144,768]{1,0:T(8,128)(2,1)} %get-tuple-element.43), channel_id=1, source_target_pairs={{0,16},{8,24},{16,0},{24,8},{1,17},{9,25},{17,1},{25,9},{2,18},{10... | collective-permute-start | bytes 663560 | tf_op jit(solution)/shard_map/ppermute | solution.py:334
  37.0 1.0 all-to-all-done.states
  38.0 1.8 %scan_states.1 = bf16[64,16,128]{2,1,0:T(8,128)(2,1)} custom-call(f32[8]{0:T(128)} %rate.7, bf16[64,16,128]{2,1,0:T(8,128)(2,1)} %all-to-all-done.states), custom_call_target="tpu_custom_call" | custom-call | tf_op jit(solution)/shard_map/scan_states/pallas_call | solution.py:57
  40.7 10.2 %all-to-all-start.1 = ((bf16[64,16,128]{2,1,0:T(8,128)(2,1)}), bf16[64,16,128]{2,1,0:T(8,128)(2,1)}, u32[]{:S(2)}, u32[]{:S(2)}) async-start(bf16[64,16,128]{2,1,0:T(8,128)(2,1)} %scan_states.1), calls=%async_computation.1 | async-start | bytes 524288 | tf_op jit(solution)/shard_map/all_to_all | solution.py:368
  52.0 1.1 copy-done.3
  53.2 4.9 %hidden_part.3.refs_8_ = bf16[288,384]{1,0:T(8,128)(2,1)} custom-call(bf16[128,3072]{1,0:T(8,128)(2,1)S(1)} %copy-done.3, bf16[128,3072]{1,0:T(8,128)(2,1)} %collective-permute-done.10.refs_1_, bf16[128,3072]{1,0:T(8,128)(2,1)} %collective-permute-done.11.refs_2_, bf16[144,3072]{1,0:T(8,128)(2,1)S(1)} %bitcast.26, ...), custom_call_target="tpu_custom_call" | custom-call | tf_op jit(solution)/shard_map/hidden_part/pallas_call | solution.py:244
  59.3 2.3 %collective-permute-start.13 = (bf16[288,384]{1,0:T(8,128)(2,1)}, bf16[288,384]{1,0:T(8,128)(2,1)}, u32[]{:S(2)}, u32[]{:S(2)}) collective-permute-start(bf16[288,384]{1,0:T(8,128)(2,1)} %hidden_part.3.refs_8_), channel_id=1, source_target_pairs={{0,16},{8,24},{16,0},{24,8},{1,17},{9,25},{17,1},{25,9},{2,18},{10... | collective-permute-start | bytes 663560 | tf_op jit(solution)/shard_map/ppermute | solution.py:334
  62.5 3.3 %intra_part.1.intra = f32[256,1024]{1,0:T(8,128)} custom-call(f32[8]{0:T(128)} %rate.7, bf16[256,1024]{1,0:T(8,128)(2,1)} %q.3, bf16[256,1024]{1,0:T(8,128)(2,1)} %k.2, bf16[256,1024]{1,0:T(8,128)(2,1)} %v.3), custom_call_target="tpu_custom_call" | custom-call | tf_op jit(solution)/shard_map/intra_part/pallas_call | solution.py:90
  65.8 2.9 %hidden_part.2.refs_12_ = bf16[288,128]{1,0:T(8,128)(2,1)} custom-call(bf16[128,3072]{1,0:T(8,128)(2,1)} %collective-permute-done.refs_0_, bf16[144,3072]{1,0:T(8,128)(2,1)S(1)} %bitcast.27, bf16[144,3072]{1,0:T(8,128)(2,1)S(1)} %collective-permute-done.1.refs_2_.refs_4_, bf16[144,3072]{1,0:T(8,128)(2,1)S(1)} %bitcast.30, ...), custom_call_target="tpu_custom_call" | custom-call | tf_op jit(solution)/shard_map/hidden_part/pallas_call | solution.py:244
  68.7 3.1 %collective-permute-start.15 = (bf16[288,128]{1,0:T(8,128)(2,1)}, bf16[288,128]{1,0:T(8,128)(2,1)S(1)}, u32[]{:S(2)}, u32[]{:S(2)}) collective-permute-start(bf16[288,128]{1,0:T(8,128)(2,1)} %hidden_part.2.refs_12_), channel_id=1, source_target_pairs={{0,8},{8,16},{16,24},{24,0},{1,9},{9,17},{17,25},{25,1},{2,10},{10... | collective-permute-start | bytes 221192 | tf_op jit(solution)/shard_map/ppermute | solution.py:334
  71.8 1.4 %collective-permute-start.17 = (bf16[288,128]{1,0:T(8,128)(2,1)}, bf16[288,128]{1,0:T(8,128)(2,1)S(1)}, u32[]{:S(2)}, u32[]{:S(2)}) collective-permute-start(bf16[288,128]{1,0:T(8,128)(2,1)} %hidden_part.2.refs_12_), channel_id=1, source_target_pairs={{0,24},{8,0},{16,8},{24,16},{1,25},{9,1},{17,9},{25,17},{2,26},{10... | collective-permute-start | bytes 221192 | tf_op jit(solution)/shard_map/ppermute | solution.py:334
  74.1 3.8 %collective-permute-done.16.refs_14_ = bf16[288,128]{1,0:T(8,128)(2,1)S(1)} collective-permute-done((bf16[288,128]{1,0:T(8,128)(2,1)}, bf16[288,128]{1,0:T(8,128)(2,1)S(1)}, u32[]{:S(2)}, u32[]{:S(2)}) %collective-permute-start.16) | collective-permute-done | bytes 73760 | tf_op jit(solution)/shard_map/ppermute | solution.py:334
  78.4 0.9 copy-done.2
  79.3 0.9 copy-done.5
  80.2 0.9 copy-done.7
  81.2 5.2 %down_part.1 = bf16[16,4,48,128]{3,2,1,0:T(8,128)(2,1)} custom-call(bf16[144,768]{1,0:T(8,128)(2,1)S(1)} %copy-done.2, bf16[144,768]{1,0:T(8,128)(2,1)} %collective-permute-done.4.refs_1_, bf16[144,768]{1,0:T(8,128)(2,1)} %collective-permute-done.6.refs_2_, bf16[144,768]{1,0:T(8,128)(2,1)} %collective-permute-done.8.refs_3_, bf16[144,768]{1,0:T(8,128)(2,1)S(1)} %copy-done.5, ...), custom_call_target="tpu_custom_call" | custom-call | tf_op jit(solution)/shard_map/down_part/pallas_call | solution.py:288
  86.4 14.8 %all-to-all-start.2 = ((bf16[64,48,128]{2,1,0:T(8,128)(2,1)}), bf16[64,48,128]{2,1,0:T(8,128)(2,1)S(1)}, u32[]{:S(2)}, u32[]{:S(2)}) async-start(bf16[64,48,128]{2,1,0:T(8,128)(2,1)} %bitcast.15), calls=%async_computation.2 | async-start | bytes 1572864 | tf_op jit(solution)/shard_map/all_to_all | solution.py:396
  101.2 2.6 %mix_part.1 = (f32[256,1024]{1,0:T(8,128)}, f32[1,256]{1,0:T(1,128)}) custom-call(f32[8]{0:T(128)} %rate.7, f32[256,1024]{1,0:T(8,128)} %intra_part.1.intra, bf16[256,1024]{1,0:T(8,128)(2,1)} %q.3, bf16[1024,128]{1,0:T(8,128)(2,1)} %bitcast.13.prefix), custom_call_target="tpu_custom_call" | custom-call | tf_op jit(solution)/shard_map/mix_part/pallas_call | solution.py:123
  103.8 11.2 %psum.7.refs_0_ = f32[1,256]{1,0:T(1,128)} all-reduce(f32[1,256]{1,0:T(1,128)} %get-tuple-element.32), channel_id=1, replica_groups=mesh['z'=8,'x'=4,'core'=2,'exp'=4] {'exp'}, use_global_device_ids=true, to_apply=%region_0.1 | all-reduce | flops 256 | bytes 2048 | tf_op jit(solution)/shard_map/psum | solution.py:400
  115.0 2.3 %norm_part.1 = bf16[256,1024]{1,0:T(8,128)(2,1)} custom-call(f32[1,256]{1,0:T(1,128)} %psum.7.refs_0_, f32[256,1024]{1,0:T(8,128)} %get-tuple-element.33.refs_1_, f32[1,1024]{1,0:T(1,128)} %bitcast.35, bf16[256,1024]{1,0:T(8,128)(2,1)} %refs_3_.1), custom_call_target="tpu_custom_call" | custom-call | tf_op jit(solution)/shard_map/norm_part/pallas_call | solution.py:158
  117.2 7.4 %all-to-all-done.2 = bf16[64,48,128]{2,1,0:T(8,128)(2,1)S(1)} async-done(((bf16[64,48,128]{2,1,0:T(8,128)(2,1)}), bf16[64,48,128]{2,1,0:T(8,128)(2,1)S(1)}, u32[]{:S(2)}, u32[]{:S(2)}) %all-to-all-start.2) | async-done | bytes 786464 | tf_op jit(solution)/shard_map/all_to_all | solution.py:396
  125.5 1.9 %finish_part.1 = bf16[48,512]{1,0:T(8,128)(2,1)} custom-call(s32[4]{0:T(128)} %bitcast.38, bf16[8,2,4,48,128]{4,3,2,1,0:T(8,128)(2,1)} %bitcast.32, f32[1,512]{1,0:T(1,128)} %bitcast.36), custom_call_target="tpu_custom_call" | custom-call | tf_op jit(solution)/shard_map/finish_part/pallas_call | solution.py:323
  (45 shorter events, 7.5 us)
Async XLA Ops:
  0.6 11.0 %collective-permute-start.1 = (bf16[144,3072]{1,0:T(8,128)(2,1)}, bf16[144,3072]{1,0:T(8,128)(2,1)S(1)}, u32[]{:S(2)}, u32[]{:S(2)}) collective-permute-start(bf16[144,3072]{1,0:T(8,128)(2,1)} %bitcast.25), channel_id=1, source_target_pairs={{0,4},{4,0},{1,5},{5,1},{2,6},{6,2},{3,7},{7,3},{8,12},{12,8},{9,1... | collective-permute-start | bytes 2654216 | tf_op jit(solution)/shard_map/ppermute | solution.py:334
  0.7 10.9 %collective-permute-start.2 = (bf16[144,3072]{1,0:T(8,128)(2,1)}, bf16[144,3072]{1,0:T(8,128)(2,1)S(1)}, u32[]{:S(2)}, u32[]{:S(2)}) collective-permute-start(bf16[144,3072]{1,0:T(8,128)(2,1)} %bitcast.28), channel_id=1, source_target_pairs={{0,4},{4,0},{1,5},{5,1},{2,6},{6,2},{3,7},{7,3},{8,12},{12,8},{9,1... | collective-permute-start | bytes 2654216 | tf_op jit(solution)/shard_map/ppermute | solution.py:334
  5.7 20.5 %copy-start.9 = (bf16[1,144,3072]{2,1,0:T(8,128)(2,1)S(1)}, bf16[1,144,3072]{2,1,0:T(8,128)(2,1)}, u32[]{:S(2)}) copy-start(bf16[1,144,3072]{2,1,0:T(8,128)(2,1)} %param.23) | copy-start | bytes 2654212
  5.7 34.1 %collective-permute-start = (bf16[128,3072]{1,0:T(8,128)(2,1)}, bf16[128,3072]{1,0:T(8,128)(2,1)}, u32[]{:S(2)}, u32[]{:S(2)}) collective-permute-start(bf16[128,3072]{1,0:T(8,128)(2,1)} %get-tuple-element.22), channel_id=1, source_target_pairs={{0,1},{1,2},{2,3},{3,0},{4,5},{5,6},{6,7},{7,4},{8,9},{9,10},{10,1... | collective-permute-start | bytes 2359304 | tf_op jit(solution)/shard_map/ppermute | solution.py:334
  7.3 43.5 %collective-permute-start.10 = (bf16[128,3072]{1,0:T(8,128)(2,1)}, bf16[128,3072]{1,0:T(8,128)(2,1)}, u32[]{:S(2)}, u32[]{:S(2)}) collective-permute-start(bf16[128,3072]{1,0:T(8,128)(2,1)} %get-tuple-element.39), channel_id=1, source_target_pairs={{0,2},{1,3},{2,0},{3,1},{4,6},{5,7},{6,4},{7,5},{8,10},{9,11},{10,... | collective-permute-start | bytes 2359304 | tf_op jit(solution)/shard_map/ppermute | solution.py:334
  10.2 41.8 %collective-permute-start.11 = (bf16[128,3072]{1,0:T(8,128)(2,1)}, bf16[128,3072]{1,0:T(8,128)(2,1)}, u32[]{:S(2)}, u32[]{:S(2)}) collective-permute-start(bf16[128,3072]{1,0:T(8,128)(2,1)} %get-tuple-element.40), channel_id=1, source_target_pairs={{0,3},{1,0},{2,1},{3,2},{4,7},{5,4},{6,5},{7,6},{8,11},{9,8},{10,9... | collective-permute-start | bytes 2359304 | tf_op jit(solution)/shard_map/ppermute | solution.py:334
  14.0 24.0 %all-to-all-start = ((bf16[64,16,128]{2,1,0:T(8,128)(2,1)}), bf16[64,16,128]{2,1,0:T(8,128)(2,1)}, u32[]{:S(2)}, u32[]{:S(2)}) async-start(bf16[64,16,128]{2,1,0:T(8,128)(2,1)} %bitcast.33), calls=%async_computation | async-start | bytes 524288 | tf_op jit(solution)/shard_map/all_to_all | solution.py:365
  31.6 20.4 %copy-start = (bf16[1,3072,144]{1,2,0:T(8,128)(2,1)S(1)}, bf16[1,3072,144]{1,2,0:T(8,128)(2,1)}, u32[]{:S(2)}) copy-start(bf16[1,3072,144]{1,2,0:T(8,128)(2,1)} %param.21) | copy-start | bytes 2654212
  31.6 20.4 %copy-start.1 = (bf16[1,3072,144]{1,2,0:T(8,128)(2,1)S(1)}, bf16[1,3072,144]{1,2,0:T(8,128)(2,1)}, u32[]{:S(2)}) copy-start(bf16[1,3072,144]{1,2,0:T(8,128)(2,1)} %param.22) | copy-start | bytes 2654212
  34.0 17.1 %collective-permute-start.4 = (bf16[144,768]{1,0:T(8,128)(2,1)}, bf16[144,768]{1,0:T(8,128)(2,1)}, u32[]{:S(2)}, u32[]{:S(2)}) collective-permute-start(bf16[144,768]{1,0:T(8,128)(2,1)} %get-tuple-element.44), channel_id=1, source_target_pairs={{0,8},{8,16},{16,24},{24,0},{1,9},{9,17},{17,25},{25,1},{2,10},{10... | collective-permute-start | bytes 663560 | tf_op jit(solution)/shard_map/ppermute | solution.py:334
  34.6 16.9 %collective-permute-start.6 = (bf16[144,768]{1,0:T(8,128)(2,1)}, bf16[144,768]{1,0:T(8,128)(2,1)}, u32[]{:S(2)}, u32[]{:S(2)}) collective-permute-start(bf16[144,768]{1,0:T(8,128)(2,1)} %get-tuple-element.43), channel_id=1, source_target_pairs={{0,16},{8,24},{16,0},{24,8},{1,17},{9,25},{17,1},{25,9},{2,18},{10... | collective-permute-start | bytes 663560 | tf_op jit(solution)/shard_map/ppermute | solution.py:334
  39.8 11.8 %collective-permute-start.8 = (bf16[144,768]{1,0:T(8,128)(2,1)}, bf16[144,768]{1,0:T(8,128)(2,1)}, u32[]{:S(2)}, u32[]{:S(2)}) collective-permute-start(bf16[144,768]{1,0:T(8,128)(2,1)} %get-tuple-element.42), channel_id=1, source_target_pairs={{0,24},{8,0},{16,8},{24,16},{1,25},{9,1},{17,9},{25,17},{2,26},{10... | collective-permute-start | bytes 663560 | tf_op jit(solution)/shard_map/ppermute | solution.py:334
  40.7 32.5 %all-to-all-start.1 = ((bf16[64,16,128]{2,1,0:T(8,128)(2,1)}), bf16[64,16,128]{2,1,0:T(8,128)(2,1)}, u32[]{:S(2)}, u32[]{:S(2)}) async-start(bf16[64,16,128]{2,1,0:T(8,128)(2,1)} %scan_states.1), calls=%async_computation.1 | async-start | bytes 524288 | tf_op jit(solution)/shard_map/all_to_all | solution.py:368
  50.9 7.8 %collective-permute-start.3 = (bf16[144,768]{1,0:T(8,128)(2,1)}, bf16[144,768]{1,0:T(8,128)(2,1)S(1)}, u32[]{:S(2)}, u32[]{:S(2)}) collective-permute-start(bf16[144,768]{1,0:T(8,128)(2,1)} %get-tuple-element.45.refs_0_), channel_id=1, source_target_pairs={{0,4},{4,0},{1,5},{5,1},{2,6},{6,2},{3,7},{7,3},{8,12},{12,8},{9,1... | collective-permute-start | bytes 663560 | tf_op jit(solution)/shard_map/ppermute | solution.py:334
  51.1 10.5 %collective-permute-start.5 = (bf16[144,768]{1,0:T(8,128)(2,1)}, bf16[144,768]{1,0:T(8,128)(2,1)S(1)}, u32[]{:S(2)}, u32[]{:S(2)}) collective-permute-start(bf16[144,768]{1,0:T(8,128)(2,1)} %collective-permute-done.4.refs_1_), channel_id=1, source_target_pairs={{0,4},{4,0},{1,5},{5,1},{2,6},{6,2},{3,7},{7,3},{8,12},{12,8},{9,1... | collective-permute-start | bytes 663560 | tf_op jit(solution)/shard_map/ppermute | solution.py:334
  51.5 14.3 %collective-permute-start.7 = (bf16[144,768]{1,0:T(8,128)(2,1)}, bf16[144,768]{1,0:T(8,128)(2,1)}, u32[]{:S(2)}, u32[]{:S(2)}) collective-permute-start(bf16[144,768]{1,0:T(8,128)(2,1)} %collective-permute-done.6.refs_2_), channel_id=1, source_target_pairs={{0,4},{4,0},{1,5},{5,1},{2,6},{6,2},{3,7},{7,3},{8,12},{12,8},{9,1... | collective-permute-start | bytes 663560 | tf_op jit(solution)/shard_map/ppermute | solution.py:334
  51.6 14.2 %collective-permute-start.9 = (bf16[144,768]{1,0:T(8,128)(2,1)}, bf16[144,768]{1,0:T(8,128)(2,1)}, u32[]{:S(2)}, u32[]{:S(2)}) collective-permute-start(bf16[144,768]{1,0:T(8,128)(2,1)} %collective-permute-done.8.refs_3_), channel_id=1, source_target_pairs={{0,4},{4,0},{1,5},{5,1},{2,6},{6,2},{3,7},{7,3},{8,12},{12,8},{9,1... | collective-permute-start | bytes 663560 | tf_op jit(solution)/shard_map/ppermute | solution.py:334
  52.0 1.1 copy-start.3
  58.0 13.7 %collective-permute-start.12 = (bf16[288,384]{1,0:T(8,128)(2,1)}, bf16[288,384]{1,0:T(8,128)(2,1)}, u32[]{:S(2)}, u32[]{:S(2)}) collective-permute-start(bf16[288,384]{1,0:T(8,128)(2,1)} %hidden_part.3.refs_8_), channel_id=1, source_target_pairs={{0,8},{8,16},{16,24},{24,0},{1,9},{9,17},{17,25},{25,1},{2,10},{10... | collective-permute-start | bytes 663560 | tf_op jit(solution)/shard_map/ppermute | solution.py:334
  58.7 0.7 copy-start.4
  59.3 13.9 %collective-permute-start.13 = (bf16[288,384]{1,0:T(8,128)(2,1)}, bf16[288,384]{1,0:T(8,128)(2,1)}, u32[]{:S(2)}, u32[]{:S(2)}) collective-permute-start(bf16[288,384]{1,0:T(8,128)(2,1)} %hidden_part.3.refs_8_), channel_id=1, source_target_pairs={{0,16},{8,24},{16,0},{24,8},{1,17},{9,25},{17,1},{25,9},{2,18},{10... | collective-permute-start | bytes 663560 | tf_op jit(solution)/shard_map/ppermute | solution.py:334
  61.7 0.7 copy-start.6
  62.3 10.9 %collective-permute-start.14 = (bf16[288,384]{1,0:T(8,128)(2,1)}, bf16[288,384]{1,0:T(8,128)(2,1)}, u32[]{:S(2)}, u32[]{:S(2)}) collective-permute-start(bf16[288,384]{1,0:T(8,128)(2,1)} %hidden_part.3.refs_8_), channel_id=1, source_target_pairs={{0,24},{8,0},{16,8},{24,16},{1,25},{9,1},{17,9},{25,17},{2,26},{10... | collective-permute-start | bytes 663560 | tf_op jit(solution)/shard_map/ppermute | solution.py:334
  68.7 5.4 %collective-permute-start.15 = (bf16[288,128]{1,0:T(8,128)(2,1)}, bf16[288,128]{1,0:T(8,128)(2,1)S(1)}, u32[]{:S(2)}, u32[]{:S(2)}) collective-permute-start(bf16[288,128]{1,0:T(8,128)(2,1)} %hidden_part.2.refs_12_), channel_id=1, source_target_pairs={{0,8},{8,16},{16,24},{24,0},{1,9},{9,17},{17,25},{25,1},{2,10},{10... | collective-permute-start | bytes 221192 | tf_op jit(solution)/shard_map/ppermute | solution.py:334
  71.8 6.1 %collective-permute-start.16 = (bf16[288,128]{1,0:T(8,128)(2,1)}, bf16[288,128]{1,0:T(8,128)(2,1)S(1)}, u32[]{:S(2)}, u32[]{:S(2)}) collective-permute-start(bf16[288,128]{1,0:T(8,128)(2,1)} %hidden_part.2.refs_12_), channel_id=1, source_target_pairs={{0,16},{8,24},{16,0},{24,8},{1,17},{9,25},{17,1},{25,9},{2,18},{10... | collective-permute-start | bytes 221192 | tf_op jit(solution)/shard_map/ppermute | solution.py:334
  71.8 6.6 %collective-permute-start.17 = (bf16[288,128]{1,0:T(8,128)(2,1)}, bf16[288,128]{1,0:T(8,128)(2,1)S(1)}, u32[]{:S(2)}, u32[]{:S(2)}) collective-permute-start(bf16[288,128]{1,0:T(8,128)(2,1)} %hidden_part.2.refs_12_), channel_id=1, source_target_pairs={{0,24},{8,0},{16,8},{24,16},{1,25},{9,1},{17,9},{25,17},{2,26},{10... | collective-permute-start | bytes 221192 | tf_op jit(solution)/shard_map/ppermute | solution.py:334
  78.4 0.9 copy-start.2
  79.3 0.9 copy-start.5
  80.2 0.9 copy-start.7
  86.4 38.2 %all-to-all-start.2 = ((bf16[64,48,128]{2,1,0:T(8,128)(2,1)}), bf16[64,48,128]{2,1,0:T(8,128)(2,1)S(1)}, u32[]{:S(2)}, u32[]{:S(2)}) async-start(bf16[64,48,128]{2,1,0:T(8,128)(2,1)} %bitcast.15), calls=%async_computation.2 | async-start | bytes 1572864 | tf_op jit(solution)/shard_map/all_to_all | solution.py:396
  124.6 0.9 copy-start.8

commit v5 on v4

--- a/solution.py
+++ b/solution.py
@@ -39,6 +39,7 @@
         in_specs=[pl.BlockSpec(memory_space=pltpu.SMEM), spec, spec],
         out_specs=pl.BlockSpec((GROUP * HEAD, HEAD), lambda h: (h, 0)),
         out_shape=jax.ShapeDtypeStruct((width, HEAD), BF),
+        compiler_params=pltpu.CompilerParams(vmem_limit_bytes=8 << 20),
         name="local_states",
     )(rate, keys, values)
 
@@ -62,6 +63,7 @@
         ],
         out_specs=pl.BlockSpec(memory_space=pltpu.VMEM),
         out_shape=jax.ShapeDtypeStruct(states.shape, BF),
+        compiler_params=pltpu.CompilerParams(vmem_limit_bytes=6 << 20),
         name="scan_states",
     )(rate, states)
 
@@ -93,6 +95,7 @@
         in_specs=[pl.BlockSpec(memory_space=pltpu.SMEM), spec, spec, spec],
         out_specs=spec,
         out_shape=jax.ShapeDtypeStruct((tokens, width), F32),
+        compiler_params=pltpu.CompilerParams(vmem_limit_bytes=14 << 20),
         name="intra_part",
     )(rate, queries, keys, values)
 
@@ -134,13 +137,16 @@
             jax.ShapeDtypeStruct((tokens, width), F32),
             jax.ShapeDtypeStruct((1, tokens), F32),
         ],
+        compiler_params=pltpu.CompilerParams(vmem_limit_bytes=14 << 20),
         name="mix_part",
     )(rate, intra, queries, prefix)
 
 
-def _norm_kernel(features, total, mixed, gain, gates, out):
+def _norm_kernel(features, *refs):
+    *squares, mixed, gain, gates, out = refs
     tokens = mixed.shape[0]
-    factor = lax.rsqrt(total[...] / features + 1e-06)
+    total = sum((part[...] for part in squares[1:]), squares[0][...])
+    factor = lax.rsqrt(total / features + 1e-06)
     column = jnp.transpose(jnp.broadcast_to(factor, (HEAD, tokens)))
     for h in range(GROUP):
         at = slice(h * HEAD, (h + 1) * HEAD)
@@ -148,26 +154,20 @@
         out[:, at] = (scaled * jax.nn.sigmoid(gates[:, at].astype(F32))).astype(BF)
 
 
-def norm_part(features, total, mixed, gain, gates):
+def norm_part(features, squares, mixed, gain, gates):
     tokens, width = mixed.shape
     spec = pl.BlockSpec((tokens, GROUP * HEAD), lambda h: (0, h))
-
-    def kernel(*refs):
-        _norm_kernel(features, *refs)
-
-    return pl.pallas_call(
-        kernel,
+    row = pl.BlockSpec((1, tokens), lambda h: (0, 0))
+    return pl.pallas_call(
+        functools.partial(_norm_kernel, features),
         grid=(width // (GROUP * HEAD),),
-        in_specs=[
-            pl.BlockSpec((1, tokens), lambda h: (0, 0)),
-            spec,
-            pl.BlockSpec((1, GROUP * HEAD), lambda h: (0, h)),
-            spec,
-        ],
+        in_specs=[row] * len(squares)
+        + [spec, pl.BlockSpec((1, GROUP * HEAD), lambda h: (0, h)), spec],
         out_specs=spec,
         out_shape=jax.ShapeDtypeStruct((tokens, width), BF),
+        compiler_params=pltpu.CompilerParams(vmem_limit_bytes=14 << 20),
         name="norm_part",
-    )(total, mixed, gain, gates)
+    )(*squares, mixed, gain, gates)
 
 
 def _pick_kernel(ids, rows, *refs):
@@ -219,6 +219,7 @@
             pltpu.SemaphoreType.DMA((count, 2)),
             pltpu.SemaphoreType.DMA((count,)),
         ],
+        compiler_params=pltpu.CompilerParams(vmem_limit_bytes=8 << 20),
         name="pick_tiles",
     )(ids, rows)
 
@@ -247,69 +248,92 @@
         out_specs=vmem,
         out_shape=jax.ShapeDtypeStruct((2 * units, count * TILE), BF),
         scratch_shapes=[pltpu.VMEM((count * TILE, model), BF)],
-        compiler_params=pltpu.CompilerParams(vmem_limit_bytes=40 << 20),
+        compiler_params=pltpu.CompilerParams(vmem_limit_bytes=24 << 20),
         name="hidden_part",
     )(*rows, *weights)
 
 
-def _down_kernel(groups, own, other, hidden, out):
-    n_exp, me_e = lax.axis_size("exp"), lax.axis_index("exp")
+def _down_kernel(own, other, hidden, out):
     n_x = len(own)
     units = own[0].shape[0]
-    blocks, columns = out.shape[0], out.shape[2]
-    for slots, held in zip(groups, hidden):
+    blocks, slots, columns = out.shape[:3]
+    wide = 2 * TILE
+    for j in range(slots // 2):
         total = None
         for k in range(n_x):
             for i, part in enumerate((own[k], other[k])):
-                h = held[k][i * units : (i + 1) * units, :]
+                h = hidden[k][i * units : (i + 1) * units, j * wide : (j + 1) * wide]
                 term = lax.dot_general(
                     part[...], h, (((0,), (0,)), ((), ())), preferred_element_type=F32
                 )
                 total = term if total is None else total + term
         total = total.astype(BF)
-        for i, slot in enumerate(slots):
-            home = lax.rem(me_e + n_exp - slot, n_exp)
+        for i in range(2):
             block = total[:, i * TILE : (i + 1) * TILE]
-            out[:, home] = block.reshape(blocks, columns, TILE)
-
-
-def down_part(groups, own, other, hidden, blocks, columns):
-    n_x = len(own)
-    n_slots = sum(len(slots) for slots in groups)
+            out[:, 2 * j + i] = block.reshape(blocks, columns, TILE)
+
+
+def down_part(own, other, hidden, blocks, columns):
+    n_x, slots = len(own), hidden[0].shape[1] // TILE
     vmem = pl.BlockSpec(memory_space=pltpu.VMEM)
 
     def kernel(*refs):
-        held = [
-            refs[n_x * (2 + g) : n_x * (3 + g)] for g in range(len(groups))
-        ]
-        _down_kernel(groups, refs[:n_x], refs[n_x : 2 * n_x], held, refs[-1])
-
-    flat = [piece for held in hidden for piece in held]
+        _down_kernel(
+            refs[:n_x], refs[n_x : 2 * n_x], refs[2 * n_x : 3 * n_x], refs[-1]
+        )
+
     return pl.pallas_call(
         kernel,
-        in_specs=[vmem] * (2 * n_x + len(flat)),
+        in_specs=[vmem] * (3 * n_x),
         out_specs=vmem,
-        out_shape=jax.ShapeDtypeStruct((blocks, n_slots, columns, TILE), BF),
-        compiler_params=pltpu.CompilerParams(vmem_limit_bytes=40 << 20),
+        out_shape=jax.ShapeDtypeStruct((blocks, slots, columns, TILE), BF),
+        compiler_params=pltpu.CompilerParams(vmem_limit_bytes=24 << 20),
         name="down_part",
-    )(*own, *other, *flat)
-
-
-def _finish_kernel(ids, parts, weight, out):
-    n_z, n_core, n_exp, columns, _ = parts.shape
+    )(*own, *other, *hidden)
+
+
+def _sum_kernel(parts, *outs):
+    n_z, n_core = parts.shape[:2]
+    for k, out in enumerate(outs):
+        for core in range(n_core):
+            total = parts[0, core, k].astype(F32)
+            for z in range(1, n_z):
+                total = total + parts[z, core, k].astype(F32)
+            out[core] = total.astype(BF)
+
+
+def sum_part(parts):
+    _, n_core, slots, columns, _ = parts.shape
+    vmem = pl.BlockSpec(memory_space=pltpu.VMEM)
+    block = jax.ShapeDtypeStruct((n_core, columns, TILE), BF)
+    return pl.pallas_call(
+        _sum_kernel,
+        in_specs=[vmem],
+        out_specs=[vmem] * slots,
+        out_shape=[block] * slots,
+        compiler_params=pltpu.CompilerParams(vmem_limit_bytes=8 << 20),
+        name="sum_part",
+    )(parts)
+
+
+def _finish_kernel(ids, *refs):
+    *parts, weight, out = refs
+    n_exp, me_e = lax.axis_size("exp"), lax.axis_index("exp")
+    columns = out.shape[0]
     tiles, half = ids.shape[0], TILE // 2
     low = lax.broadcasted_iota(jnp.int32, (columns, TILE), 1) < half
     for t in range(tiles):
         rank = jnp.int32(0)
         for earlier in range(t):
             rank = rank + (ids[earlier] == ids[t]).astype(jnp.int32)
-        sums = []
-        for core in range(n_core):
-            total = jnp.zeros((columns, TILE), F32)
-            for z in range(n_z):
-                total = total + parts[z, core, ids[t]].astype(F32)
-            sums.append(total.astype(BF).astype(F32))
-        first, second = sums
+        slot = lax.rem(ids[t] + n_exp - me_e, n_exp)
+        halves = []
+        for core in range(2):
+            found = parts[0][core].astype(F32)
+            for k in range(1, n_exp):
+                found = jnp.where(slot == k, parts[k][core].astype(F32), found)
+            halves.append(found)
+        first, second = halves
         zero = jnp.where(low, first, pltpu.roll(second, half, 1))
         one = jnp.where(low, pltpu.roll(first, half, 1), second)
         rows = jnp.where(rank == 0, zero, one)
@@ -318,15 +342,16 @@
 
 
 def finish_part(ids, parts, weight):
-    columns = parts.shape[3]
+    columns = parts[0].shape[1]
     vmem = pl.BlockSpec(memory_space=pltpu.VMEM)
     return pl.pallas_call(
         _finish_kernel,
-        in_specs=[pl.BlockSpec(memory_space=pltpu.SMEM), vmem, vmem],
+        in_specs=[pl.BlockSpec(memory_space=pltpu.SMEM)] + [vmem] * (len(parts) + 1),
         out_specs=vmem,
         out_shape=jax.ShapeDtypeStruct((columns, weight.shape[1]), BF),
+        compiler_params=pltpu.CompilerParams(vmem_limit_bytes=6 << 20),
         name="finish_part",
-    )(ids, parts, weight)
+    )(ids, *parts, weight)
 
 
 def shift(array, axis, by):
@@ -368,14 +393,11 @@
     prefix = lax.all_to_all(pieces, CTX, 0, 0, tiled=True).reshape(width, HEAD)
     intra = intra_part(decay_rate, queries, keys, values)
 
-    split = w_down[0].reshape(units, n_z, n_x, n_core * columns)
-    split = jnp.transpose(split, (2, 0, 1, 3)).reshape(n_x, units, chunk)
     me_x = lax.axis_index("x")
     down_own, down_other = [], []
     for k in range(n_x):
-        part = lax.dynamic_index_in_dim(
-            split, lax.rem(me_x + k, n_x), 0, keepdims=False
-        )
+        start = lax.rem(me_x + k, n_x) * chunk
+        part = lax.dynamic_slice(w_down[0], (0, start), (units, chunk))
         part = shift(part, "x", k) if k else part
         down_own.append(part)
         down_other.append(shift(part, "core", 1))
@@ -384,24 +406,31 @@
     )
 
     weights = (gate_own, gate_other, up_own, up_other)
-    early = [k for k in range(n_exp) if k != LAST]
-    groups = [early, [LAST]]
-    hidden = []
-    for slots in groups:
-        mine = hidden_part([arrived[k] for k in slots], weights)
-        hidden.append([mine] + [shift(mine, "x", k) for k in range(1, n_x)])
-    hidden[-1][0], prefix = lax.optimization_barrier((hidden[-1][0], prefix))
-    parts = down_part(groups, down_own, down_other, hidden, n_z * n_core, columns)
-    parts = parts.reshape(-1, columns, TILE)
-    parts = lax.all_to_all(parts, ("z", "core", "exp"), 0, 0, tiled=True)
-    parts = parts.reshape(n_z, n_core, n_exp, columns, TILE)
+    hidden = hidden_part(arrived, weights)
+    hidden = [hidden] + [shift(hidden, "x", k) for k in range(1, n_x)]
+    parts = down_part(down_own, down_other, hidden, n_z * n_core, columns)
+    parts, prefix = lax.optimization_barrier((parts, prefix))
+    parts = lax.all_to_all(parts, ("z", "core"), 0, 0, tiled=True)
 
     mixed, squares = mix_part(decay_rate, intra, queries, prefix)
-    total = lax.psum(squares, "exp")
+    squares = [squares] + [shift(squares, "exp", k) for k in range(1, n_exp)]
+    parts, *squares = lax.optimization_barrier((parts, *squares))
     attention_out = norm_part(
-        float(width * n_exp), total, mixed, norm_gain[None, :], gates
+        float(width * n_exp), squares, mixed, norm_gain[None, :], gates
     )
-    moe_out = jnp.swapaxes(finish_part(ids, parts, row_weight[None, :]), 0, 1)
+
+    parts = sum_part(parts.reshape(n_z, n_core, n_exp, columns, TILE))
+    homes = []
+    for k in range(n_exp):
+        pairs = []
+        for z in range(n_z):
+            for x in range(n_x):
+                chip = x * n_z + z
+                for e in range(n_exp):
+                    home = chip * n_exp + (e + n_exp - k) % n_exp
+                    pairs.append(((z * n_x + x) * n_exp + e, home))
+        homes.append(lax.ppermute(parts[k], ("z", "x", "exp"), pairs))
+    moe_out = jnp.swapaxes(finish_part(ids, homes, row_weight[None, :]), 0, 1)
     return attention_out, moe_out
 
 

time: 129 us -> 150 us (1.16)
  starting transfers between devices: 56.1 us -> 88.4 us
  waiting for transfers between devices: 13.6 us -> 26.7 us
  blocking collectives: 11.2 us -> 0 us
  Pallas kernels: 31.7 us -> 22.8 us
  local copies, waits for them, and re-layouts: 14.1 us -> 10.4 us
    ppermute x0 -> x4, starting transfers between devices: none -> 23 us  [on_device(): homes.append(lax.ppermute(parts[k], ('z', 'x', 'exp'), pairs))]
    ppermute x18, starting transfers between devices: 18.9 us -> 38.4 us  [shift(): return lax.ppermute(array, axis, [(i, (i + by) % n) for i in range(n)])]
    ppermute x18, waiting for transfers between devices: 5.17 us -> 19.5 us  [shift(): return lax.ppermute(array, axis, [(i, (i + by) % n) for i in range(n)])]
    psum x1 -> x0, blocking collectives: 11.2 us -> none  [on_device(): total = lax.psum(squares, 'exp')]
    all_to_all x1, starting transfers between devices: 14.8 us -> 7.11 us  [on_device(): parts = lax.all_to_all(parts, ('z', 'core'), 0, 0, tiled=True)]
    unnamed x20 -> x44, local copies, waits for them, and re-layouts: 6.23 us -> 9.06 us
    squeeze x1 -> x0, local copies, waits for them, and re-layouts: 2.39 us -> none  [on_device(): lax.dynamic_index_in_dim(split, lax.rem(me_x + k, n_x), 0, keepdims=False)]
    all_to_all x1, starting transfers between devices: 10.2 us -> 7.9 us  [on_device(): prefix = lax.all_to_all(pieces, CTX, 0, 0, tiled=True).reshape(width, HEAD)]
  transfers between devices with their start and end apart: 21 -> 25, of which waited for: 5 -> 6; matrix products, arithmetic and copies ran while one was open for 6% -> 1% of each run, Pallas kernels for 19% -> 14%
where the time goes in v5:
time: 150 us; the launch traced here: 149 us
  starting transfers between devices  88.4 us (59%)
  waiting for transfers between devices  26.7 us (18%)
  Pallas kernels  22.8 us (15%)
  local copies, waits for them, and re-layouts  10.4 us (7%)
    ppermute x18, starting transfers between devices, shift(): return lax.ppermute(array, axis, [(i, (i + by) % n) for i in range(n)])  38.4 us
    ppermute x4, starting transfers between devices, on_device(): homes.append(lax.ppermute(parts[k], ('z', 'x', 'exp'), pairs))  23 us
    ppermute x18, waiting for transfers between devices, shift(): return lax.ppermute(array, axis, [(i, (i + by) % n) for i in range(n)])  19.5 us
    all_to_all x1, starting transfers between devices, on_device(): pieces = lax.all_to_all(pieces, CTX, 0, 0, tiled=True)  12 us
    unnamed x44, local copies, waits for them, and re-layouts  9.06 us
    all_to_all x1, starting transfers between devices, on_device(): prefix = lax.all_to_all(pieces, CTX, 0, 0, tiled=True).reshape(width, HEAD)  7.9 us
    all_to_all x1, waiting for transfers between devices, on_device(): parts = lax.all_to_all(parts, ('z', 'core'), 0, 0, tiled=True)  7.2 us
    all_to_all x1, starting transfers between devices, on_device(): parts = lax.all_to_all(parts, ('z', 'core'), 0, 0, tiled=True)  7.11 us
  transfers between devices with their start and end apart: 25, of which 6 were waited for; matrix products, arithmetic and copies ran while one was open for 1% of the time, Pallas kernels for 14%

profile of v5, /device:TPU:6, one launch (start us, length us, event | category | flops | bytes accessed | tf_op | source)
XLA Modules:
  0.0 149.2 jit_solution(8941719354103357310)
XLA Ops:
  1.2 1.9 %copy-done = bf16[512,3072]{1,0:T(8,128)(2,1)S(1)} copy-done((bf16[512,3072]{1,0:T(8,128)(2,1)S(1)}, bf16[512,3072]{1,0:T(8,128)(2,1)}, u32[]{:S(2)}) %copy-start) | copy-done | bytes 3145752
  3.8 3.6 %pick_tiles.1 = (bf16[128,3072]{1,0:T(8,128)(2,1)}, bf16[128,3072]{1,0:T(8,128)(2,1)}, bf16[128,3072]{1,0:T(8,128)(2,1)}, bf16[128,3072]{1,0:T(8,128)(2,1)S(1)}) custom-call(s32[4]{0:T(128)S(1)} %bitcast.29, bf16[512,3072]{1,0:T(8,128)(2,1)S(1)} %copy-done), custom_call_target="tpu_custom_call" | custom-call | tf_op jit(solution)/shard_map/pick_tiles/pallas_call | solution.py:209
  8.3 1.6 %collective-permute-start.5 = (bf16[128,3072]{1,0:T(8,128)(2,1)}, bf16[128,3072]{1,0:T(8,128)(2,1)}, u32[]{:S(2)}, u32[]{:S(2)}) collective-permute-start(bf16[128,3072]{1,0:T(8,128)(2,1)} %get-tuple-element.32), channel_id=1, source_target_pairs={{0,1},{1,2},{2,3},{3,0},{4,5},{5,6},{6,7},{7,4},{8,9},{9,10},{10,1... | collective-permute-start | bytes 2359304 | tf_op jit(solution)/shard_map/ppermute | solution.py:359
  9.9 2.9 %collective-permute-start.10 = (bf16[128,3072]{1,0:T(8,128)(2,1)}, bf16[128,3072]{1,0:T(8,128)(2,1)}, u32[]{:S(2)}, u32[]{:S(2)}) collective-permute-start(bf16[128,3072]{1,0:T(8,128)(2,1)} %get-tuple-element.41), channel_id=1, source_target_pairs={{0,2},{1,3},{2,0},{3,1},{4,6},{5,7},{6,4},{7,5},{8,10},{9,11},{10,... | collective-permute-start | bytes 2359304 | tf_op jit(solution)/shard_map/ppermute | solution.py:359
  12.8 1.3 collective-permute-start.11
  14.2 1.9 %local_states.1 = bf16[1024,128]{1,0:T(8,128)(2,1)} custom-call(f32[8]{0:T(128)S(1)} %copy-done.17, bf16[256,1024]{1,0:T(8,128)(2,1)S(1)} %copy-done.1, bf16[256,1024]{1,0:T(8,128)(2,1)S(1)} %copy-done.2), custom_call_target="tpu_custom_call" | custom-call | tf_op jit(solution)/shard_map/local_states/pallas_call | solution.py:36
  16.1 12.0 %all-to-all-start = ((bf16[64,16,128]{2,1,0:T(8,128)(2,1)}), bf16[64,16,128]{2,1,0:T(8,128)(2,1)S(1)}, u32[]{:S(2)}, u32[]{:S(2)}) async-start(bf16[64,16,128]{2,1,0:T(8,128)(2,1)} %bitcast.9), calls=%async_computation | async-start | bytes 524288 | tf_op jit(solution)/shard_map/all_to_all | solution.py:390
  28.1 1.3 dynamic-slice_bitcast_fusion
  31.4 17.0 %collective-permute-start.2 = (bf16[144,768]{1,0:T(8,128)(2,1)S(1)}, bf16[144,768]{1,0:T(8,128)(2,1)}, u32[]{:S(2)}, u32[]{:S(2)}) collective-permute-start(bf16[144,768]{1,0:T(8,128)(2,1)S(1)} %get-tuple-element.62), channel_id=1, source_target_pairs={{0,8},{8,16},{16,24},{24,0},{1,9},{9,17},{17,25},{25,1},{2,10},{10... | collective-permute-start | bytes 663560 | tf_op jit(solution)/shard_map/ppermute | solution.py:359
  49.0 2.9 %collective-permute-done.2.refs_1_ = bf16[144,768]{1,0:T(8,128)(2,1)} collective-permute-done((bf16[144,768]{1,0:T(8,128)(2,1)S(1)}, bf16[144,768]{1,0:T(8,128)(2,1)}, u32[]{:S(2)}, u32[]{:S(2)}) %collective-permute-start.2) | collective-permute-done | bytes 221216 | tf_op jit(solution)/shard_map/ppermute | solution.py:359
  52.4 1.4 scan_states.1
  53.9 7.9 %all-to-all-start.1 = ((bf16[64,16,128]{2,1,0:T(8,128)(2,1)}), bf16[64,16,128]{2,1,0:T(8,128)(2,1)S(1)}, u32[]{:S(2)}, u32[]{:S(2)}) async-start(bf16[64,16,128]{2,1,0:T(8,128)(2,1)} %scan_states.1), calls=%async_computation.1 | async-start | bytes 524288 | tf_op jit(solution)/shard_map/all_to_all | solution.py:393
  61.8 2.0 %intra_part.1.intra = f32[256,1024]{1,0:T(8,128)S(1)} custom-call(f32[8]{0:T(128)S(1)} %copy-done.17, bf16[256,1024]{1,0:T(8,128)(2,1)S(1)} %copy-done.3, bf16[256,1024]{1,0:T(8,128)(2,1)S(1)} %copy-done.1, bf16[256,1024]{1,0:T(8,128)(2,1)S(1)} %copy-done.2), custom_call_target="tpu_custom_call" | custom-call | tf_op jit(solution)/shard_map/intra_part/pallas_call | solution.py:92
  63.9 1.2 copy-done.6
  65.1 1.2 copy-done.7
  66.3 5.9 %hidden_part.1.refs_8_ = bf16[288,512]{1,0:T(8,128)(2,1)S(1)} custom-call(bf16[128,3072]{1,0:T(8,128)(2,1)S(1)} %copy-done.13, bf16[128,3072]{1,0:T(8,128)(2,1)} %collective-permute-done.5.refs_1_, bf16[128,3072]{1,0:T(8,128)(2,1)} %collective-permute-done.10.refs_2_, bf16[128,3072]{1,0:T(8,128)(2,1)} %collective-permute-done.11.refs_3_, ...), custom_call_target="tpu_custom_call" | custom-call | tf_op jit(solution)/shard_map/hidden_part/pallas_call | solution.py:245
  73.1 1.3 collective-permute-start.13
  74.4 1.9 %collective-permute-start.12 = (bf16[288,512]{1,0:T(8,128)(2,1)S(1)}, bf16[288,512]{1,0:T(8,128)(2,1)S(1)}, u32[]{:S(2)}, u32[]{:S(2)}) collective-permute-start(bf16[288,512]{1,0:T(8,128)(2,1)S(1)} %hidden_part.1.refs_8_), channel_id=1, source_target_pairs={{0,8},{8,16},{16,24},{24,0},{1,9},{9,17},{17,25},{25,1},{2,10},{10... | collective-permute-start | bytes 884744 | tf_op jit(solution)/shard_map/ppermute | solution.py:359
  76.3 12.5 %collective-permute-done.14.refs_11_ = bf16[288,512]{1,0:T(8,128)(2,1)S(1)} collective-permute-done((bf16[288,512]{1,0:T(8,128)(2,1)S(1)}, bf16[288,512]{1,0:T(8,128)(2,1)S(1)}, u32[]{:S(2)}, u32[]{:S(2)}) %collective-permute-start.14) | collective-permute-done | bytes 294944 | tf_op jit(solution)/shard_map/ppermute | solution.py:359
  89.4 4.0 %down_part.1 = bf16[16,4,48,128]{3,2,1,0:T(8,128)(2,1)} custom-call(bf16[144,768]{1,0:T(8,128)(2,1)S(1)} %get-tuple-element.63.refs_0_, bf16[144,768]{1,0:T(8,128)(2,1)} %collective-permute-done.2.refs_1_, bf16[144,768]{1,0:T(8,128)(2,1)S(1)} %collective-permute-done.3.refs_2_, bf16[144,768]{1,0:T(8,128)(2,1)S(1)} %collective-permute-done.4.refs_3_, ...), custom_call_target="tpu_custom_call" | custom-call | tf_op jit(solution)/shard_map/down_part/pallas_call | solution.py:285
  93.5 7.1 %all-to-all-start.2 = ((bf16[16,4,48,128]{3,2,1,0:T(8,128)(2,1)}), bf16[16,4,48,128]{3,2,1,0:T(8,128)(2,1)S(1)}, u32[]{:S(2)}, u32[]{:S(2)}) async-start(bf16[16,4,48,128]{3,2,1,0:T(8,128)(2,1)} %down_part.1), calls=%async_computation.2 | async-start | bytes 1572864 | tf_op jit(solution)/shard_map/all_to_all | solution.py:413
  100.6 1.3 mix_part.1
  102.9 6.4 %collective-permute-start.16 = (f32[1,256]{1,0:T(1,128)S(1)}, f32[1,256]{1,0:T(1,128)S(1)}, u32[]{:S(2)}, u32[]{:S(2)}) collective-permute-start(f32[1,256]{1,0:T(1,128)S(1)} %get-tuple-element.50.refs_0_), channel_id=1, source_target_pairs={{0,2},{1,3},{2,0},{3,1},{4,6},{5,7},{6,4},{7,5},{8,10},{9,11},{10,... | collective-permute-start | bytes 3080 | tf_op jit(solution)/shard_map/ppermute | solution.py:359
  109.3 1.4 collective-permute-start.15
  110.8 3.2 %collective-permute-done.15.refs_1_ = f32[1,256]{1,0:T(1,128)S(1)} collective-permute-done((f32[1,256]{1,0:T(1,128)S(1)}, f32[1,256]{1,0:T(1,128)S(1)}, u32[]{:S(2)}, u32[]{:S(2)}) %collective-permute-start.15) | collective-permute-done | bytes 1056 | tf_op jit(solution)/shard_map/ppermute | solution.py:359
  114.1 7.2 %all-to-all-done.2 = bf16[16,4,48,128]{3,2,1,0:T(8,128)(2,1)S(1)} async-done(((bf16[16,4,48,128]{3,2,1,0:T(8,128)(2,1)}), bf16[16,4,48,128]{3,2,1,0:T(8,128)(2,1)S(1)}, u32[]{:S(2)}, u32[]{:S(2)}) %all-to-all-start.2) | async-done | bytes 786464 | tf_op jit(solution)/shard_map/all_to_all | solution.py:413
  121.4 6.3 %collective-permute-start.18 = (bf16[2,48,128]{2,1,0:T(8,128)(2,1)S(1)}, bf16[2,48,128]{2,1,0:T(8,128)(2,1)S(1)}, u32[]{:S(2)}, u32[]{:S(2)}) collective-permute-start(bf16[2,48,128]{2,1,0:T(8,128)(2,1)S(1)} %get-tuple-element.56), channel_id=1, source_target_pairs={{0,0},{1,1},{2,2},{3,3},{8,64},{9,65},{10,66},{11,67},{16,128},{17... | collective-permute-start | bytes 73736 | tf_op jit(solution)/shard_map/ppermute | solution.py:432
  128.6 6.9 %collective-permute-start.20 = (bf16[2,48,128]{2,1,0:T(8,128)(2,1)S(1)}, bf16[2,48,128]{2,1,0:T(8,128)(2,1)S(1)}, u32[]{:S(2)}, u32[]{:S(2)}) collective-permute-start(bf16[2,48,128]{2,1,0:T(8,128)(2,1)S(1)} %get-tuple-element.58), channel_id=1, source_target_pairs={{0,2},{1,3},{2,0},{3,1},{8,66},{9,67},{10,64},{11,65},{16,130},{17... | collective-permute-start | bytes 73736 | tf_op jit(solution)/shard_map/ppermute | solution.py:432
  135.5 8.9 %collective-permute-start.21 = (bf16[2,48,128]{2,1,0:T(8,128)(2,1)S(1)}, bf16[2,48,128]{2,1,0:T(8,128)(2,1)S(1)}, u32[]{:S(2)}, u32[]{:S(2)}) collective-permute-start(bf16[2,48,128]{2,1,0:T(8,128)(2,1)S(1)} %get-tuple-element.59), channel_id=1, source_target_pairs={{0,1},{1,2},{2,3},{3,0},{8,65},{9,66},{10,67},{11,64},{16,129},{17... | collective-permute-start | bytes 73736 | tf_op jit(solution)/shard_map/ppermute | solution.py:432
  144.4 1.2 copy-done.5
  146.7 1.2 norm_part.1
  147.9 1.3 finish_part.1
  (73 shorter events, 10.0 us)
Async XLA Ops:
  0.6 13.5 %copy-start.17 = (f32[8]{0:T(128)S(1)}, f32[8]{0:T(128)}, u32[]{:S(2)}) copy-start(f32[8]{0:T(128)} %rate.7) | copy-start | bytes 100
  0.6 13.5 %collective-permute-start = (bf16[144,3072]{1,0:T(8,128)(2,1)}, bf16[144,3072]{1,0:T(8,128)(2,1)S(1)}, u32[]{:S(2)}, u32[]{:S(2)}) collective-permute-start(bf16[144,3072]{1,0:T(8,128)(2,1)} %bitcast.23), channel_id=1, source_target_pairs={{0,4},{4,0},{1,5},{5,1},{2,6},{6,2},{3,7},{7,3},{8,12},{12,8},{9,1... | collective-permute-start | bytes 2654216 | tf_op jit(solution)/shard_map/ppermute | solution.py:359
  0.7 13.4 %collective-permute-start.1 = (bf16[144,3072]{1,0:T(8,128)(2,1)}, bf16[144,3072]{1,0:T(8,128)(2,1)S(1)}, u32[]{:S(2)}, u32[]{:S(2)}) collective-permute-start(bf16[144,3072]{1,0:T(8,128)(2,1)} %bitcast.25), channel_id=1, source_target_pairs={{0,4},{4,0},{1,5},{5,1},{2,6},{6,2},{3,7},{7,3},{8,12},{12,8},{9,1... | collective-permute-start | bytes 2654216 | tf_op jit(solution)/shard_map/ppermute | solution.py:359
  3.8 10.4 %copy-start.2 = (bf16[256,1024]{1,0:T(8,128)(2,1)S(1)}, bf16[256,1024]{1,0:T(8,128)(2,1)}, u32[]{:S(2)}) copy-start(bf16[256,1024]{1,0:T(8,128)(2,1)} %v.3) | copy-start | bytes 1572868
  8.3 53.4 %copy-start.3 = (bf16[256,1024]{1,0:T(8,128)(2,1)S(1)}, bf16[256,1024]{1,0:T(8,128)(2,1)}, u32[]{:S(2)}) copy-start(bf16[256,1024]{1,0:T(8,128)(2,1)} %q.3) | copy-start | bytes 1572868
  8.3 23.1 %collective-permute-start.5 = (bf16[128,3072]{1,0:T(8,128)(2,1)}, bf16[128,3072]{1,0:T(8,128)(2,1)}, u32[]{:S(2)}, u32[]{:S(2)}) collective-permute-start(bf16[128,3072]{1,0:T(8,128)(2,1)} %get-tuple-element.32), channel_id=1, source_target_pairs={{0,1},{1,2},{2,3},{3,0},{4,5},{5,6},{6,7},{7,4},{8,9},{9,10},{10,1... | collective-permute-start | bytes 2359304 | tf_op jit(solution)/shard_map/ppermute | solution.py:359
  9.9 54.0 %collective-permute-start.10 = (bf16[128,3072]{1,0:T(8,128)(2,1)}, bf16[128,3072]{1,0:T(8,128)(2,1)}, u32[]{:S(2)}, u32[]{:S(2)}) collective-permute-start(bf16[128,3072]{1,0:T(8,128)(2,1)} %get-tuple-element.41), channel_id=1, source_target_pairs={{0,2},{1,3},{2,0},{3,1},{4,6},{5,7},{6,4},{7,5},{8,10},{9,11},{10,... | collective-permute-start | bytes 2359304 | tf_op jit(solution)/shard_map/ppermute | solution.py:359
  12.8 51.1 %collective-permute-start.11 = (bf16[128,3072]{1,0:T(8,128)(2,1)}, bf16[128,3072]{1,0:T(8,128)(2,1)}, u32[]{:S(2)}, u32[]{:S(2)}) collective-permute-start(bf16[128,3072]{1,0:T(8,128)(2,1)} %get-tuple-element.42), channel_id=1, source_target_pairs={{0,3},{1,0},{2,1},{3,2},{4,7},{5,4},{6,5},{7,6},{8,11},{9,8},{10,9... | collective-permute-start | bytes 2359304 | tf_op jit(solution)/shard_map/ppermute | solution.py:359
  16.1 36.3 %all-to-all-start = ((bf16[64,16,128]{2,1,0:T(8,128)(2,1)}), bf16[64,16,128]{2,1,0:T(8,128)(2,1)S(1)}, u32[]{:S(2)}, u32[]{:S(2)}) async-start(bf16[64,16,128]{2,1,0:T(8,128)(2,1)} %bitcast.9), calls=%async_computation | async-start | bytes 524288 | tf_op jit(solution)/shard_map/all_to_all | solution.py:390
  29.4 19.0 %collective-permute-start.4 = (bf16[144,768]{1,0:T(8,128)(2,1)S(1)}, bf16[144,768]{1,0:T(8,128)(2,1)S(1)}, u32[]{:S(2)}, u32[]{:S(2)}) collective-permute-start(bf16[144,768]{1,0:T(8,128)(2,1)S(1)} %get-tuple-element.60), channel_id=1, source_target_pairs={{0,24},{8,0},{16,8},{24,16},{1,25},{9,1},{17,9},{25,17},{2,26},{10... | collective-permute-start | bytes 663560 | tf_op jit(solution)/shard_map/ppermute | solution.py:359
  30.4 18.1 %collective-permute-start.3 = (bf16[144,768]{1,0:T(8,128)(2,1)S(1)}, bf16[144,768]{1,0:T(8,128)(2,1)S(1)}, u32[]{:S(2)}, u32[]{:S(2)}) collective-permute-start(bf16[144,768]{1,0:T(8,128)(2,1)S(1)} %get-tuple-element.61), channel_id=1, source_target_pairs={{0,16},{8,24},{16,0},{24,8},{1,17},{9,25},{17,1},{25,9},{2,18},{10... | collective-permute-start | bytes 663560 | tf_op jit(solution)/shard_map/ppermute | solution.py:359
  31.4 20.5 %collective-permute-start.2 = (bf16[144,768]{1,0:T(8,128)(2,1)S(1)}, bf16[144,768]{1,0:T(8,128)(2,1)}, u32[]{:S(2)}, u32[]{:S(2)}) collective-permute-start(bf16[144,768]{1,0:T(8,128)(2,1)S(1)} %get-tuple-element.62), channel_id=1, source_target_pairs={{0,8},{8,16},{16,24},{24,0},{1,9},{9,17},{17,25},{25,1},{2,10},{10... | collective-permute-start | bytes 663560 | tf_op jit(solution)/shard_map/ppermute | solution.py:359
  48.5 3.5 %collective-permute-start.6 = (bf16[144,768]{1,0:T(8,128)(2,1)S(1)}, bf16[144,768]{1,0:T(8,128)(2,1)S(1)}, u32[]{:S(2)}, u32[]{:S(2)}) collective-permute-start(bf16[144,768]{1,0:T(8,128)(2,1)S(1)} %get-tuple-element.63.refs_0_), channel_id=1, source_target_pairs={{0,4},{4,0},{1,5},{5,1},{2,6},{6,2},{3,7},{7,3},{8,12},{12,8},{9,1... | collective-permute-start | bytes 663560 | tf_op jit(solution)/shard_map/ppermute | solution.py:359
  48.5 15.4 %collective-permute-start.9 = (bf16[144,768]{1,0:T(8,128)(2,1)S(1)}, bf16[144,768]{1,0:T(8,128)(2,1)}, u32[]{:S(2)}, u32[]{:S(2)}) collective-permute-start(bf16[144,768]{1,0:T(8,128)(2,1)S(1)} %collective-permute-done.4.refs_3_), channel_id=1, source_target_pairs={{0,4},{4,0},{1,5},{5,1},{2,6},{6,2},{3,7},{7,3},{8,12},{12,8},{9,1... | collective-permute-start | bytes 663560 | tf_op jit(solution)/shard_map/ppermute | solution.py:359
  51.9 11.9 %collective-permute-start.8 = (bf16[144,768]{1,0:T(8,128)(2,1)S(1)}, bf16[144,768]{1,0:T(8,128)(2,1)}, u32[]{:S(2)}, u32[]{:S(2)}) collective-permute-start(bf16[144,768]{1,0:T(8,128)(2,1)S(1)} %collective-permute-done.3.refs_2_), channel_id=1, source_target_pairs={{0,4},{4,0},{1,5},{5,1},{2,6},{6,2},{3,7},{7,3},{8,12},{12,8},{9,1... | collective-permute-start | bytes 663560 | tf_op jit(solution)/shard_map/ppermute | solution.py:359
  51.9 11.9 %collective-permute-start.7 = (bf16[144,768]{1,0:T(8,128)(2,1)}, bf16[144,768]{1,0:T(8,128)(2,1)}, u32[]{:S(2)}, u32[]{:S(2)}) collective-permute-start(bf16[144,768]{1,0:T(8,128)(2,1)} %collective-permute-done.2.refs_1_), channel_id=1, source_target_pairs={{0,4},{4,0},{1,5},{5,1},{2,6},{6,2},{3,7},{7,3},{8,12},{12,8},{9,1... | collective-permute-start | bytes 663560 | tf_op jit(solution)/shard_map/ppermute | solution.py:359
  53.9 39.6 %all-to-all-start.1 = ((bf16[64,16,128]{2,1,0:T(8,128)(2,1)}), bf16[64,16,128]{2,1,0:T(8,128)(2,1)S(1)}, u32[]{:S(2)}, u32[]{:S(2)}) async-start(bf16[64,16,128]{2,1,0:T(8,128)(2,1)} %scan_states.1), calls=%async_computation.1 | async-start | bytes 524288 | tf_op jit(solution)/shard_map/all_to_all | solution.py:393
  66.3 23.2 %copy-start.16 = (bf16[144,768]{1,0:T(8,128)(2,1)S(1)}, bf16[144,768]{1,0:T(8,128)(2,1)}, u32[]{:S(2)}) copy-start(bf16[144,768]{1,0:T(8,128)(2,1)} %copy-done.15) | copy-start | bytes 663556
  72.1 72.3 %copy-start.18 = (f32[1024]{0:T(1024)S(1)}, f32[1024]{0:T(1024)}, u32[]{:S(2)}) copy-start(f32[1024]{0:T(1024)} %param.17) | copy-start | bytes 12292
  72.1 16.7 %collective-permute-start.14 = (bf16[288,512]{1,0:T(8,128)(2,1)S(1)}, bf16[288,512]{1,0:T(8,128)(2,1)S(1)}, u32[]{:S(2)}, u32[]{:S(2)}) collective-permute-start(bf16[288,512]{1,0:T(8,128)(2,1)S(1)} %hidden_part.1.refs_8_), channel_id=1, source_target_pairs={{0,24},{8,0},{16,8},{24,16},{1,25},{9,1},{17,9},{25,17},{2,26},{10... | collective-permute-start | bytes 884744 | tf_op jit(solution)/shard_map/ppermute | solution.py:359
  73.1 15.8 %collective-permute-start.13 = (bf16[288,512]{1,0:T(8,128)(2,1)S(1)}, bf16[288,512]{1,0:T(8,128)(2,1)S(1)}, u32[]{:S(2)}, u32[]{:S(2)}) collective-permute-start(bf16[288,512]{1,0:T(8,128)(2,1)S(1)} %hidden_part.1.refs_8_), channel_id=1, source_target_pairs={{0,16},{8,24},{16,0},{24,8},{1,17},{9,25},{17,1},{25,9},{2,18},{10... | collective-permute-start | bytes 884744 | tf_op jit(solution)/shard_map/ppermute | solution.py:359
  74.4 15.0 %collective-permute-start.12 = (bf16[288,512]{1,0:T(8,128)(2,1)S(1)}, bf16[288,512]{1,0:T(8,128)(2,1)S(1)}, u32[]{:S(2)}, u32[]{:S(2)}) collective-permute-start(bf16[288,512]{1,0:T(8,128)(2,1)S(1)} %hidden_part.1.refs_8_), channel_id=1, source_target_pairs={{0,8},{8,16},{16,24},{24,0},{1,9},{9,17},{17,25},{25,1},{2,10},{10... | collective-permute-start | bytes 884744 | tf_op jit(solution)/shard_map/ppermute | solution.py:359
  93.5 54.4 %copy-start.19 = (f32[512]{0:T(512)S(1)}, f32[512]{0:T(512)}, u32[]{:S(2)}) copy-start(f32[512]{0:T(512)} %param.20) | copy-start | bytes 6148
  93.5 54.4 %copy-start.21 = (s32[4,1]{0,1:T(1,128)S(1)}, s32[4,1]{0,1:T(1,128)}, u32[]{:S(2)}) copy-start(s32[4,1]{0,1:T(1,128)} %param.19) | copy-start | bytes 52
  93.5 27.8 %all-to-all-start.2 = ((bf16[16,4,48,128]{3,2,1,0:T(8,128)(2,1)}), bf16[16,4,48,128]{3,2,1,0:T(8,128)(2,1)S(1)}, u32[]{:S(2)}, u32[]{:S(2)}) async-start(bf16[16,4,48,128]{3,2,1,0:T(8,128)(2,1)} %down_part.1), calls=%async_computation.2 | async-start | bytes 1572864 | tf_op jit(solution)/shard_map/all_to_all | solution.py:413
  102.9 7.8 %collective-permute-start.17 = (f32[1,256]{1,0:T(1,128)S(1)}, f32[1,256]{1,0:T(1,128)S(1)}, u32[]{:S(2)}, u32[]{:S(2)}) collective-permute-start(f32[1,256]{1,0:T(1,128)S(1)} %get-tuple-element.50.refs_0_), channel_id=1, source_target_pairs={{0,3},{1,0},{2,1},{3,2},{4,7},{5,4},{6,5},{7,6},{8,11},{9,8},{10,9... | collective-permute-start | bytes 3080 | tf_op jit(solution)/shard_map/ppermute | solution.py:359
  102.9 7.9 %collective-permute-start.16 = (f32[1,256]{1,0:T(1,128)S(1)}, f32[1,256]{1,0:T(1,128)S(1)}, u32[]{:S(2)}, u32[]{:S(2)}) collective-permute-start(f32[1,256]{1,0:T(1,128)S(1)} %get-tuple-element.50.refs_0_), channel_id=1, source_target_pairs={{0,2},{1,3},{2,0},{3,1},{4,6},{5,7},{6,4},{7,5},{8,10},{9,11},{10,... | collective-permute-start | bytes 3080 | tf_op jit(solution)/shard_map/ppermute | solution.py:359
  109.3 4.8 %collective-permute-start.15 = (f32[1,256]{1,0:T(1,128)S(1)}, f32[1,256]{1,0:T(1,128)S(1)}, u32[]{:S(2)}, u32[]{:S(2)}) collective-permute-start(f32[1,256]{1,0:T(1,128)S(1)} %get-tuple-element.50.refs_0_), channel_id=1, source_target_pairs={{0,1},{1,2},{2,3},{3,0},{4,5},{5,6},{6,7},{7,4},{8,9},{9,10},{10,1... | collective-permute-start | bytes 3080 | tf_op jit(solution)/shard_map/ppermute | solution.py:359
  121.4 26.5 %collective-permute-start.18 = (bf16[2,48,128]{2,1,0:T(8,128)(2,1)S(1)}, bf16[2,48,128]{2,1,0:T(8,128)(2,1)S(1)}, u32[]{:S(2)}, u32[]{:S(2)}) collective-permute-start(bf16[2,48,128]{2,1,0:T(8,128)(2,1)S(1)} %get-tuple-element.56), channel_id=1, source_target_pairs={{0,0},{1,1},{2,2},{3,3},{8,64},{9,65},{10,66},{11,67},{16,128},{17... | collective-permute-start | bytes 73736 | tf_op jit(solution)/shard_map/ppermute | solution.py:432
  127.7 20.2 %collective-permute-start.19 = (bf16[2,48,128]{2,1,0:T(8,128)(2,1)S(1)}, bf16[2,48,128]{2,1,0:T(8,128)(2,1)S(1)}, u32[]{:S(2)}, u32[]{:S(2)}) collective-permute-start(bf16[2,48,128]{2,1,0:T(8,128)(2,1)S(1)} %get-tuple-element.57), channel_id=1, source_target_pairs={{0,3},{1,0},{2,1},{3,2},{8,67},{9,64},{10,65},{11,66},{16,131},{17... | collective-permute-start | bytes 73736 | tf_op jit(solution)/shard_map/ppermute | solution.py:432
  128.6 19.2 %collective-permute-start.20 = (bf16[2,48,128]{2,1,0:T(8,128)(2,1)S(1)}, bf16[2,48,128]{2,1,0:T(8,128)(2,1)S(1)}, u32[]{:S(2)}, u32[]{:S(2)}) collective-permute-start(bf16[2,48,128]{2,1,0:T(8,128)(2,1)S(1)} %get-tuple-element.58), channel_id=1, source_target_pairs={{0,2},{1,3},{2,0},{3,1},{8,66},{9,67},{10,64},{11,65},{16,130},{17... | collective-permute-start | bytes 73736 | tf_op jit(solution)/shard_map/ppermute | solution.py:432
  135.5 12.4 %collective-permute-start.21 = (bf16[2,48,128]{2,1,0:T(8,128)(2,1)S(1)}, bf16[2,48,128]{2,1,0:T(8,128)(2,1)S(1)}, u32[]{:S(2)}, u32[]{:S(2)}) collective-permute-start(bf16[2,48,128]{2,1,0:T(8,128)(2,1)S(1)} %get-tuple-element.59), channel_id=1, source_target_pairs={{0,1},{1,2},{2,3},{3,0},{8,65},{9,66},{10,67},{11,64},{16,129},{17... | collective-permute-start | bytes 73736 | tf_op jit(solution)/shard_map/ppermute | solution.py:432
  (15 other events, 31.6 us)

commit v6 on v5

--- a/solution.py
+++ b/solution.py
@@ -257,7 +257,7 @@
     n_x = len(own)
     units = own[0].shape[0]
     blocks, slots, columns = out.shape[:3]
-    wide = 2 * TILE
+    me_e, wide = lax.axis_index("exp"), 2 * TILE
     for j in range(slots // 2):
         total = None
         for k in range(n_x):
@@ -270,7 +270,8 @@
         total = total.astype(BF)
         for i in range(2):
             block = total[:, i * TILE : (i + 1) * TILE]
-            out[:, 2 * j + i] = block.reshape(blocks, columns, TILE)
+            home = lax.rem(me_e + slots - (2 * j + i), slots)
+            out[:, home] = block.reshape(blocks, columns, TILE)
 
 
 def down_part(own, other, hidden, blocks, columns):
@@ -292,48 +293,21 @@
     )(*own, *other, *hidden)
 
 
-def _sum_kernel(parts, *outs):
-    n_z, n_core = parts.shape[:2]
-    for k, out in enumerate(outs):
-        for core in range(n_core):
-            total = parts[0, core, k].astype(F32)
-            for z in range(1, n_z):
-                total = total + parts[z, core, k].astype(F32)
-            out[core] = total.astype(BF)
-
-
-def sum_part(parts):
-    _, n_core, slots, columns, _ = parts.shape
-    vmem = pl.BlockSpec(memory_space=pltpu.VMEM)
-    block = jax.ShapeDtypeStruct((n_core, columns, TILE), BF)
-    return pl.pallas_call(
-        _sum_kernel,
-        in_specs=[vmem],
-        out_specs=[vmem] * slots,
-        out_shape=[block] * slots,
-        compiler_params=pltpu.CompilerParams(vmem_limit_bytes=8 << 20),
-        name="sum_part",
-    )(parts)
-
-
-def _finish_kernel(ids, *refs):
-    *parts, weight, out = refs
-    n_exp, me_e = lax.axis_size("exp"), lax.axis_index("exp")
-    columns = out.shape[0]
+def _finish_kernel(ids, parts, weight, out):
+    n_z, n_core, n_exp, columns, _ = parts.shape
     tiles, half = ids.shape[0], TILE // 2
     low = lax.broadcasted_iota(jnp.int32, (columns, TILE), 1) < half
     for t in range(tiles):
         rank = jnp.int32(0)
         for earlier in range(t):
             rank = rank + (ids[earlier] == ids[t]).astype(jnp.int32)
-        slot = lax.rem(ids[t] + n_exp - me_e, n_exp)
-        halves = []
-        for core in range(2):
-            found = parts[0][core].astype(F32)
-            for k in range(1, n_exp):
-                found = jnp.where(slot == k, parts[k][core].astype(F32), found)
-            halves.append(found)
-        first, second = halves
+        sums = []
+        for core in range(n_core):
+            total = jnp.zeros((columns, TILE), F32)
+            for z in range(n_z):
+                total = total + parts[z, core, ids[t]].astype(F32)
+            sums.append(total.astype(BF).astype(F32))
+        first, second = sums
         zero = jnp.where(low, first, pltpu.roll(second, half, 1))
         one = jnp.where(low, pltpu.roll(first, half, 1), second)
         rows = jnp.where(rank == 0, zero, one)
@@ -342,16 +316,16 @@
 
 
 def finish_part(ids, parts, weight):
-    columns = parts[0].shape[1]
+    columns = parts.shape[3]
     vmem = pl.BlockSpec(memory_space=pltpu.VMEM)
     return pl.pallas_call(
         _finish_kernel,
-        in_specs=[pl.BlockSpec(memory_space=pltpu.SMEM)] + [vmem] * (len(parts) + 1),
+        in_specs=[pl.BlockSpec(memory_space=pltpu.SMEM), vmem, vmem],
         out_specs=vmem,
         out_shape=jax.ShapeDtypeStruct((columns, weight.shape[1]), BF),
-        compiler_params=pltpu.CompilerParams(vmem_limit_bytes=6 << 20),
+        compiler_params=pltpu.CompilerParams(vmem_limit_bytes=8 << 20),
         name="finish_part",
-    )(ids, *parts, weight)
+    )(ids, parts, weight)
 
 
 def shift(array, axis, by):
@@ -379,58 +353,62 @@
     units = gate_own.shape[0]
 
     picked = pick_tiles(ids, moe_rows, n_exp)
+    *picked, keys_late = lax.optimization_barrier((*picked, keys))
     arrived = [picked[-1]]
     arrived += [shift(picked[k - 1], "exp", k) for k in range(1, n_exp)]
-    gate_other, up_other, w_down, keys_late = lax.optimization_barrier(
-        (gate_other, up_other, w_down, keys)
+    gate_other, up_other, keys_late = lax.optimization_barrier(
+        (gate_other, up_other, keys_late)
     )
 
     states = local_states(decay_rate, keys_late, values)
+    states, w_down = lax.optimization_barrier((states, w_down))
     pieces = states.reshape(n_ctx, width // n_ctx, HEAD)
     pieces = lax.all_to_all(pieces, CTX, 0, 0, tiled=True)
     pieces = scan_states(float(tokens), decay_rate, pieces)
+    split = w_down[0].reshape(units, n_z, n_x, n_core * columns)
+    split = jnp.transpose(split, (2, 0, 1, 3)).reshape(n_x, units, chunk)
+    me_x = lax.axis_index("x")
+    chunks = [
+        lax.dynamic_index_in_dim(split, lax.rem(me_x + k, n_x), 0, keepdims=False)
+        for k in range(n_x)
+    ]
+    down_own, down_other = [chunks[0]] + [None] * (n_x - 1), [None] * n_x
+    lanes = (
+        (("x", 1), ("x", 3), ("core", 1), ("core", 3)),
+        (("x", 2), ("core", 0), ("core", 2)),
+    )
+    for lane in lanes:
+        last = None
+        for axis, k in lane:
+            part = chunks[k] if axis == "x" else down_own[k]
+            if last is not None and last is not part:
+                part, last = lax.optimization_barrier((part, last))
+            last = shift(part, axis, k if axis == "x" else 1)
+            if axis == "x":
+                down_own[k] = last
+            else:
+                down_other[k] = last
     arrived[LAST], pieces = lax.optimization_barrier((arrived[LAST], pieces))
-    prefix = lax.all_to_all(pieces, CTX, 0, 0, tiled=True).reshape(width, HEAD)
-    intra = intra_part(decay_rate, queries, keys, values)
-
-    me_x = lax.axis_index("x")
-    down_own, down_other = [], []
-    for k in range(n_x):
-        start = lax.rem(me_x + k, n_x) * chunk
-        part = lax.dynamic_slice(w_down[0], (0, start), (units, chunk))
-        part = shift(part, "x", k) if k else part
-        down_own.append(part)
-        down_other.append(shift(part, "core", 1))
-    arrived[LAST], intra, *down_other = lax.optimization_barrier(
-        (arrived[LAST], intra, *down_other)
-    )
 
     weights = (gate_own, gate_other, up_own, up_other)
     hidden = hidden_part(arrived, weights)
+    hidden, queries = lax.optimization_barrier((hidden, queries))
     hidden = [hidden] + [shift(hidden, "x", k) for k in range(1, n_x)]
+    intra = intra_part(decay_rate, queries, keys, values)
+    hidden[1], intra = lax.optimization_barrier((hidden[1], intra))
+    prefix = lax.all_to_all(pieces, CTX, 0, 0, tiled=True).reshape(width, HEAD)
     parts = down_part(down_own, down_other, hidden, n_z * n_core, columns)
     parts, prefix = lax.optimization_barrier((parts, prefix))
-    parts = lax.all_to_all(parts, ("z", "core"), 0, 0, tiled=True)
+    parts = parts.reshape(-1, columns, TILE)
+    parts = lax.all_to_all(parts, ("z", "core", "exp"), 0, 0, tiled=True)
+    parts = parts.reshape(n_z, n_core, n_exp, columns, TILE)
 
     mixed, squares = mix_part(decay_rate, intra, queries, prefix)
-    squares = [squares] + [shift(squares, "exp", k) for k in range(1, n_exp)]
-    parts, *squares = lax.optimization_barrier((parts, *squares))
+    squares = [lax.psum(squares, "exp")]
     attention_out = norm_part(
         float(width * n_exp), squares, mixed, norm_gain[None, :], gates
     )
-
-    parts = sum_part(parts.reshape(n_z, n_core, n_exp, columns, TILE))
-    homes = []
-    for k in range(n_exp):
-        pairs = []
-        for z in range(n_z):
-            for x in range(n_x):
-                chip = x * n_z + z
-                for e in range(n_exp):
-                    home = chip * n_exp + (e + n_exp - k) % n_exp
-                    pairs.append(((z * n_x + x) * n_exp + e, home))
-        homes.append(lax.ppermute(parts[k], ("z", "x", "exp"), pairs))
-    moe_out = jnp.swapaxes(finish_part(ids, homes, row_weight[None, :]), 0, 1)
+    moe_out = jnp.swapaxes(finish_part(ids, parts, row_weight[None, :]), 0, 1)
     return attention_out, moe_out
 
 

time: 150 us -> 129 us (0.86)
  starting transfers between devices: 88.4 us -> 44.3 us
  local copies, waits for them, and re-layouts: 10.4 us -> 24.4 us
  blocking collectives: 0 us -> 10.6 us
  waiting for transfers between devices: 26.7 us -> 25.1 us
    ppermute x18 -> x15, starting transfers between devices: 38.4 us -> 14.4 us  [shift(): return lax.ppermute(array, axis, [(i, (i + by) % n) for i in range(n)])]
    ppermute x4 -> x0, starting transfers between devices: 23 us -> none  [on_device(): homes.append(lax.ppermute(parts[k], ('z', 'x', 'exp'), pairs))]
    psum x0 -> x1, blocking collectives: none -> 10.6 us  [on_device(): squares = [lax.psum(squares, 'exp')]]
    unnamed x44 -> x40, local copies, waits for them, and re-layouts: 9.06 us -> 13.3 us
    another operation x0 -> x1, local copies, waits for them, and re-layouts: none -> 3.66 us  [on_device(): split = w_down[0].reshape(units, n_z, n_x, n_core * columns)]
    reshape x0 -> x1, local copies, waits for them, and re-layouts: none -> 2.88 us  [on_device(): split = jnp.transpose(split, (2, 0, 1, 3)).reshape(n_x, units, chunk)]
    transpose x0 -> x1, local copies, waits for them, and re-layouts: none -> 2.46 us  [on_device(): split = jnp.transpose(split, (2, 0, 1, 3)).reshape(n_x, units, chunk)]
    ppermute x18 -> x15, waiting for transfers between devices: 19.5 us -> 17.1 us  [shift(): return lax.ppermute(array, axis, [(i, (i + by) % n) for i in range(n)])]
  transfers between devices with their start and end apart: 25 -> 18, of which waited for: 6 -> 5; matrix products, arithmetic and copies ran while one was open for 1% -> 9% of each run, Pallas kernels for 14% -> 16%
where the time goes in v6:
time: 129 us; the launch traced here: 127 us
  starting transfers between devices  44.3 us (34%)
  waiting for transfers between devices  25.1 us (19%)
  local copies, waits for them, and re-layouts  24.4 us (19%)
  Pallas kernels  22.1 us (17%)
  blocking collectives  10.6 us (8%)
    ppermute x15, waiting for transfers between devices, shift(): return lax.ppermute(array, axis, [(i, (i + by) % n) for i in range(n)])  17.1 us
    ppermute x15, starting transfers between devices, shift(): return lax.ppermute(array, axis, [(i, (i + by) % n) for i in range(n)])  14.4 us
    unnamed x40, local copies, waits for them, and re-layouts  13.3 us
    all_to_all x1, starting transfers between devices, on_device(): pieces = lax.all_to_all(pieces, CTX, 0, 0, tiled=True)  12 us
    psum x1, blocking collectives, on_device(): squares = [lax.psum(squares, 'exp')]  10.6 us
    all_to_all x1, starting transfers between devices, on_device(): prefix = lax.all_to_all(pieces, CTX, 0, 0, tiled=True).reshape(width, HEAD)  10 us
    all_to_all x1, starting transfers between devices, on_device(): parts = lax.all_to_all(parts, ('z', 'core', 'exp'), 0, 0, tiled=True)  7.98 us
    all_to_all x1, waiting for transfers between devices, on_device(): parts = lax.all_to_all(parts, ('z', 'core', 'exp'), 0, 0, tiled=True)  7.95 us
  transfers between devices with their start and end apart: 18, of which 5 were waited for; matrix products, arithmetic and copies ran while one was open for 9% of the time, Pallas kernels for 16%

profile of v6, /device:TPU:6, one launch (start us, length us, event | category | flops | bytes accessed | tf_op | source)
XLA Modules:
  0.0 127.4 jit_solution(4643604776440659336)
XLA Ops:
  1.2 1.9 %copy-done = bf16[512,3072]{1,0:T(8,128)(2,1)S(1)} copy-done((bf16[512,3072]{1,0:T(8,128)(2,1)S(1)}, bf16[512,3072]{1,0:T(8,128)(2,1)}, u32[]{:S(2)}) %copy-start) | copy-done | bytes 3145752
  3.8 3.6 %pick_tiles.1 = (bf16[128,3072]{1,0:T(8,128)(2,1)}, bf16[128,3072]{1,0:T(8,128)(2,1)}, bf16[128,3072]{1,0:T(8,128)(2,1)}, bf16[128,3072]{1,0:T(8,128)(2,1)S(1)}) custom-call(s32[4]{0:T(128)S(1)} %bitcast.33, bf16[512,3072]{1,0:T(8,128)(2,1)S(1)} %copy-done), custom_call_target="tpu_custom_call" | custom-call | tf_op jit(solution)/shard_map/pick_tiles/pallas_call | solution.py:209
  7.4 1.7 %collective-permute-start = (bf16[128,3072]{1,0:T(8,128)(2,1)}, bf16[128,3072]{1,0:T(8,128)(2,1)S(1)}, u32[]{:S(2)}, u32[]{:S(2)}) collective-permute-start(bf16[128,3072]{1,0:T(8,128)(2,1)} %get-tuple-element.36), channel_id=1, source_target_pairs={{0,1},{1,2},{2,3},{3,0},{4,5},{5,6},{6,7},{7,4},{8,9},{9,10},{10,1... | collective-permute-start | bytes 2359304 | tf_op jit(solution)/shard_map/ppermute | solution.py:333
  9.1 2.9 %collective-permute-start.3 = (bf16[128,3072]{1,0:T(8,128)(2,1)}, bf16[128,3072]{1,0:T(8,128)(2,1)}, u32[]{:S(2)}, u32[]{:S(2)}) collective-permute-start(bf16[128,3072]{1,0:T(8,128)(2,1)} %get-tuple-element.41), channel_id=1, source_target_pairs={{0,2},{1,3},{2,0},{3,1},{4,6},{5,7},{6,4},{7,5},{8,10},{9,11},{10,... | collective-permute-start | bytes 2359304 | tf_op jit(solution)/shard_map/ppermute | solution.py:333
  12.0 1.3 %collective-permute-start.4 = (bf16[128,3072]{1,0:T(8,128)(2,1)}, bf16[128,3072]{1,0:T(8,128)(2,1)}, u32[]{:S(2)}, u32[]{:S(2)}) collective-permute-start(bf16[128,3072]{1,0:T(8,128)(2,1)} %get-tuple-element.42), channel_id=1, source_target_pairs={{0,3},{1,0},{2,1},{3,2},{4,7},{5,4},{6,5},{7,6},{8,11},{9,8},{10,9... | collective-permute-start | bytes 2359304 | tf_op jit(solution)/shard_map/ppermute | solution.py:333
  15.2 1.9 %local_states.1 = bf16[1024,128]{1,0:T(8,128)(2,1)} custom-call(f32[8]{0:T(128)S(1)} %copy-done.15, bf16[256,1024]{1,0:T(8,128)(2,1)S(1)} %copy-done.1, bf16[256,1024]{1,0:T(8,128)(2,1)S(1)} %copy-done.2), custom_call_target="tpu_custom_call" | custom-call | tf_op jit(solution)/shard_map/local_states/pallas_call | solution.py:36
  17.1 12.0 %all-to-all-start = ((bf16[64,16,128]{2,1,0:T(8,128)(2,1)}), bf16[64,16,128]{2,1,0:T(8,128)(2,1)S(1)}, u32[]{:S(2)}, u32[]{:S(2)}) async-start(bf16[64,16,128]{2,1,0:T(8,128)(2,1)} %bitcast.5), calls=%async_computation | async-start | bytes 524288 | tf_op jit(solution)/shard_map/all_to_all | solution.py:366
  29.1 3.7 %reshape_squeeze.3 = bf16[144,8,4,96]{3,2,1,0:T(4,128)(2,1)} reshape(bf16[1,144,3072]{2,1,0:T(8,128)(2,1)} %param.23) | data formatting | bytes 1769472 | tf_op jit(solution)/shard_map/reshape;squeeze | solution.py:368
  32.8 2.5 %copy.14 = bf16[4,144,8,96]{3,2,1,0:T(8,128)(2,1)} copy(bf16[4,144,8,96]{3,0,2,1:T(4,128)(2,1)} %bitcast.35) | data formatting | bytes 1769472 | tf_op jit(solution)/shard_map/transpose | solution.py:369
  35.2 2.9 %reshape.20 = bf16[4,144,768]{2,1,0:T(8,128)(2,1)} reshape(bf16[4,144,8,96]{3,2,1,0:T(8,128)(2,1)} %copy.14) | data formatting | bytes 1769472 | tf_op jit(solution)/shard_map/reshape | solution.py:369
  38.1 2.1 %dynamic-slice_bitcast_fusion = (bf16[144,768]{1,0:T(8,128)(2,1)}, bf16[144,768]{1,0:T(8,128)(2,1)}, bf16[144,768]{1,0:T(8,128)(2,1)S(1)}, bf16[144,768]{1,0:T(8,128)(2,1)S(1)}) fusion(bf16[4,144,768]{2,1,0:T(8,128)(2,1)} %reshape.20, s32[]{:T(128)S(6)} %select_n.16, s32[]{:T(128)S(6)} %select_n.15, s32[]{:T(128)S(6)} %select_n.14, s32[]{:T(128)S(6)} %select_n.13), kind=kLoop, calls=%fused_computation | loop fusion | bytes 1769488 | tf_op jit(solution)/shard_map/jit(dynamic_index_in_dim)/squeeze | solution.py:372
  40.6 2.5 %collective-permute-start.7 = (bf16[144,768]{1,0:T(8,128)(2,1)}, bf16[144,768]{1,0:T(8,128)(2,1)S(1)}, u32[]{:S(2)}, u32[]{:S(2)}) collective-permute-start(bf16[144,768]{1,0:T(8,128)(2,1)} %get-tuple-element.61), channel_id=1, source_target_pairs={{0,16},{8,24},{16,0},{24,8},{1,17},{9,25},{17,1},{25,9},{2,18},{10... | collective-permute-start | bytes 663560 | tf_op jit(solution)/shard_map/ppermute | solution.py:333
  43.1 5.3 %collective-permute-done.6.refs_1_ = bf16[144,768]{1,0:T(8,128)(2,1)S(1)} collective-permute-done((bf16[144,768]{1,0:T(8,128)(2,1)S(1)}, bf16[144,768]{1,0:T(8,128)(2,1)S(1)}, u32[]{:S(2)}, u32[]{:S(2)}) %collective-permute-start.6) | collective-permute-done | bytes 221216 | tf_op jit(solution)/shard_map/ppermute | solution.py:333
  49.3 1.4 %scan_states.1 = bf16[64,16,128]{2,1,0:T(8,128)(2,1)} custom-call(f32[8]{0:T(128)S(1)} %copy-done.15, bf16[64,16,128]{2,1,0:T(8,128)(2,1)S(1)} %all-to-all-done.states), custom_call_target="tpu_custom_call" | custom-call | tf_op jit(solution)/shard_map/scan_states/pallas_call | solution.py:58
  51.6 10.0 %all-to-all-start.1 = ((bf16[64,16,128]{2,1,0:T(8,128)(2,1)}), bf16[64,16,128]{2,1,0:T(8,128)(2,1)S(1)}, u32[]{:S(2)}, u32[]{:S(2)}) async-start(bf16[64,16,128]{2,1,0:T(8,128)(2,1)} %scan_states.1), calls=%async_computation.1 | async-start | bytes 524288 | tf_op jit(solution)/shard_map/all_to_all | solution.py:399
  63.5 1.2 copy-done.7
  64.6 1.2 copy-done.9
  65.8 1.2 copy-done.11
  68.1 5.6 %hidden_part.1.refs_8_ = bf16[288,512]{1,0:T(8,128)(2,1)S(1)} custom-call(bf16[128,3072]{1,0:T(8,128)(2,1)S(1)} %get-tuple-element.35.refs_0_, bf16[128,3072]{1,0:T(8,128)(2,1)S(1)} %copy-done.13, bf16[128,3072]{1,0:T(8,128)(2,1)} %collective-permute-done.3.refs_2_, bf16[128,3072]{1,0:T(8,128)(2,1)} %collective-permute-done.4.refs_3_, ...), custom_call_target="tpu_custom_call" | custom-call | tf_op jit(solution)/shard_map/hidden_part/pallas_call | solution.py:245
  74.2 2.5 %collective-permute-start.13 = (bf16[288,512]{1,0:T(8,128)(2,1)S(1)}, bf16[288,512]{1,0:T(8,128)(2,1)S(1)}, u32[]{:S(2)}, u32[]{:S(2)}) collective-permute-start(bf16[288,512]{1,0:T(8,128)(2,1)S(1)} %hidden_part.1.refs_8_), channel_id=1, source_target_pairs={{0,16},{8,24},{16,0},{24,8},{1,17},{9,25},{17,1},{25,9},{2,18},{10... | collective-permute-start | bytes 884744 | tf_op jit(solution)/shard_map/ppermute | solution.py:333
  77.2 2.0 %intra_part.1.intra = f32[256,1024]{1,0:T(8,128)S(1)} custom-call(f32[8]{0:T(128)S(1)} %copy-done.15, bf16[256,1024]{1,0:T(8,128)(2,1)S(1)} %copy-done.3, bf16[256,1024]{1,0:T(8,128)(2,1)S(1)} %copy-done.1, bf16[256,1024]{1,0:T(8,128)(2,1)S(1)} %copy-done.2), custom_call_target="tpu_custom_call" | custom-call | tf_op jit(solution)/shard_map/intra_part/pallas_call | solution.py:92
  79.2 4.4 %collective-permute-done.5.refs_9_ = bf16[288,512]{1,0:T(8,128)(2,1)S(1)} collective-permute-done((bf16[288,512]{1,0:T(8,128)(2,1)S(1)}, bf16[288,512]{1,0:T(8,128)(2,1)S(1)}, u32[]{:S(2)}, u32[]{:S(2)}) %collective-permute-start.5) | collective-permute-done | bytes 294944 | tf_op jit(solution)/shard_map/ppermute | solution.py:333
  83.6 2.0 %collective-permute-done.13.refs_10_ = bf16[288,512]{1,0:T(8,128)(2,1)S(1)} collective-permute-done((bf16[288,512]{1,0:T(8,128)(2,1)S(1)}, bf16[288,512]{1,0:T(8,128)(2,1)S(1)}, u32[]{:S(2)}, u32[]{:S(2)}) %collective-permute-start.13) | collective-permute-done | bytes 294944 | tf_op jit(solution)/shard_map/ppermute | solution.py:333
  85.6 5.3 %collective-permute-done.14.refs_11_ = bf16[288,512]{1,0:T(8,128)(2,1)S(1)} collective-permute-done((bf16[288,512]{1,0:T(8,128)(2,1)S(1)}, bf16[288,512]{1,0:T(8,128)(2,1)S(1)}, u32[]{:S(2)}, u32[]{:S(2)}) %collective-permute-start.14) | collective-permute-done | bytes 294944 | tf_op jit(solution)/shard_map/ppermute | solution.py:333
  91.0 3.7 %down_part.1 = bf16[16,4,48,128]{3,2,1,0:T(8,128)(2,1)} custom-call(bf16[144,768]{1,0:T(8,128)(2,1)S(1)} %get-tuple-element.50.refs_0_, bf16[144,768]{1,0:T(8,128)(2,1)S(1)} %collective-permute-done.6.refs_1_, bf16[144,768]{1,0:T(8,128)(2,1)S(1)} %collective-permute-done.7.refs_2_, bf16[144,768]{1,0:T(8,128)(2,1)} %collective-permute-done.8.refs_3_, ...), custom_call_target="tpu_custom_call" | custom-call | tf_op jit(solution)/shard_map/down_part/pallas_call | solution.py:286
  94.7 8.0 %all-to-all-start.2 = ((bf16[64,48,128]{2,1,0:T(8,128)(2,1)}), bf16[64,48,128]{2,1,0:T(8,128)(2,1)S(1)}, u32[]{:S(2)}, u32[]{:S(2)}) async-start(bf16[64,48,128]{2,1,0:T(8,128)(2,1)} %bitcast.13), calls=%async_computation.2 | async-start | bytes 1572864 | tf_op jit(solution)/shard_map/all_to_all | solution.py:403
  102.7 1.3 %mix_part.1 = (f32[256,1024]{1,0:T(8,128)S(1)}, f32[1,256]{1,0:T(1,128)S(1)}) custom-call(f32[8]{0:T(128)S(1)} %copy-done.15, f32[256,1024]{1,0:T(8,128)S(1)} %intra_part.1.intra, bf16[256,1024]{1,0:T(8,128)(2,1)S(1)} %copy-done.3, bf16[1024,128]{1,0:T(8,128)(2,1)S(1)} %bitcast.26), custom_call_target="tpu_custom_call" | custom-call | tf_op jit(solution)/shard_map/mix_part/pallas_call | solution.py:126
  105.0 10.6 %psum.7.refs_0_ = f32[1,256]{1,0:T(1,128)S(1)} all-reduce(f32[1,256]{1,0:T(1,128)S(1)} %get-tuple-element.57), channel_id=1, replica_groups=mesh['z'=8,'x'=4,'core'=2,'exp'=4] {'exp'}, use_global_device_ids=true, to_apply=%region_0.1 | all-reduce | flops 256 | bytes 2048 | tf_op jit(solution)/shard_map/psum | solution.py:407
  115.7 1.2 copy-done.5
  116.9 1.2 norm_part.1
  118.1 8.0 %all-to-all-done.2 = bf16[64,48,128]{2,1,0:T(8,128)(2,1)S(1)} async-done(((bf16[64,48,128]{2,1,0:T(8,128)(2,1)}), bf16[64,48,128]{2,1,0:T(8,128)(2,1)S(1)}, u32[]{:S(2)}, u32[]{:S(2)}) %all-to-all-start.2) | async-done | bytes 786464 | tf_op jit(solution)/shard_map/all_to_all | solution.py:403
  126.0 1.3 %finish_part.1 = bf16[48,512]{1,0:T(8,128)(2,1)} custom-call(s32[4]{0:T(128)S(1)} %bitcast.34, bf16[8,2,4,48,128]{4,3,2,1,0:T(8,128)(2,1)S(1)} %bitcast.25, f32[1,512]{1,0:T(1,128)S(1)} %bitcast.32), custom_call_target="tpu_custom_call" | custom-call | tf_op jit(solution)/shard_map/finish_part/pallas_call | solution.py:321
  (58 shorter events, 10.3 us)
Async XLA Ops:
  0.6 12.7 %collective-permute-start.1 = (bf16[144,3072]{1,0:T(8,128)(2,1)}, bf16[144,3072]{1,0:T(8,128)(2,1)S(1)}, u32[]{:S(2)}, u32[]{:S(2)}) collective-permute-start(bf16[144,3072]{1,0:T(8,128)(2,1)} %bitcast.27), channel_id=1, source_target_pairs={{0,4},{4,0},{1,5},{5,1},{2,6},{6,2},{3,7},{7,3},{8,12},{12,8},{9,1... | collective-permute-start | bytes 2654216 | tf_op jit(solution)/shard_map/ppermute | solution.py:333
  0.7 13.5 %collective-permute-start.2 = (bf16[144,3072]{1,0:T(8,128)(2,1)}, bf16[144,3072]{1,0:T(8,128)(2,1)S(1)}, u32[]{:S(2)}, u32[]{:S(2)}) collective-permute-start(bf16[144,3072]{1,0:T(8,128)(2,1)} %bitcast.29), channel_id=1, source_target_pairs={{0,4},{4,0},{1,5},{5,1},{2,6},{6,2},{3,7},{7,3},{8,12},{12,8},{9,1... | collective-permute-start | bytes 2654216 | tf_op jit(solution)/shard_map/ppermute | solution.py:333
  1.2 1.9 %copy-start = (bf16[512,3072]{1,0:T(8,128)(2,1)S(1)}, bf16[512,3072]{1,0:T(8,128)(2,1)}, u32[]{:S(2)}) copy-start(bf16[512,3072]{1,0:T(8,128)(2,1)} %rows.1) | copy-start | bytes 9437188
  3.8 11.4 %copy-start.1 = (bf16[256,1024]{1,0:T(8,128)(2,1)S(1)}, bf16[256,1024]{1,0:T(8,128)(2,1)}, u32[]{:S(2)}) copy-start(bf16[256,1024]{1,0:T(8,128)(2,1)} %k.2) | copy-start | bytes 1572868
  3.8 11.4 %copy-start.2 = (bf16[256,1024]{1,0:T(8,128)(2,1)S(1)}, bf16[256,1024]{1,0:T(8,128)(2,1)}, u32[]{:S(2)}) copy-start(bf16[256,1024]{1,0:T(8,128)(2,1)} %v.3) | copy-start | bytes 1572868
  3.8 11.4 %copy-start.15 = (f32[8]{0:T(128)S(1)}, f32[8]{0:T(128)}, u32[]{:S(2)}) copy-start(f32[8]{0:T(128)} %rate.7) | copy-start | bytes 100
  7.4 43.3 %collective-permute-start = (bf16[128,3072]{1,0:T(8,128)(2,1)}, bf16[128,3072]{1,0:T(8,128)(2,1)S(1)}, u32[]{:S(2)}, u32[]{:S(2)}) collective-permute-start(bf16[128,3072]{1,0:T(8,128)(2,1)} %get-tuple-element.36), channel_id=1, source_target_pairs={{0,1},{1,2},{2,3},{3,0},{4,5},{5,6},{6,7},{7,4},{8,9},{9,10},{10,1... | collective-permute-start | bytes 2359304 | tf_op jit(solution)/shard_map/ppermute | solution.py:333
  9.1 53.2 %collective-permute-start.3 = (bf16[128,3072]{1,0:T(8,128)(2,1)}, bf16[128,3072]{1,0:T(8,128)(2,1)}, u32[]{:S(2)}, u32[]{:S(2)}) collective-permute-start(bf16[128,3072]{1,0:T(8,128)(2,1)} %get-tuple-element.41), channel_id=1, source_target_pairs={{0,2},{1,3},{2,0},{3,1},{4,6},{5,7},{6,4},{7,5},{8,10},{9,11},{10,... | collective-permute-start | bytes 2359304 | tf_op jit(solution)/shard_map/ppermute | solution.py:333
  12.0 50.3 %collective-permute-start.4 = (bf16[128,3072]{1,0:T(8,128)(2,1)}, bf16[128,3072]{1,0:T(8,128)(2,1)}, u32[]{:S(2)}, u32[]{:S(2)}) collective-permute-start(bf16[128,3072]{1,0:T(8,128)(2,1)} %get-tuple-element.42), channel_id=1, source_target_pairs={{0,3},{1,0},{2,1},{3,2},{4,7},{5,4},{6,5},{7,6},{8,11},{9,8},{10,9... | collective-permute-start | bytes 2359304 | tf_op jit(solution)/shard_map/ppermute | solution.py:333
  17.1 32.2 %all-to-all-start = ((bf16[64,16,128]{2,1,0:T(8,128)(2,1)}), bf16[64,16,128]{2,1,0:T(8,128)(2,1)S(1)}, u32[]{:S(2)}, u32[]{:S(2)}) async-start(bf16[64,16,128]{2,1,0:T(8,128)(2,1)} %bitcast.5), calls=%async_computation | async-start | bytes 524288 | tf_op jit(solution)/shard_map/all_to_all | solution.py:366
  40.2 8.3 %collective-permute-start.6 = (bf16[144,768]{1,0:T(8,128)(2,1)S(1)}, bf16[144,768]{1,0:T(8,128)(2,1)S(1)}, u32[]{:S(2)}, u32[]{:S(2)}) collective-permute-start(bf16[144,768]{1,0:T(8,128)(2,1)S(1)} %get-tuple-element.62), channel_id=1, source_target_pairs={{0,8},{8,16},{16,24},{24,0},{1,9},{9,17},{17,25},{25,1},{2,10},{10... | collective-permute-start | bytes 663560 | tf_op jit(solution)/shard_map/ppermute | solution.py:333
  40.6 21.0 %collective-permute-start.7 = (bf16[144,768]{1,0:T(8,128)(2,1)}, bf16[144,768]{1,0:T(8,128)(2,1)S(1)}, u32[]{:S(2)}, u32[]{:S(2)}) collective-permute-start(bf16[144,768]{1,0:T(8,128)(2,1)} %get-tuple-element.61), channel_id=1, source_target_pairs={{0,16},{8,24},{16,0},{24,8},{1,17},{9,25},{17,1},{25,9},{2,18},{10... | collective-permute-start | bytes 663560 | tf_op jit(solution)/shard_map/ppermute | solution.py:333
  48.5 13.4 %collective-permute-start.8 = (bf16[144,768]{1,0:T(8,128)(2,1)}, bf16[144,768]{1,0:T(8,128)(2,1)}, u32[]{:S(2)}, u32[]{:S(2)}) collective-permute-start(bf16[144,768]{1,0:T(8,128)(2,1)} %get-tuple-element.49), channel_id=1, source_target_pairs={{0,24},{8,0},{16,8},{24,16},{1,25},{9,1},{17,9},{25,17},{2,26},{10... | collective-permute-start | bytes 663560 | tf_op jit(solution)/shard_map/ppermute | solution.py:333
  51.6 43.0 %all-to-all-start.1 = ((bf16[64,16,128]{2,1,0:T(8,128)(2,1)}), bf16[64,16,128]{2,1,0:T(8,128)(2,1)S(1)}, u32[]{:S(2)}, u32[]{:S(2)}) async-start(bf16[64,16,128]{2,1,0:T(8,128)(2,1)} %scan_states.1), calls=%async_computation.1 | async-start | bytes 524288 | tf_op jit(solution)/shard_map/all_to_all | solution.py:399
  61.7 15.5 %copy-start.3 = (bf16[256,1024]{1,0:T(8,128)(2,1)S(1)}, bf16[256,1024]{1,0:T(8,128)(2,1)}, u32[]{:S(2)}) copy-start(bf16[256,1024]{1,0:T(8,128)(2,1)} %q.1) | copy-start | bytes 1572868
  61.7 15.0 %collective-permute-start.9 = (bf16[144,768]{1,0:T(8,128)(2,1)S(1)}, bf16[144,768]{1,0:T(8,128)(2,1)S(1)}, u32[]{:S(2)}, u32[]{:S(2)}) collective-permute-start(bf16[144,768]{1,0:T(8,128)(2,1)S(1)} %get-tuple-element.50.refs_0_), channel_id=1, source_target_pairs={{0,4},{4,0},{1,5},{5,1},{2,6},{6,2},{3,7},{7,3},{8,12},{12,8},{9,1... | collective-permute-start | bytes 663560 | tf_op jit(solution)/shard_map/ppermute | solution.py:333
  61.9 14.8 %collective-permute-start.10 = (bf16[144,768]{1,0:T(8,128)(2,1)S(1)}, bf16[144,768]{1,0:T(8,128)(2,1)S(1)}, u32[]{:S(2)}, u32[]{:S(2)}) collective-permute-start(bf16[144,768]{1,0:T(8,128)(2,1)S(1)} %collective-permute-done.6.refs_1_), channel_id=1, source_target_pairs={{0,4},{4,0},{1,5},{5,1},{2,6},{6,2},{3,7},{7,3},{8,12},{12,8},{9,1... | collective-permute-start | bytes 663560 | tf_op jit(solution)/shard_map/ppermute | solution.py:333
  62.3 1.2 copy-start.6
  63.5 1.2 copy-start.7
  64.6 1.2 copy-start.9
  65.8 1.2 copy-start.11
  73.7 9.9 %collective-permute-start.5 = (bf16[288,512]{1,0:T(8,128)(2,1)S(1)}, bf16[288,512]{1,0:T(8,128)(2,1)S(1)}, u32[]{:S(2)}, u32[]{:S(2)}) collective-permute-start(bf16[288,512]{1,0:T(8,128)(2,1)S(1)} %hidden_part.1.refs_8_), channel_id=1, source_target_pairs={{0,8},{8,16},{16,24},{24,0},{1,9},{9,17},{17,25},{25,1},{2,10},{10... | collective-permute-start | bytes 884744 | tf_op jit(solution)/shard_map/ppermute | solution.py:333
  74.2 11.4 %collective-permute-start.13 = (bf16[288,512]{1,0:T(8,128)(2,1)S(1)}, bf16[288,512]{1,0:T(8,128)(2,1)S(1)}, u32[]{:S(2)}, u32[]{:S(2)}) collective-permute-start(bf16[288,512]{1,0:T(8,128)(2,1)S(1)} %hidden_part.1.refs_8_), channel_id=1, source_target_pairs={{0,16},{8,24},{16,0},{24,8},{1,17},{9,25},{17,1},{25,9},{2,18},{10... | collective-permute-start | bytes 884744 | tf_op jit(solution)/shard_map/ppermute | solution.py:333
  76.7 14.3 %collective-permute-start.14 = (bf16[288,512]{1,0:T(8,128)(2,1)S(1)}, bf16[288,512]{1,0:T(8,128)(2,1)S(1)}, u32[]{:S(2)}, u32[]{:S(2)}) collective-permute-start(bf16[288,512]{1,0:T(8,128)(2,1)S(1)} %hidden_part.1.refs_8_), channel_id=1, source_target_pairs={{0,24},{8,0},{16,8},{24,16},{1,25},{9,1},{17,9},{25,17},{2,26},{10... | collective-permute-start | bytes 884744 | tf_op jit(solution)/shard_map/ppermute | solution.py:333
  76.7 6.9 %collective-permute-start.11 = (bf16[144,768]{1,0:T(8,128)(2,1)S(1)}, bf16[144,768]{1,0:T(8,128)(2,1)S(1)}, u32[]{:S(2)}, u32[]{:S(2)}) collective-permute-start(bf16[144,768]{1,0:T(8,128)(2,1)S(1)} %collective-permute-done.7.refs_2_), channel_id=1, source_target_pairs={{0,4},{4,0},{1,5},{5,1},{2,6},{6,2},{3,7},{7,3},{8,12},{12,8},{9,1... | collective-permute-start | bytes 663560 | tf_op jit(solution)/shard_map/ppermute | solution.py:333
  76.7 14.3 %collective-permute-start.12 = (bf16[144,768]{1,0:T(8,128)(2,1)}, bf16[144,768]{1,0:T(8,128)(2,1)S(1)}, u32[]{:S(2)}, u32[]{:S(2)}) collective-permute-start(bf16[144,768]{1,0:T(8,128)(2,1)} %collective-permute-done.8.refs_3_), channel_id=1, source_target_pairs={{0,4},{4,0},{1,5},{5,1},{2,6},{6,2},{3,7},{7,3},{8,12},{12,8},{9,1... | collective-permute-start | bytes 663560 | tf_op jit(solution)/shard_map/ppermute | solution.py:333
  94.7 31.4 %all-to-all-start.2 = ((bf16[64,48,128]{2,1,0:T(8,128)(2,1)}), bf16[64,48,128]{2,1,0:T(8,128)(2,1)S(1)}, u32[]{:S(2)}, u32[]{:S(2)}) async-start(bf16[64,48,128]{2,1,0:T(8,128)(2,1)} %bitcast.13), calls=%async_computation.2 | async-start | bytes 1572864 | tf_op jit(solution)/shard_map/all_to_all | solution.py:403
  102.6 13.0 %copy-start.14 = (bf16[256,1024]{1,0:T(8,128)(2,1)S(1)}, bf16[256,1024]{1,0:T(8,128)(2,1)}, u32[]{:S(2)}) copy-start(bf16[256,1024]{1,0:T(8,128)(2,1)} %refs_3_.1) | copy-start | bytes 1572868
  102.7 13.0 %copy-start.16 = (f32[1024]{0:T(1024)S(1)}, f32[1024]{0:T(1024)}, u32[]{:S(2)}) copy-start(f32[1024]{0:T(1024)} %param.17) | copy-start | bytes 12292
  105.0 21.0 %copy-start.17 = (f32[512]{0:T(512)S(1)}, f32[512]{0:T(512)}, u32[]{:S(2)}) copy-start(f32[512]{0:T(512)} %param.20) | copy-start | bytes 6148
  105.0 21.0 %copy-start.19 = (s32[4,1]{0,1:T(1,128)S(1)}, s32[4,1]{0,1:T(1,128)}, u32[]{:S(2)}) copy-start(s32[4,1]{0,1:T(1,128)} %param.19) | copy-start | bytes 52
  115.7 1.2 copy-start.5
  (6 other events, 5.5 us)

commit v7 on v6

--- a/solution.py
+++ b/solution.py
@@ -219,38 +219,91 @@
             pltpu.SemaphoreType.DMA((count, 2)),
             pltpu.SemaphoreType.DMA((count,)),
         ],
-        compiler_params=pltpu.CompilerParams(vmem_limit_bytes=8 << 20),
+        compiler_params=pltpu.CompilerParams(vmem_limit_bytes=58 << 20),
         name="pick_tiles",
     )(ids, rows)
 
 
 def _hidden_kernel(count, *refs):
-    rows, weights = refs[:count], refs[count : count + 4]
-    held, out = refs[-1], refs[-2]
-    gate_own, gate_other, up_own, up_other = weights
-    units = gate_own.shape[0]
-    for i in range(count):
-        held[i * TILE : (i + 1) * TILE, :] = rows[i][...]
-    x = held[...]
-    for i, (gate, up) in enumerate(((gate_own, up_own), (gate_other, up_other))):
-        dims = (((1,), (1,)), ((), ()))
-        g = lax.dot_general(gate[...], x, dims, preferred_element_type=F32)
-        u = lax.dot_general(up[...], x, dims, preferred_element_type=F32)
-        out[i * units : (i + 1) * units, :] = (jax.nn.silu(g) * u).astype(BF)
+    sources, out = refs[: count + 4], refs[count + 4]
+    rows, weights, sems = refs[count + 5 :]
+    units = weights.shape[1]
+    targets = [rows.at[i * TILE : (i + 1) * TILE, :] for i in range(count)]
+    targets += [weights.at[i] for i in range(4)]
+    copies = [
+        pltpu.make_async_copy(source, target, sems.at[i])
+        for i, (source, target) in enumerate(zip(sources, targets))
+    ]
+    first = [count, count + 2, 0, 1, count + 1, count + 3]
+    order = first + [i for i in range(count + 4) if i not in first]
+    for i in order:
+        copies[i].start()
+    dims = (((1,), (1,)), ((), ()))
+    wide = 2 * TILE
+    for j in range(count // 2):
+        ready = [2 * j, 2 * j + 1] if j else []
+        for i in ready:
+            copies[i].wait()
+        for i in range(2):
+            if j == 0:
+                for n in first[:4] if i == 0 else first[4:]:
+                    copies[n].wait()
+            x = rows[j * wide : (j + 1) * wide, :]
+            g = lax.dot_general(weights[i], x, dims, preferred_element_type=F32)
+            u = lax.dot_general(weights[2 + i], x, dims, preferred_element_type=F32)
+            out[i * units : (i + 1) * units, j * wide : (j + 1) * wide] = (
+                jax.nn.silu(g) * u
+            ).astype(BF)
 
 
 def hidden_part(rows, weights):
-    count, units, model = len(rows), weights[0].shape[0], weights[0].shape[1]
-    vmem = pl.BlockSpec(memory_space=pltpu.VMEM)
+    count, (units, model) = len(rows), weights[0].shape
     return pl.pallas_call(
         functools.partial(_hidden_kernel, count),
-        in_specs=[vmem] * (count + 4),
-        out_specs=vmem,
+        in_specs=[pl.BlockSpec(memory_space=pl.ANY)] * (count + 4),
+        out_specs=pl.BlockSpec(memory_space=pltpu.VMEM),
         out_shape=jax.ShapeDtypeStruct((2 * units, count * TILE), BF),
-        scratch_shapes=[pltpu.VMEM((count * TILE, model), BF)],
-        compiler_params=pltpu.CompilerParams(vmem_limit_bytes=24 << 20),
+        scratch_shapes=[
+            pltpu.VMEM((count * TILE, model), BF),
+            pltpu.VMEM((4, units, model), BF),
+            pltpu.SemaphoreType.DMA((count + 4,)),
+        ],
+        compiler_params=pltpu.CompilerParams(vmem_limit_bytes=58 << 20),
         name="hidden_part",
     )(*rows, *weights)
+
+
+def _split_kernel(n_z, weight, *outs):
+    me_x, n_x = lax.axis_index("x"), len(outs)
+    units, window = weight.shape[0], weight.shape[1] // n_z
+    own = window // n_x
+    lane = lax.broadcasted_iota(jnp.int32, (units, window), 1)
+    for g in range(n_z // n_x):
+        parts = [
+            weight[:, z * window : (z + 1) * window].astype(F32)
+            for z in range(g * n_x, (g + 1) * n_x)
+        ]
+        for k, out in enumerate(outs):
+            target = lax.rem(me_x + k, n_x)
+            total = jnp.zeros((units, window), F32)
+            for i, part in enumerate(parts):
+                turn = lax.rem(i + n_x - target, n_x) * own
+                here = (lane >= i * own) & (lane < (i + 1) * own)
+                total = jnp.where(here, pltpu.roll(part, turn, 1), total)
+            out[:, g * window : (g + 1) * window] = total.astype(BF)
+
+
+def split_columns(weight, n_z, n_x):
+    units, model = weight.shape
+    vmem = pl.BlockSpec(memory_space=pltpu.VMEM)
+    return pl.pallas_call(
+        functools.partial(_split_kernel, n_z),
+        in_specs=[vmem],
+        out_specs=[vmem] * n_x,
+        out_shape=[jax.ShapeDtypeStruct((units, model // n_x), BF)] * n_x,
+        compiler_params=pltpu.CompilerParams(vmem_limit_bytes=14 << 20),
+        name="split_columns",
+    )(weight)
 
 
 def _down_kernel(own, other, hidden, out):
@@ -344,7 +397,6 @@
     model = moe_rows.shape[1]
     ids = tile_expert[:, 0]
     columns = model // n_ctx
-    chunk = model // n_x
 
     gate_own = jnp.swapaxes(w_gate[0], 0, 1)
     up_own = jnp.swapaxes(w_up[0], 0, 1)
@@ -365,13 +417,7 @@
     pieces = states.reshape(n_ctx, width // n_ctx, HEAD)
     pieces = lax.all_to_all(pieces, CTX, 0, 0, tiled=True)
     pieces = scan_states(float(tokens), decay_rate, pieces)
-    split = w_down[0].reshape(units, n_z, n_x, n_core * columns)
-    split = jnp.transpose(split, (2, 0, 1, 3)).reshape(n_x, units, chunk)
-    me_x = lax.axis_index("x")
-    chunks = [
-        lax.dynamic_index_in_dim(split, lax.rem(me_x + k, n_x), 0, keepdims=False)
-        for k in range(n_x)
-    ]
+    chunks = split_columns(w_down[0], n_z, n_x)
     down_own, down_other = [chunks[0]] + [None] * (n_x - 1), [None] * n_x
     lanes = (
         (("x", 1), ("x", 3), ("core", 1), ("core", 3)),

time: 129 us -> 123 us (0.953)
  local copies, waits for them, and re-layouts: 24.4 us -> 5.06 us
  starting transfers between devices: 44.3 us -> 52.6 us
  Pallas kernels: 22.1 us -> 26.1 us
  waiting for transfers between devices: 25.1 us -> 26.6 us
    unnamed x40 -> x34, local copies, waits for them, and re-layouts: 13.3 us -> 5.06 us
    all_to_all x1, starting transfers between devices: 7.98 us -> 15 us  [on_device(): parts = lax.all_to_all(parts, ('z', 'core', 'exp'), 0, 0, tiled=True)]
    another operation x1 -> x0, local copies, waits for them, and re-layouts: 3.66 us -> none  [on_device(): split = w_down[0].reshape(units, n_z, n_x, n_core * columns)]
    pallas_call x1 -> x2, Pallas kernels: 5.58 us -> 8.59 us  [the longest x1 7.26 us: hidden_part(): pl.pallas_call(functools.partial(_hidden_kernel, count), in_specs=[pl.Blo...]
    reshape x1 -> x0, local copies, waits for them, and re-layouts: 2.88 us -> none  [on_device(): split = jnp.transpose(split, (2, 0, 1, 3)).reshape(n_x, units, chunk)]
    transpose x1 -> x0, local copies, waits for them, and re-layouts: 2.46 us -> none  [on_device(): split = jnp.transpose(split, (2, 0, 1, 3)).reshape(n_x, units, chunk)]
    squeeze x1 -> x0, local copies, waits for them, and re-layouts: 2.09 us -> none  [on_device(): lax.dynamic_index_in_dim(split, lax.rem(me_x + k, n_x), 0, keepdims=False)]
    ppermute x15, waiting for transfers between devices: 17.1 us -> 18.5 us  [shift(): return lax.ppermute(array, axis, [(i, (i + by) % n) for i in range(n)])]
  transfers between devices with their start and end apart: 18 -> 18, of which waited for: 5 -> 4; matrix products, arithmetic and copies ran while one was open for 9% -> 0% of each run, Pallas kernels for 16% -> 20%
where the time goes in v7:
time: 123 us; the launch traced here: 122 us
  starting transfers between devices  52.6 us (43%)
  waiting for transfers between devices  26.6 us (22%)
  Pallas kernels  26.1 us (21%)
  blocking collectives  10.5 us (9%)
  local copies, waits for them, and re-layouts  5.06 us (4%)
    ppermute x15, waiting for transfers between devices, shift(): return lax.ppermute(array, axis, [(i, (i + by) % n) for i in range(n)])  18.5 us
    all_to_all x1, starting transfers between devices, on_device(): parts = lax.all_to_all(parts, ('z', 'core', 'exp'), 0, 0, tiled=True)  15 us
    ppermute x15, starting transfers between devices, shift(): return lax.ppermute(array, axis, [(i, (i + by) % n) for i in range(n)])  14.8 us
    all_to_all x1, starting transfers between devices, on_device(): pieces = lax.all_to_all(pieces, CTX, 0, 0, tiled=True)  12 us
    all_to_all x1, starting transfers between devices, on_device(): prefix = lax.all_to_all(pieces, CTX, 0, 0, tiled=True).reshape(width, HEAD)  10.9 us
    psum x1, blocking collectives, on_device(): squares = [lax.psum(squares, 'exp')]  10.5 us
    all_to_all x1, waiting for transfers between devices, on_device(): parts = lax.all_to_all(parts, ('z', 'core', 'exp'), 0, 0, tiled=True)  8.14 us
    pallas_call x1, Pallas kernels, hidden_part(): pl.pallas_call(functools.partial(_hidden_kernel, count), in_specs=[pl.Blo...  7.26 us
  transfers between devices with their start and end apart: 18, of which 4 were waited for; matrix products, arithmetic and copies ran while one was open for 0% of the time, Pallas kernels for 20%

profile of v7, /device:TPU:6, one launch (start us, length us, event | category | flops | bytes accessed | tf_op | source)
XLA Modules:
  0.0 121.7 jit_solution(8249071673638326817)
XLA Ops:
  1.3 4.4 %pick_tiles.1 = (bf16[128,3072]{1,0:T(8,128)(2,1)}, bf16[128,3072]{1,0:T(8,128)(2,1)}, bf16[128,3072]{1,0:T(8,128)(2,1)}, bf16[128,3072]{1,0:T(8,128)(2,1)}) custom-call(s32[4]{0:T(128)} %bitcast.20, bf16[512,3072]{1,0:T(8,128)(2,1)} %rows.1), custom_call_target="tpu_custom_call" | custom-call | tf_op jit(solution)/shard_map/pick_tiles/pallas_call | solution.py:209
  5.7 1.6 %collective-permute-start = (bf16[128,3072]{1,0:T(8,128)(2,1)}, bf16[128,3072]{1,0:T(8,128)(2,1)}, u32[]{:S(2)}, u32[]{:S(2)}) collective-permute-start(bf16[128,3072]{1,0:T(8,128)(2,1)} %get-tuple-element.40), channel_id=1, source_target_pairs={{0,1},{1,2},{2,3},{3,0},{4,5},{5,6},{6,7},{7,4},{8,9},{9,10},{10,1... | collective-permute-start | bytes 2359304 | tf_op jit(solution)/shard_map/ppermute | solution.py:386
  7.4 2.9 %collective-permute-start.3 = (bf16[128,3072]{1,0:T(8,128)(2,1)}, bf16[128,3072]{1,0:T(8,128)(2,1)}, u32[]{:S(2)}, u32[]{:S(2)}) collective-permute-start(bf16[128,3072]{1,0:T(8,128)(2,1)} %get-tuple-element.45), channel_id=1, source_target_pairs={{0,2},{1,3},{2,0},{3,1},{4,6},{5,7},{6,4},{7,5},{8,10},{9,11},{10,... | collective-permute-start | bytes 2359304 | tf_op jit(solution)/shard_map/ppermute | solution.py:386
  10.3 1.4 %collective-permute-start.4 = (bf16[128,3072]{1,0:T(8,128)(2,1)}, bf16[128,3072]{1,0:T(8,128)(2,1)}, u32[]{:S(2)}, u32[]{:S(2)}) collective-permute-start(bf16[128,3072]{1,0:T(8,128)(2,1)} %get-tuple-element.46), channel_id=1, source_target_pairs={{0,3},{1,0},{2,1},{3,2},{4,7},{5,4},{6,5},{7,6},{8,11},{9,8},{10,9... | collective-permute-start | bytes 2359304 | tf_op jit(solution)/shard_map/ppermute | solution.py:386
  11.7 1.9 %local_states.1 = bf16[1024,128]{1,0:T(8,128)(2,1)} custom-call(f32[8]{0:T(128)S(1)} %copy-done.12, bf16[256,1024]{1,0:T(8,128)(2,1)S(1)} %copy-done, bf16[256,1024]{1,0:T(8,128)(2,1)S(1)} %copy-done.1), custom_call_target="tpu_custom_call" | custom-call | tf_op jit(solution)/shard_map/local_states/pallas_call | solution.py:36
  13.6 12.0 %all-to-all-start = ((bf16[64,16,128]{2,1,0:T(8,128)(2,1)}), bf16[64,16,128]{2,1,0:T(8,128)(2,1)S(1)}, u32[]{:S(2)}, u32[]{:S(2)}) async-start(bf16[64,16,128]{2,1,0:T(8,128)(2,1)} %bitcast.5), calls=%async_computation | async-start | bytes 524288 | tf_op jit(solution)/shard_map/all_to_all | solution.py:418
  25.6 1.3 %split_columns.1 = (bf16[144,768]{1,0:T(8,128)(2,1)S(1)}, bf16[144,768]{1,0:T(8,128)(2,1)S(1)}, bf16[144,768]{1,0:T(8,128)(2,1)S(1)}, bf16[144,768]{1,0:T(8,128)(2,1)S(1)}) custom-call(bf16[144,3072]{1,0:T(8,128)(2,1)S(1)} %bitcast.17), custom_call_target="tpu_custom_call" | custom-call | tf_op jit(solution)/shard_map/split_columns/pallas_call | solution.py:299
  26.9 0.5 collective-permute-start.6
  27.5 2.5 %collective-permute-start.7 = (bf16[144,768]{1,0:T(8,128)(2,1)S(1)}, bf16[144,768]{1,0:T(8,128)(2,1)}, u32[]{:S(2)}, u32[]{:S(2)}) collective-permute-start(bf16[144,768]{1,0:T(8,128)(2,1)S(1)} %get-tuple-element.55), channel_id=1, source_target_pairs={{0,16},{8,24},{16,0},{24,8},{1,17},{9,25},{17,1},{25,9},{2,18},{10... | collective-permute-start | bytes 663560 | tf_op jit(solution)/shard_map/ppermute | solution.py:386
  29.9 7.3 %collective-permute-done.6.refs_1_ = bf16[144,768]{1,0:T(8,128)(2,1)S(1)} collective-permute-done((bf16[144,768]{1,0:T(8,128)(2,1)S(1)}, bf16[144,768]{1,0:T(8,128)(2,1)S(1)}, u32[]{:S(2)}, u32[]{:S(2)}) %collective-permute-start.6) | collective-permute-done | bytes 221216 | tf_op jit(solution)/shard_map/ppermute | solution.py:386
  37.2 0.6 collective-permute-start.8
  37.8 1.4 %scan_states.1 = bf16[64,16,128]{2,1,0:T(8,128)(2,1)} custom-call(f32[8]{0:T(128)S(1)} %copy-done.12, bf16[64,16,128]{2,1,0:T(8,128)(2,1)S(1)} %all-to-all-done.states), custom_call_target="tpu_custom_call" | custom-call | tf_op jit(solution)/shard_map/scan_states/pallas_call | solution.py:58
  39.2 10.9 %all-to-all-start.1 = ((bf16[64,16,128]{2,1,0:T(8,128)(2,1)}), bf16[64,16,128]{2,1,0:T(8,128)(2,1)S(1)}, u32[]{:S(2)}, u32[]{:S(2)}) async-start(bf16[64,16,128]{2,1,0:T(8,128)(2,1)} %scan_states.1), calls=%async_computation.1 | async-start | bytes 524288 | tf_op jit(solution)/shard_map/all_to_all | solution.py:445
  50.7 7.3 %hidden_part.1.refs_8_ = bf16[288,512]{1,0:T(8,128)(2,1)} custom-call(bf16[128,3072]{1,0:T(8,128)(2,1)} %get-tuple-element.39.refs_0_, bf16[128,3072]{1,0:T(8,128)(2,1)} %collective-permute-done.refs_1_, bf16[128,3072]{1,0:T(8,128)(2,1)} %collective-permute-done.3.refs_2_, bf16[128,3072]{1,0:T(8,128)(2,1)} %collective-permute-done.4.refs_3_, ...), custom_call_target="tpu_custom_call" | custom-call | tf_op jit(solution)/shard_map/hidden_part/pallas_call | solution.py:261
  58.0 0.6 collective-permute-start.5
  58.6 1.5 %collective-permute-start.14 = (bf16[288,512]{1,0:T(8,128)(2,1)}, bf16[288,512]{1,0:T(8,128)(2,1)S(1)}, u32[]{:S(2)}, u32[]{:S(2)}) collective-permute-start(bf16[288,512]{1,0:T(8,128)(2,1)} %hidden_part.1.refs_8_), channel_id=1, source_target_pairs={{0,24},{8,0},{16,8},{24,16},{1,25},{9,1},{17,9},{25,17},{2,26},{10... | collective-permute-start | bytes 884744 | tf_op jit(solution)/shard_map/ppermute | solution.py:386
  60.1 1.5 %collective-permute-start.13 = (bf16[288,512]{1,0:T(8,128)(2,1)}, bf16[288,512]{1,0:T(8,128)(2,1)S(1)}, u32[]{:S(2)}, u32[]{:S(2)}) collective-permute-start(bf16[288,512]{1,0:T(8,128)(2,1)} %hidden_part.1.refs_8_), channel_id=1, source_target_pairs={{0,16},{8,24},{16,0},{24,8},{1,17},{9,25},{17,1},{25,9},{2,18},{10... | collective-permute-start | bytes 884744 | tf_op jit(solution)/shard_map/ppermute | solution.py:386
  62.1 2.0 %intra_part.1.intra = f32[256,1024]{1,0:T(8,128)S(1)} custom-call(f32[8]{0:T(128)S(1)} %copy-done.12, bf16[256,1024]{1,0:T(8,128)(2,1)S(1)} %copy-done.2, bf16[256,1024]{1,0:T(8,128)(2,1)S(1)} %copy-done, bf16[256,1024]{1,0:T(8,128)(2,1)S(1)} %copy-done.1), custom_call_target="tpu_custom_call" | custom-call | tf_op jit(solution)/shard_map/intra_part/pallas_call | solution.py:92
  64.1 4.0 %collective-permute-done.5.refs_9_ = bf16[288,512]{1,0:T(8,128)(2,1)S(1)} collective-permute-done((bf16[288,512]{1,0:T(8,128)(2,1)}, bf16[288,512]{1,0:T(8,128)(2,1)S(1)}, u32[]{:S(2)}, u32[]{:S(2)}) %collective-permute-start.5) | collective-permute-done | bytes 294944 | tf_op jit(solution)/shard_map/ppermute | solution.py:386
  68.1 7.1 %collective-permute-done.14.refs_11_ = bf16[288,512]{1,0:T(8,128)(2,1)S(1)} collective-permute-done((bf16[288,512]{1,0:T(8,128)(2,1)}, bf16[288,512]{1,0:T(8,128)(2,1)S(1)}, u32[]{:S(2)}, u32[]{:S(2)}) %collective-permute-start.14) | collective-permute-done | bytes 294944 | tf_op jit(solution)/shard_map/ppermute | solution.py:386
  75.3 1.0 copy-done.3
  76.3 0.9 copy-done.9
  77.2 0.9 copy-done.11
  78.1 3.8 %down_part.1 = bf16[16,4,48,128]{3,2,1,0:T(8,128)(2,1)} custom-call(bf16[144,768]{1,0:T(8,128)(2,1)S(1)} %copy-done.9, bf16[144,768]{1,0:T(8,128)(2,1)S(1)} %copy-done.11, bf16[144,768]{1,0:T(8,128)(2,1)} %collective-permute-done.7.refs_2_, bf16[144,768]{1,0:T(8,128)(2,1)} %collective-permute-done.8.refs_3_, ...), custom_call_target="tpu_custom_call" | custom-call | tf_op jit(solution)/shard_map/down_part/pallas_call | solution.py:339
  82.0 15.0 %all-to-all-start.2 = ((bf16[64,48,128]{2,1,0:T(8,128)(2,1)}), bf16[64,48,128]{2,1,0:T(8,128)(2,1)S(1)}, u32[]{:S(2)}, u32[]{:S(2)}) async-start(bf16[64,48,128]{2,1,0:T(8,128)(2,1)} %bitcast.9), calls=%async_computation.2 | async-start | bytes 1572864 | tf_op jit(solution)/shard_map/all_to_all | solution.py:449
  97.0 1.3 %mix_part.1 = (f32[256,1024]{1,0:T(8,128)S(1)}, f32[1,256]{1,0:T(1,128)S(1)}) custom-call(f32[8]{0:T(128)S(1)} %copy-done.12, f32[256,1024]{1,0:T(8,128)S(1)} %intra_part.1.intra, bf16[256,1024]{1,0:T(8,128)(2,1)S(1)} %copy-done.2, bf16[1024,128]{1,0:T(8,128)(2,1)S(1)} %bitcast.16), custom_call_target="tpu_custom_call" | custom-call | tf_op jit(solution)/shard_map/mix_part/pallas_call | solution.py:126
  98.4 1.0 copy-done.4
  99.3 10.5 %psum.7.refs_0_ = f32[1,256]{1,0:T(1,128)S(1)} all-reduce(f32[1,256]{1,0:T(1,128)S(1)} %get-tuple-element.65), channel_id=1, replica_groups=mesh['z'=8,'x'=4,'core'=2,'exp'=4] {'exp'}, use_global_device_ids=true, to_apply=%region_0.0 | all-reduce | flops 256 | bytes 2048 | tf_op jit(solution)/shard_map/psum | solution.py:453
  109.8 1.2 %copy-done.5 = f32[256,1024]{1,0:T(8,128)S(1)} copy-done((f32[256,1024]{1,0:T(8,128)S(1)}, f32[256,1024]{1,0:T(8,128)}, u32[]{:S(2)}) %copy-start.5) | copy-done | bytes 1048600
  111.0 1.2 norm_part.1
  112.2 8.1 %all-to-all-done.2 = bf16[64,48,128]{2,1,0:T(8,128)(2,1)S(1)} async-done(((bf16[64,48,128]{2,1,0:T(8,128)(2,1)}), bf16[64,48,128]{2,1,0:T(8,128)(2,1)S(1)}, u32[]{:S(2)}, u32[]{:S(2)}) %all-to-all-start.2) | async-done | bytes 786464 | tf_op jit(solution)/shard_map/all_to_all | solution.py:449
  120.4 1.3 %finish_part.1 = bf16[48,512]{1,0:T(8,128)(2,1)} custom-call(s32[4]{0:T(128)S(1)} %bitcast.21, bf16[8,2,4,48,128]{4,3,2,1,0:T(8,128)(2,1)S(1)} %bitcast.15, f32[1,512]{1,0:T(1,128)S(1)} %bitcast.19), custom_call_target="tpu_custom_call" | custom-call | tf_op jit(solution)/shard_map/finish_part/pallas_call | solution.py:374
  (49 shorter events, 1.8 us)
Async XLA Ops:
  0.6 11.0 %copy-start = (bf16[256,1024]{1,0:T(8,128)(2,1)S(1)}, bf16[256,1024]{1,0:T(8,128)(2,1)}, u32[]{:S(2)}) copy-start(bf16[256,1024]{1,0:T(8,128)(2,1)} %k.2) | copy-start | bytes 1572868
  0.6 11.0 %copy-start.12 = (f32[8]{0:T(128)S(1)}, f32[8]{0:T(128)}, u32[]{:S(2)}) copy-start(f32[8]{0:T(128)} %rate.7) | copy-start | bytes 100
  0.7 11.0 %copy-start.1 = (bf16[256,1024]{1,0:T(8,128)(2,1)S(1)}, bf16[256,1024]{1,0:T(8,128)(2,1)}, u32[]{:S(2)}) copy-start(bf16[256,1024]{1,0:T(8,128)(2,1)} %v.3) | copy-start | bytes 1572868
  0.7 24.9 %copy-start.6 = (bf16[1,144,3072]{2,1,0:T(8,128)(2,1)S(1)}, bf16[1,144,3072]{2,1,0:T(8,128)(2,1)}, u32[]{:S(2)}) copy-start(bf16[1,144,3072]{2,1,0:T(8,128)(2,1)} %param.23) | copy-start | bytes 2654212
  0.7 11.0 %collective-permute-start.1 = (bf16[144,3072]{1,0:T(8,128)(2,1)}, bf16[144,3072]{1,0:T(8,128)(2,1)S(1)}, u32[]{:S(2)}, u32[]{:S(2)}) collective-permute-start(bf16[144,3072]{1,0:T(8,128)(2,1)} %bitcast.22), channel_id=1, source_target_pairs={{0,4},{4,0},{1,5},{5,1},{2,6},{6,2},{3,7},{7,3},{8,12},{12,8},{9,1... | collective-permute-start | bytes 2654216 | tf_op jit(solution)/shard_map/ppermute | solution.py:386
  0.8 10.9 %collective-permute-start.2 = (bf16[144,3072]{1,0:T(8,128)(2,1)}, bf16[144,3072]{1,0:T(8,128)(2,1)}, u32[]{:S(2)}, u32[]{:S(2)}) collective-permute-start(bf16[144,3072]{1,0:T(8,128)(2,1)} %bitcast.24), channel_id=1, source_target_pairs={{0,4},{4,0},{1,5},{5,1},{2,6},{6,2},{3,7},{7,3},{8,12},{12,8},{9,1... | collective-permute-start | bytes 2654216 | tf_op jit(solution)/shard_map/ppermute | solution.py:386
  5.7 33.5 %collective-permute-start = (bf16[128,3072]{1,0:T(8,128)(2,1)}, bf16[128,3072]{1,0:T(8,128)(2,1)}, u32[]{:S(2)}, u32[]{:S(2)}) collective-permute-start(bf16[128,3072]{1,0:T(8,128)(2,1)} %get-tuple-element.40), channel_id=1, source_target_pairs={{0,1},{1,2},{2,3},{3,0},{4,5},{5,6},{6,7},{7,4},{8,9},{9,10},{10,1... | collective-permute-start | bytes 2359304 | tf_op jit(solution)/shard_map/ppermute | solution.py:386
  7.4 43.4 %collective-permute-start.3 = (bf16[128,3072]{1,0:T(8,128)(2,1)}, bf16[128,3072]{1,0:T(8,128)(2,1)}, u32[]{:S(2)}, u32[]{:S(2)}) collective-permute-start(bf16[128,3072]{1,0:T(8,128)(2,1)} %get-tuple-element.45), channel_id=1, source_target_pairs={{0,2},{1,3},{2,0},{3,1},{4,6},{5,7},{6,4},{7,5},{8,10},{9,11},{10,... | collective-permute-start | bytes 2359304 | tf_op jit(solution)/shard_map/ppermute | solution.py:386
  10.3 40.5 %collective-permute-start.4 = (bf16[128,3072]{1,0:T(8,128)(2,1)}, bf16[128,3072]{1,0:T(8,128)(2,1)}, u32[]{:S(2)}, u32[]{:S(2)}) collective-permute-start(bf16[128,3072]{1,0:T(8,128)(2,1)} %get-tuple-element.46), channel_id=1, source_target_pairs={{0,3},{1,0},{2,1},{3,2},{4,7},{5,4},{6,5},{7,6},{8,11},{9,8},{10,9... | collective-permute-start | bytes 2359304 | tf_op jit(solution)/shard_map/ppermute | solution.py:386
  11.6 13.9 %copy-start.16 = (bf16[144,3072]{1,0:T(8,128)(2,1)}, bf16[144,3072]{1,0:T(8,128)(2,1)S(1)}, u32[]{:S(2)}) copy-start(bf16[144,3072]{1,0:T(8,128)(2,1)S(1)} %collective-permute-done.1.refs_5_) | copy-start | bytes 2654212
  13.6 24.2 %all-to-all-start = ((bf16[64,16,128]{2,1,0:T(8,128)(2,1)}), bf16[64,16,128]{2,1,0:T(8,128)(2,1)S(1)}, u32[]{:S(2)}, u32[]{:S(2)}) async-start(bf16[64,16,128]{2,1,0:T(8,128)(2,1)} %bitcast.5), calls=%async_computation | async-start | bytes 524288 | tf_op jit(solution)/shard_map/all_to_all | solution.py:418
  26.9 31.1 %copy-start.8 = (bf16[144,768]{1,0:T(8,128)(2,1)}, bf16[144,768]{1,0:T(8,128)(2,1)S(1)}, u32[]{:S(2)}) copy-start(bf16[144,768]{1,0:T(8,128)(2,1)S(1)} %get-tuple-element.58.refs_0_) | copy-start | bytes 663556
  26.9 10.3 %collective-permute-start.6 = (bf16[144,768]{1,0:T(8,128)(2,1)S(1)}, bf16[144,768]{1,0:T(8,128)(2,1)S(1)}, u32[]{:S(2)}, u32[]{:S(2)}) collective-permute-start(bf16[144,768]{1,0:T(8,128)(2,1)S(1)} %get-tuple-element.54), channel_id=1, source_target_pairs={{0,8},{8,16},{16,24},{24,0},{1,9},{9,17},{17,25},{25,1},{2,10},{10... | collective-permute-start | bytes 663560 | tf_op jit(solution)/shard_map/ppermute | solution.py:386
  27.5 22.7 %collective-permute-start.7 = (bf16[144,768]{1,0:T(8,128)(2,1)S(1)}, bf16[144,768]{1,0:T(8,128)(2,1)}, u32[]{:S(2)}, u32[]{:S(2)}) collective-permute-start(bf16[144,768]{1,0:T(8,128)(2,1)S(1)} %get-tuple-element.55), channel_id=1, source_target_pairs={{0,16},{8,24},{16,0},{24,8},{1,17},{9,25},{17,1},{25,9},{2,18},{10... | collective-permute-start | bytes 663560 | tf_op jit(solution)/shard_map/ppermute | solution.py:386
  37.2 20.8 %copy-start.10 = (bf16[144,768]{1,0:T(8,128)(2,1)}, bf16[144,768]{1,0:T(8,128)(2,1)S(1)}, u32[]{:S(2)}) copy-start(bf16[144,768]{1,0:T(8,128)(2,1)S(1)} %collective-permute-done.6.refs_1_) | copy-start | bytes 663556
  37.2 13.2 %collective-permute-start.8 = (bf16[144,768]{1,0:T(8,128)(2,1)S(1)}, bf16[144,768]{1,0:T(8,128)(2,1)}, u32[]{:S(2)}, u32[]{:S(2)}) collective-permute-start(bf16[144,768]{1,0:T(8,128)(2,1)S(1)} %get-tuple-element.57), channel_id=1, source_target_pairs={{0,24},{8,0},{16,8},{24,16},{1,25},{9,1},{17,9},{25,17},{2,26},{10... | collective-permute-start | bytes 663560 | tf_op jit(solution)/shard_map/ppermute | solution.py:386
  39.2 42.7 %all-to-all-start.1 = ((bf16[64,16,128]{2,1,0:T(8,128)(2,1)}), bf16[64,16,128]{2,1,0:T(8,128)(2,1)S(1)}, u32[]{:S(2)}, u32[]{:S(2)}) async-start(bf16[64,16,128]{2,1,0:T(8,128)(2,1)} %scan_states.1), calls=%async_computation.1 | async-start | bytes 524288 | tf_op jit(solution)/shard_map/all_to_all | solution.py:445
  50.1 12.0 %copy-start.2 = (bf16[256,1024]{1,0:T(8,128)(2,1)S(1)}, bf16[256,1024]{1,0:T(8,128)(2,1)}, u32[]{:S(2)}) copy-start(bf16[256,1024]{1,0:T(8,128)(2,1)} %q.1) | copy-start | bytes 1572868
  50.1 11.5 %collective-permute-start.9 = (bf16[144,768]{1,0:T(8,128)(2,1)S(1)}, bf16[144,768]{1,0:T(8,128)(2,1)S(1)}, u32[]{:S(2)}, u32[]{:S(2)}) collective-permute-start(bf16[144,768]{1,0:T(8,128)(2,1)S(1)} %get-tuple-element.58.refs_0_), channel_id=1, source_target_pairs={{0,4},{4,0},{1,5},{5,1},{2,6},{6,2},{3,7},{7,3},{8,12},{12,8},{9,1... | collective-permute-start | bytes 663560 | tf_op jit(solution)/shard_map/ppermute | solution.py:386
  50.4 11.2 %collective-permute-start.10 = (bf16[144,768]{1,0:T(8,128)(2,1)S(1)}, bf16[144,768]{1,0:T(8,128)(2,1)S(1)}, u32[]{:S(2)}, u32[]{:S(2)}) collective-permute-start(bf16[144,768]{1,0:T(8,128)(2,1)S(1)} %collective-permute-done.6.refs_1_), channel_id=1, source_target_pairs={{0,4},{4,0},{1,5},{5,1},{2,6},{6,2},{3,7},{7,3},{8,12},{12,8},{9,1... | collective-permute-start | bytes 663560 | tf_op jit(solution)/shard_map/ppermute | solution.py:386
  58.0 10.1 %collective-permute-start.5 = (bf16[288,512]{1,0:T(8,128)(2,1)}, bf16[288,512]{1,0:T(8,128)(2,1)S(1)}, u32[]{:S(2)}, u32[]{:S(2)}) collective-permute-start(bf16[288,512]{1,0:T(8,128)(2,1)} %hidden_part.1.refs_8_), channel_id=1, source_target_pairs={{0,8},{8,16},{16,24},{24,0},{1,9},{9,17},{17,25},{25,1},{2,10},{10... | collective-permute-start | bytes 884744 | tf_op jit(solution)/shard_map/ppermute | solution.py:386
  58.6 16.7 %collective-permute-start.14 = (bf16[288,512]{1,0:T(8,128)(2,1)}, bf16[288,512]{1,0:T(8,128)(2,1)S(1)}, u32[]{:S(2)}, u32[]{:S(2)}) collective-permute-start(bf16[288,512]{1,0:T(8,128)(2,1)} %hidden_part.1.refs_8_), channel_id=1, source_target_pairs={{0,24},{8,0},{16,8},{24,16},{1,25},{9,1},{17,9},{25,17},{2,26},{10... | collective-permute-start | bytes 884744 | tf_op jit(solution)/shard_map/ppermute | solution.py:386
  60.1 15.2 %collective-permute-start.13 = (bf16[288,512]{1,0:T(8,128)(2,1)}, bf16[288,512]{1,0:T(8,128)(2,1)S(1)}, u32[]{:S(2)}, u32[]{:S(2)}) collective-permute-start(bf16[288,512]{1,0:T(8,128)(2,1)} %hidden_part.1.refs_8_), channel_id=1, source_target_pairs={{0,16},{8,24},{16,0},{24,8},{1,17},{9,25},{17,1},{25,9},{2,18},{10... | collective-permute-start | bytes 884744 | tf_op jit(solution)/shard_map/ppermute | solution.py:386
  61.6 6.6 %collective-permute-start.11 = (bf16[144,768]{1,0:T(8,128)(2,1)}, bf16[144,768]{1,0:T(8,128)(2,1)S(1)}, u32[]{:S(2)}, u32[]{:S(2)}) collective-permute-start(bf16[144,768]{1,0:T(8,128)(2,1)} %collective-permute-done.7.refs_2_), channel_id=1, source_target_pairs={{0,4},{4,0},{1,5},{5,1},{2,6},{6,2},{3,7},{7,3},{8,12},{12,8},{9,1... | collective-permute-start | bytes 663560 | tf_op jit(solution)/shard_map/ppermute | solution.py:386
  61.6 13.7 %collective-permute-start.12 = (bf16[144,768]{1,0:T(8,128)(2,1)}, bf16[144,768]{1,0:T(8,128)(2,1)S(1)}, u32[]{:S(2)}, u32[]{:S(2)}) collective-permute-start(bf16[144,768]{1,0:T(8,128)(2,1)} %collective-permute-done.8.refs_3_), channel_id=1, source_target_pairs={{0,4},{4,0},{1,5},{5,1},{2,6},{6,2},{3,7},{7,3},{8,12},{12,8},{9,1... | collective-permute-start | bytes 663560 | tf_op jit(solution)/shard_map/ppermute | solution.py:386
  62.1 47.7 %copy-start.7 = (bf16[256,1024]{1,0:T(8,128)(2,1)S(1)}, bf16[256,1024]{1,0:T(8,128)(2,1)}, u32[]{:S(2)}) copy-start(bf16[256,1024]{1,0:T(8,128)(2,1)} %refs_3_.1) | copy-start | bytes 1572868
  62.1 47.7 %copy-start.13 = (f32[1024]{0:T(1024)S(1)}, f32[1024]{0:T(1024)}, u32[]{:S(2)}) copy-start(f32[1024]{0:T(1024)} %param.17) | copy-start | bytes 12292
  82.0 38.4 %copy-start.14 = (f32[512]{0:T(512)S(1)}, f32[512]{0:T(512)}, u32[]{:S(2)}) copy-start(f32[512]{0:T(512)} %param.20) | copy-start | bytes 6148
  82.0 38.4 %copy-start.15 = (s32[4,1]{0,1:T(1,128)S(1)}, s32[4,1]{0,1:T(1,128)}, u32[]{:S(2)}) copy-start(s32[4,1]{0,1:T(1,128)} %param.19) | copy-start | bytes 52
  82.0 38.4 %all-to-all-start.2 = ((bf16[64,48,128]{2,1,0:T(8,128)(2,1)}), bf16[64,48,128]{2,1,0:T(8,128)(2,1)S(1)}, u32[]{:S(2)}, u32[]{:S(2)}) async-start(bf16[64,48,128]{2,1,0:T(8,128)(2,1)} %bitcast.9), calls=%async_computation.2 | async-start | bytes 1572864 | tf_op jit(solution)/shard_map/all_to_all | solution.py:449
  98.3 1.0 copy-start.4
  109.8 1.2 %copy-start.5 = (f32[256,1024]{1,0:T(8,128)S(1)}, f32[256,1024]{1,0:T(8,128)}, u32[]{:S(2)}) copy-start(f32[256,1024]{1,0:T(8,128)} %copy-done.4) | copy-start | bytes 3145732
  (3 other events, 2.8 us)
